TPU v7x, 32 devices: a whole 2x2x4 slice. The times are simulated.
32 devices in a mesh: seq: 8 (over z, x), row: 4 (over y, core).
Axes of the slice: x: 2, y: 2, z: 4, core: 2. Of those that a mesh axis runs over, the one named last changes fastest.
Arguments:
- tokens: bfloat16 [8, 1024, 2048], P('row', 'seq'), may hold values from -6 to 6
- first_layer_values: bfloat16 [8, 1024, 2048], P('row', 'seq'), may hold values from -6 to 6
- document_lengths: int32 [8, 4], P('row'), may hold values from 1 to 512, 1024 in all within a row
- vectors: bfloat16 [19, 2048], P(None, ('seq', 'row')), may hold values from -6 to 3
- lowrank_down: bfloat16 [2048, 512], P(('seq', 'row')), may hold values from -0.125 to 0.125
- lowrank_up: bfloat16 [512, 2048], P(None, ('seq', 'row')), may hold values from -0.625 to 0.625
- square: bfloat16 [4, 2048, 2048], P(None, ('seq', 'row')), may hold values from -0.125 to 0.125
- channel_key_weight: bfloat16 [2048, 8192], P(('seq', 'row')), may hold values from -0.125 to 0.125
- channel_value_weight: bfloat16 [8192, 2048], P(('seq', 'row')), may hold values from -0.0625 to 0.0625
- output_gradient: bfloat16 [8, 1024, 2048], P('row', 'seq'), may hold values from -6 to 6
Outputs:
- mixed: bfloat16 [8, 1024, 2048], P('row', 'seq')
- tokens_grad: bfloat16 [8, 1024, 2048], P('row', 'seq')
- first_grad: bfloat16 [8, 1024, 2048], P('row', 'seq')
- vectors_gradient: float32 [19, 2048], P(None, ('seq', 'row'))
- lowrank_down_gradient: float32 [2048, 512], P(('seq', 'row'))
- lowrank_up_gradient: float32 [512, 2048], P(None, ('seq', 'row'))
- square_grad: float32 [4, 2048, 2048], P(None, ('seq', 'row'))
- key_grad: float32 [2048, 8192], P(('seq', 'row'))
- value_grad: float32 [8192, 2048], P(('seq', 'row'))
All inputs are finite; a program needn't handle non-finite values.
Results may differ from a plain program's by a relative error of at most 0.015.
Values may be sent and summed in bfloat16 or wider, within the bound.
A program may use at most 448 MiB of HBM per device.

v0:
```python
import jax
import jax.numpy as jnp
from jax import lax
from jax.sharding import PartitionSpec as P

EMBED_DIMENSION = 2048
ATTENTION_SPLITS = 32
SPLIT_DIMENSION = 64
DECAY_INNER = 96
LA = 96
LV = 64
BLOCK = 64


HIGHEST = lax.Precision.HIGHEST
CONTRACT_ROWS = (((0,), (0,)), ((), ()))
CONTRACT_COLS = (((1,), (1,)), ((), ()))


def from_behind(value, axis, steps):
    count = lax.axis_size(axis)
    first, last = (max(0, -steps), min(count, count - steps))
    return lax.ppermute(value, axis, [(source, source + steps) for source in range(first, last)])


def layer_norm(layer_inputs, norm_gain, norm_bias):
    middle = jnp.mean(layer_inputs, axis=-1, keepdims=True)
    centred = layer_inputs - middle
    spread = jnp.mean(centred * centred, axis=-1, keepdims=True)
    return centred * lax.rsqrt(spread + 1e-05) * norm_gain + norm_bias


def shift_mix(hidden, edge_row, keep_mask, mixes):
    shifted = jnp.concatenate([edge_row[:, None, :], hidden[:, :-1, :]], axis=1) * keep_mask
    return hidden[None] + (shifted - hidden)[None] * mixes[:, None, None, :]


def forward_dot(layer_inputs, weight_part):
    return jnp.dot(layer_inputs, weight_part, preferred_element_type=jnp.float32)


def input_grad(grad_piece, weight_part):
    return lax.dot_general(
        grad_piece, weight_part, CONTRACT_COLS, preferred_element_type=jnp.float32
    )


def weight_grad(layer_inputs, grad_piece):
    return lax.dot_general(
        layer_inputs, grad_piece, CONTRACT_ROWS, preferred_element_type=jnp.float32
    )


def accurate_multiply(left_side, right_side):
    return jnp.dot(left_side, right_side, precision=HIGHEST)


def high_outer(left_side, right_side):
    return lax.dot_general(left_side, right_side, CONTRACT_COLS, precision=HIGHEST)


def accurate_dot(left_side, right_side):
    return lax.dot_general(left_side, right_side, CONTRACT_ROWS, precision=HIGHEST)


def block_step(carry_state, block_items):
    (
        acceptance_lines,
        log_forgetting,
        address_adjusted,
        content_lines,
        address_unitlength,
        recurrent_state_update,
        seg_ids,
        restart_markers,
    ) = block_items
    block_len = acceptance_lines.shape[0]
    beta_keys = address_unitlength * recurrent_state_update
    cumulative = jnp.cumsum(log_forgetting, axis=0)
    preceding = cumulative - log_forgetting
    query_u = address_unitlength * jnp.exp(preceding)
    query_o = acceptance_lines * jnp.exp(cumulative)
    keys_back = address_adjusted * jnp.exp(-cumulative)
    betas_back = beta_keys * jnp.exp(-cumulative)
    before_id = seg_ids[0] - restart_markers[0]
    carried = (seg_ids == before_id).astype(jnp.float32)[:, None]
    same_doc = seg_ids[:, None] == seg_ids[None, :]
    row_iota = lax.broadcasted_iota(jnp.int32, (block_len, block_len), 0)
    col_iota = lax.broadcasted_iota(jnp.int32, (block_len, block_len), 1)
    strict = same_doc & (row_iota > col_iota)
    inclusive = same_doc & (row_iota >= col_iota)
    mass_keys = jnp.where(strict, high_outer(query_u, keys_back), 0.0)
    mass_betas = jnp.where(strict, high_outer(query_u, betas_back), 0.0)
    right_hand = carried * high_outer(query_u, carry_state) + accurate_multiply(
        mass_keys, content_lines
    )
    system = mass_betas + jnp.eye(block_len, dtype=jnp.float32)
    removed = jax.scipy.linalg.solve_triangular(system, right_hand, lower=True, unit_diagonal=True)
    outputs = (
        carried * high_outer(query_o, carry_state)
        + accurate_multiply(
            jnp.where(inclusive, high_outer(query_o, keys_back), 0.0), content_lines
        )
        - accurate_multiply(jnp.where(inclusive, high_outer(query_o, betas_back), 0.0), removed)
    )
    live = (seg_ids == seg_ids[-1]).astype(jnp.float32)[:, None]
    tail = jnp.exp(cumulative[-1])[None, :]
    new_state = (
        carried[-1, 0] * carry_state * tail
        + accurate_dot(content_lines * live, keys_back * tail)
        - accurate_dot(removed * live, betas_back * tail)
    )
    return (new_state, outputs)


def unit_recurrence(
    acceptance_lines,
    log_forgetting,
    address_adjusted,
    content_lines,
    address_unitlength,
    recurrent_state_update,
    seg_ids,
    restart_markers,
):
    blocks_count = acceptance_lines.shape[0] // BLOCK
    pieces = (
        acceptance_lines,
        log_forgetting,
        address_adjusted,
        content_lines,
        address_unitlength,
        recurrent_state_update,
        seg_ids,
        restart_markers,
    )
    block_items = tuple(
        (
            portion_item.reshape((blocks_count, BLOCK) + portion_item.shape[1:])
            for portion_item in pieces
        )
    )
    start_state = jnp.zeros((SPLIT_DIMENSION, SPLIT_DIMENSION), jnp.float32)
    _, outputs = lax.scan(jax.checkpoint(block_step), start_state, block_items)
    return outputs.reshape(acceptance_lines.shape)


def head_mixing(
    cotangent_forwarded,
    scaling_each_split,
    offset_each_split,
    extra_each_split,
    piece_elements,
    restart_each_split,
):
    length_all = cotangent_forwarded.shape[0]
    unit_count = cotangent_forwarded.shape[1]
    pieces = cotangent_forwarded.reshape(length_all, unit_count, 6, SPLIT_DIMENSION)
    shares_drawn = [pieces[:, :, member, :] for member in range(6)]
    outputs = jax.vmap(unit_recurrence, in_axes=(1, 1, 1, 1, 1, 1, 0, 0), out_axes=1)(
        shares_drawn[0],
        shares_drawn[1],
        shares_drawn[2],
        shares_drawn[3],
        shares_drawn[4],
        shares_drawn[5],
        piece_elements,
        restart_each_split,
    )
    middle = jnp.mean(outputs, axis=-1, keepdims=True)
    centred = outputs - middle
    spread = jnp.mean(centred * centred, axis=-1, keepdims=True)
    standardized_lines = (
        centred * lax.rsqrt(spread + 1.0) * scaling_each_split[None] + offset_each_split[None]
    )
    extra_summed = jnp.sum(
        shares_drawn[0] * shares_drawn[2] * extra_each_split[None], axis=-1, keepdims=True
    )
    return standardized_lines + extra_summed * shares_drawn[3]


def lowrank_middle(decay_lower_map, rate_lower_map, residual_lower_map, gate_lower_map):
    return (
        jnp.tanh(decay_lower_map),
        rate_lower_map,
        residual_lower_map,
        jax.nn.sigmoid(gate_lower_map),
    )


def prepare(
    rec_proj,
    key_proj,
    val_proj,
    decay_upper_map,
    rate_upper_map,
    residual_upper_map,
    first_layer_vals,
    small_rows,
):
    log_forgetting = -0.606531 * jax.nn.sigmoid(small_rows[0] + decay_upper_map)
    recurrent_state_update = jax.nn.sigmoid(small_rows[1] + rate_upper_map)
    val_gate = jax.nn.sigmoid(small_rows[2] + residual_upper_map)
    values_mixed = val_proj + (first_layer_vals - val_proj) * val_gate
    key_scaled = (key_proj * small_rows[3]).reshape(
        key_proj.shape[0], ATTENTION_SPLITS, SPLIT_DIMENSION
    )
    address_unitlength = (
        key_scaled * lax.rsqrt(jnp.sum(key_scaled * key_scaled, axis=-1, keepdims=True) + 1e-06)
    ).reshape(key_proj.shape)
    address_adjusted = key_proj * (1.0 + (recurrent_state_update - 1.0) * small_rows[4])
    return jnp.stack(
        [
            rec_proj,
            log_forgetting,
            address_adjusted,
            values_mixed,
            address_unitlength,
            recurrent_state_update,
        ]
    )


def per_device(
    tokens,
    first_layer_values,
    document_lengths,
    vectors,
    lowrank_down,
    lowrank_up,
    square,
    channel_key_weight,
    channel_value_weight,
    output_gradient,
):
    rows_here = tokens.shape[0]
    seg_len = tokens.shape[1]
    tok_count = rows_here * seg_len
    seq_width = lax.axis_size("seq")
    seq_rank = lax.axis_index("seq")
    length_all = seg_len * seq_width
    unit_count = rows_here * ATTENTION_SPLITS // seq_width
    trimmed_decay = DECAY_INNER
    trimmed_rate = DECAY_INNER + LA
    trimmed_mix = DECAY_INNER + LA + LV
    starts = jnp.cumsum(document_lengths, axis=1) - document_lengths
    positions = jnp.arange(length_all, dtype=jnp.int32)
    resets_all = jnp.any(positions[None, :, None] == starts[:, None, :], axis=2).astype(jnp.float32)
    seg_all = (
        jnp.sum((positions[None, :, None] >= starts[:, None, :]).astype(jnp.float32), axis=2) - 1.0
    )
    resets_here = lax.dynamic_slice_in_dim(resets_all, seq_rank * seg_len, seg_len, 1)
    keep_mask = (1.0 - resets_here)[:, :, None]
    unit_ids = seq_rank * unit_count + jnp.arange(unit_count, dtype=jnp.int32)
    row_pick = (
        unit_ids[:, None] // ATTENTION_SPLITS == jnp.arange(rows_here, dtype=jnp.int32)[None, :]
    ).astype(jnp.float32)
    split_choosing = (
        unit_ids[:, None] % ATTENTION_SPLITS
        == jnp.arange(ATTENTION_SPLITS, dtype=jnp.int32)[None, :]
    ).astype(jnp.float32)
    restart_each_split = accurate_multiply(row_pick, resets_all)
    piece_elements = accurate_multiply(row_pick, seg_all)
    vec_all, down_all, up_all, square_all = (
        lax.all_gather(vectors, ("seq", "row"), axis=1, tiled=True),
        lax.all_gather(lowrank_down, ("seq", "row"), axis=0, tiled=True),
        lax.all_gather(lowrank_up, ("seq", "row"), axis=1, tiled=True),
        lax.all_gather(square, ("seq", "row"), axis=1, tiled=True),
    )
    vector_values = vec_all.astype(jnp.float32)
    down_parts = (
        down_all[:, :trimmed_decay],
        down_all[:, trimmed_decay:trimmed_rate],
        down_all[:, trimmed_rate:trimmed_mix],
        down_all[:, trimmed_mix:],
    )
    up_parts = (
        up_all[:trimmed_decay],
        up_all[trimmed_decay:trimmed_rate],
        up_all[trimmed_rate:trimmed_mix],
        up_all[trimmed_mix:],
    )

    def time_mix(hidden, edge_row, mixes):
        return shift_mix(hidden, edge_row, keep_mask, mixes)

    def channel_mix(hidden, edge_row, mixes):
        return shift_mix(hidden, edge_row, keep_mask, mixes)[0]

    x_in = tokens.astype(jnp.float32)
    hidden_one, norm_one_pull = jax.vjp(layer_norm, x_in, vector_values[0], vector_values[1])
    edge_one = from_behind(hidden_one[:, -1, :], "seq", 1)
    mixed_f, mix_one_pull = jax.vjp(time_mix, hidden_one, edge_one, vector_values[4:10])
    mixed_incoming = mixed_f.astype(jnp.bfloat16).reshape(6, tok_count, EMBED_DIMENSION)
    rec_proj = forward_dot(mixed_incoming[0], square_all[0])
    key_proj = forward_dot(mixed_incoming[2], square_all[1])
    val_proj = forward_dot(mixed_incoming[3], square_all[2])
    down_inputs = (mixed_incoming[1], mixed_incoming[4], mixed_incoming[3], mixed_incoming[5])
    lower_results = tuple(
        (forward_dot(source, weight_part) for source, weight_part in zip(down_inputs, down_parts))
    )
    middles, middle_pull = jax.vjp(
        lowrank_middle, lower_results[0], lower_results[1], lower_results[2], lower_results[3]
    )
    middles_low = tuple((portion_item.astype(jnp.bfloat16) for portion_item in middles))
    up_outs = tuple(
        (
            forward_dot(portion_item, weight_part)
            for portion_item, weight_part in zip(middles_low, up_parts)
        )
    )
    first_in = first_layer_values.reshape(tok_count, EMBED_DIMENSION).astype(jnp.float32)
    stacked, prepare_pull = jax.vjp(
        prepare,
        rec_proj,
        key_proj,
        val_proj,
        up_outs[0],
        up_outs[1],
        up_outs[2],
        first_in,
        vector_values[10:15],
    )
    cotangent_forwarded = (
        stacked.astype(jnp.bfloat16)
        .reshape(6, rows_here, seg_len, ATTENTION_SPLITS, SPLIT_DIMENSION)
        .transpose(2, 1, 3, 0, 4)
        .reshape(seg_len, rows_here * ATTENTION_SPLITS, 6 * SPLIT_DIMENSION)
    )
    heads_incoming = lax.all_to_all(
        cotangent_forwarded, "seq", split_axis=1, concat_axis=0, tiled=True
    )
    scaling_each_split = accurate_multiply(
        split_choosing, vector_values[16].reshape(ATTENTION_SPLITS, SPLIT_DIMENSION)
    )
    offset_each_split = accurate_multiply(
        split_choosing, vector_values[17].reshape(ATTENTION_SPLITS, SPLIT_DIMENSION)
    )
    extra_each_split = accurate_multiply(
        split_choosing, vector_values[15].reshape(ATTENTION_SPLITS, SPLIT_DIMENSION)
    )

    def split_private_layout(cargo_arriving, scaling_arriving, offset_arriving, extra_arriving):
        return head_mixing(
            cargo_arriving,
            scaling_arriving,
            offset_arriving,
            extra_arriving,
            piece_elements,
            restart_each_split,
        )

    heads_out, head_pullback = jax.vjp(
        split_private_layout,
        heads_incoming.astype(jnp.float32),
        scaling_each_split,
        offset_each_split,
        extra_each_split,
    )
    back_in = lax.all_to_all(
        heads_out.astype(jnp.bfloat16), "seq", split_axis=0, concat_axis=1, tiled=True
    )
    back_tokens = (
        back_in.reshape(seg_len, rows_here, EMBED_DIMENSION)
        .transpose(1, 0, 2)
        .reshape(tok_count, EMBED_DIMENSION)
        .astype(jnp.float32)
    )
    gate_upper_map = up_outs[3]
    gated = (back_tokens * gate_upper_map).astype(jnp.bfloat16)
    after_mix = x_in + forward_dot(gated, square_all[3]).reshape(
        rows_here, seg_len, EMBED_DIMENSION
    )
    hidden_two, norm_two_pull = jax.vjp(layer_norm, after_mix, vector_values[2], vector_values[3])
    edge_two = from_behind(hidden_two[:, -1, :], "seq", 1)
    key_mixed, mix_two_pull = jax.vjp(channel_mix, hidden_two, edge_two, vector_values[18:19])
    key_in = key_mixed.astype(jnp.bfloat16).reshape(tok_count, EMBED_DIMENSION)
    key_all, value_all = (
        lax.all_gather(channel_key_weight, ("seq", "row"), axis=0, tiled=True),
        lax.all_gather(channel_value_weight, ("seq", "row"), axis=0, tiled=True),
    )
    key_act = forward_dot(key_in, key_all)
    squared = jnp.square(jax.nn.relu(key_act)).astype(jnp.bfloat16)
    ffn_out = forward_dot(squared, value_all)
    mixed = (after_mix + ffn_out.reshape(rows_here, seg_len, EMBED_DIMENSION)).astype(jnp.bfloat16)
    grad_low = output_gradient.reshape(tok_count, EMBED_DIMENSION)
    grad_out = grad_low.astype(jnp.float32)
    grad_hidden = input_grad(grad_low, value_all)
    grad_key_act = (grad_hidden * 2.0 * jax.nn.relu(key_act)).astype(jnp.bfloat16)
    grad_key_in = input_grad(grad_key_act, key_all).reshape(rows_here, seg_len, EMBED_DIMENSION)
    grad_hidden_two, grad_edge_two, grad_cmix = mix_two_pull(grad_key_in)
    edge_back_two = from_behind(grad_edge_two, "seq", -1)
    grad_hidden_two = grad_hidden_two.at[:, -1, :].add(edge_back_two)
    grad_after_norm, grad_gain_two, grad_bias_two = norm_two_pull(grad_hidden_two)
    grad_after = grad_out.reshape(rows_here, seg_len, EMBED_DIMENSION) + grad_after_norm
    grad_att = grad_after.reshape(tok_count, EMBED_DIMENSION).astype(jnp.bfloat16)
    grad_gated = input_grad(grad_att, square_all[3])
    grad_back = (grad_gated * gate_upper_map).astype(jnp.bfloat16)
    grad_gate_up = grad_gated * back_tokens
    grad_send = (
        grad_back.reshape(rows_here, seg_len, EMBED_DIMENSION)
        .transpose(1, 0, 2)
        .reshape(seg_len, rows_here * ATTENTION_SPLITS, SPLIT_DIMENSION)
    )
    grad_heads_in = lax.all_to_all(grad_send, "seq", split_axis=1, concat_axis=0, tiled=True)
    (
        derivative_cargo,
        derivative_scaling_splits,
        derivative_offset_splits,
        derivative_extra_splits,
    ) = head_pullback(grad_heads_in.astype(jnp.float32))
    grad_tokens_in = lax.all_to_all(
        derivative_cargo.astype(jnp.bfloat16), "seq", split_axis=0, concat_axis=1, tiled=True
    )
    grad_stacked = (
        grad_tokens_in.reshape(seg_len, rows_here, ATTENTION_SPLITS, 6, SPLIT_DIMENSION)
        .transpose(3, 1, 0, 2, 4)
        .reshape(6, tok_count, EMBED_DIMENSION)
        .astype(jnp.float32)
    )
    prepared = prepare_pull(grad_stacked)
    grad_rec_low = prepared[0].astype(jnp.bfloat16)
    grad_key_low = prepared[1].astype(jnp.bfloat16)
    grad_val_low = prepared[2].astype(jnp.bfloat16)
    grad_first = prepared[6]
    grad_small = prepared[7]
    grad_up_low = tuple(
        (
            portion_item.astype(jnp.bfloat16)
            for portion_item in (prepared[3], prepared[4], prepared[5], grad_gate_up)
        )
    )
    grad_middles = tuple(
        (
            input_grad(grad_piece, weight_part)
            for grad_piece, weight_part in zip(grad_up_low, up_parts)
        )
    )
    grad_downs = middle_pull(grad_middles)
    grad_down_low = tuple((portion_item.astype(jnp.bfloat16) for portion_item in grad_downs))
    grad_mixed = jnp.stack(
        [
            input_grad(grad_rec_low, square_all[0]),
            input_grad(grad_down_low[0], down_parts[0]),
            input_grad(grad_key_low, square_all[1]),
            input_grad(grad_val_low, square_all[2]) + input_grad(grad_down_low[2], down_parts[2]),
            input_grad(grad_down_low[1], down_parts[1]),
            input_grad(grad_down_low[3], down_parts[3]),
        ]
    ).reshape(6, rows_here, seg_len, EMBED_DIMENSION)
    grad_hidden_one, grad_edge_one, grad_mixes = mix_one_pull(grad_mixed)
    edge_back_one = from_behind(grad_edge_one, "seq", -1)
    grad_hidden_one = grad_hidden_one.at[:, -1, :].add(edge_back_one)
    grad_x_norm, grad_gain_one, grad_bias_one = norm_one_pull(grad_hidden_one)
    tokens_grad = (grad_after + grad_x_norm).astype(jnp.bfloat16)
    first_grad = grad_first.reshape(rows_here, seg_len, EMBED_DIMENSION).astype(jnp.bfloat16)
    extra_full_array = accurate_dot(split_choosing, derivative_extra_splits).reshape(
        EMBED_DIMENSION
    )
    scaling_full_array = accurate_dot(split_choosing, derivative_scaling_splits).reshape(
        EMBED_DIMENSION
    )
    offset_full_array = accurate_dot(split_choosing, derivative_offset_splits).reshape(
        EMBED_DIMENSION
    )
    vec_grad = jnp.concatenate(
        [
            jnp.stack([grad_gain_one, grad_bias_one, grad_gain_two, grad_bias_two]),
            grad_mixes,
            grad_small,
            jnp.stack([extra_full_array, scaling_full_array, offset_full_array]),
            grad_cmix,
        ],
        axis=0,
    )
    row_width = lax.axis_size("row")

    def column_order(matrix):
        width = matrix.shape[1]
        split = matrix.reshape(
            matrix.shape[0], seq_width, row_width, width // (seq_width * row_width)
        )
        return split.transpose(0, 2, 1, 3).reshape(matrix.shape[0], width)

    shares = (
        lax.all_to_all(
            column_order(mixed_incoming[0]), "row", split_axis=1, concat_axis=0, tiled=True
        ),
        lax.all_to_all(
            column_order(mixed_incoming[1]), "row", split_axis=1, concat_axis=0, tiled=True
        ),
        lax.all_to_all(
            column_order(mixed_incoming[2]), "row", split_axis=1, concat_axis=0, tiled=True
        ),
        lax.all_to_all(
            column_order(mixed_incoming[3]), "row", split_axis=1, concat_axis=0, tiled=True
        ),
        lax.all_to_all(
            column_order(mixed_incoming[4]), "row", split_axis=1, concat_axis=0, tiled=True
        ),
        lax.all_to_all(
            column_order(mixed_incoming[5]), "row", split_axis=1, concat_axis=0, tiled=True
        ),
        lax.all_to_all(column_order(gated), "row", split_axis=1, concat_axis=0, tiled=True),
        lax.all_to_all(column_order(key_in), "row", split_axis=1, concat_axis=0, tiled=True),
        lax.all_to_all(column_order(squared), "row", split_axis=1, concat_axis=0, tiled=True),
        lax.all_to_all(
            column_order(grad_up_low[0]), "row", split_axis=1, concat_axis=0, tiled=True
        ),
        lax.all_to_all(
            column_order(grad_up_low[1]), "row", split_axis=1, concat_axis=0, tiled=True
        ),
        lax.all_to_all(
            column_order(grad_up_low[2]), "row", split_axis=1, concat_axis=0, tiled=True
        ),
        lax.all_to_all(
            column_order(grad_up_low[3]), "row", split_axis=1, concat_axis=0, tiled=True
        ),
    )
    grads_all = (
        lax.all_gather(grad_rec_low, "row", axis=0, tiled=True),
        lax.all_gather(grad_key_low, "row", axis=0, tiled=True),
        lax.all_gather(grad_val_low, "row", axis=0, tiled=True),
        lax.all_gather(grad_att, "row", axis=0, tiled=True),
        lax.all_gather(grad_down_low[0], "row", axis=0, tiled=True),
        lax.all_gather(grad_down_low[1], "row", axis=0, tiled=True),
        lax.all_gather(grad_down_low[2], "row", axis=0, tiled=True),
        lax.all_gather(grad_down_low[3], "row", axis=0, tiled=True),
        lax.all_gather(grad_key_act, "row", axis=0, tiled=True),
        lax.all_gather(grad_low, "row", axis=0, tiled=True),
        lax.all_gather(middles_low[0], "row", axis=0, tiled=True),
        lax.all_gather(middles_low[1], "row", axis=0, tiled=True),
        lax.all_gather(middles_low[2], "row", axis=0, tiled=True),
        lax.all_gather(middles_low[3], "row", axis=0, tiled=True),
    )
    square_part = jnp.stack(
        [
            weight_grad(shares[0], grads_all[0]),
            weight_grad(shares[2], grads_all[1]),
            weight_grad(shares[3], grads_all[2]),
            weight_grad(shares[6], grads_all[3]),
        ]
    )
    down_sources = (shares[1], shares[4], shares[3], shares[5])
    down_part = jnp.concatenate(
        [
            weight_grad(source, grad_piece)
            for source, grad_piece in zip(down_sources, grads_all[4:8])
        ],
        axis=1,
    )
    up_part = jnp.concatenate(
        [
            weight_grad(portion_item, grad_piece)
            for portion_item, grad_piece in zip(grads_all[10:14], shares[9:13])
        ],
        axis=0,
    )
    key_part = weight_grad(shares[7], grads_all[8])
    value_part = weight_grad(shares[8], grads_all[9])
    vec_order = (
        vec_grad.reshape(vec_grad.shape[0], seq_width, row_width, -1)
        .transpose(0, 2, 1, 3)
        .reshape(vec_grad.shape)
    )
    vec_rows = lax.psum_scatter(
        vec_order.astype(jnp.bfloat16), "row", scatter_dimension=1, tiled=True
    ).astype(jnp.float32)
    (
        vectors_gradient,
        lowrank_down_gradient,
        lowrank_up_gradient,
        squared_total,
        key_grad,
        value_grad,
    ) = (
        lax.psum_scatter(vec_rows, "seq", scatter_dimension=1, tiled=True),
        lax.psum_scatter(down_part, "seq", scatter_dimension=0, tiled=True),
        lax.psum_scatter(up_part, "seq", scatter_dimension=1, tiled=True),
        lax.psum_scatter(square_part, "seq", scatter_dimension=1, tiled=True),
        lax.psum_scatter(key_part, "seq", scatter_dimension=0, tiled=True),
        lax.psum_scatter(value_part, "seq", scatter_dimension=0, tiled=True),
    )
    return (
        mixed,
        tokens_grad,
        first_grad,
        vectors_gradient,
        lowrank_down_gradient,
        lowrank_up_gradient,
        squared_total,
        key_grad,
        value_grad,
    )


def solution(mesh):
    in_specs = (
        P("row", "seq", None),
        P("row", "seq", None),
        P("row", None),
        P(None, ("seq", "row")),
        P(("seq", "row"), None),
        P(None, ("seq", "row")),
        P(None, ("seq", "row"), None),
        P(("seq", "row"), None),
        P(("seq", "row"), None),
        P("row", "seq", None),
    )
    out_specs = (
        P("row", "seq", None),
        P("row", "seq", None),
        P("row", "seq", None),
        P(None, ("seq", "row")),
        P(("seq", "row"), None),
        P(None, ("seq", "row")),
        P(None, ("seq", "row"), None),
        P(("seq", "row"), None),
        P(("seq", "row"), None),
    )
    return jax.shard_map(
        per_device, mesh=mesh, in_specs=in_specs, out_specs=out_specs, check_vma=False
    )
```

profile of v0, /device:TPU:0, one launch (start us, length us, event | category | flops | bytes accessed | tf_op | source)
XLA Modules:
  0.0 4944.5 jit_solution(18303970922382963752)
XLA Ops:
  10.0 43.8 all-gather
  72.2 56.1 %all-gather.17.cloned.1.call-done = bf16[512,2048]{0,1:T(8,128)(2,1)} async-done(((bf16[512,64]{0,1:T(8,128)(2,1)}), bf16[512,2048]{0,1:T(8,128)(2,1)}) %all-gather.17.cloned.1.call-update) | async-done | bytes 2097168 | tf_op jit(solution)/shard_map/all_gather | solution.py:267
  147.3 177.4 %all-gather.13.cloned.1.call-done = bf16[4,2048,2048]{2,1,0:T(8,128)(2,1)} async-done(((bf16[4,64,2048]{2,1,0:T(8,128)(2,1)}), bf16[4,2048,2048]{2,1,0:T(8,128)(2,1)}) %all-gather.13.cloned.1.call-update) | async-done | bytes 33554448 | tf_op jit(solution)/shard_map/all_gather | solution.py:268
  420.3 235.2 %all-to-all-done = bf16[128,64,384]{0,2,1:T(8,128)(2,1)} async-done(((bf16[128,64,384]{0,2,1:T(8,128)(2,1)}), bf16[128,64,384]{0,2,1:T(8,128)(2,1)}, u32[]{:S(2)}, u32[]{:S(2)}) %all-to-all-start) | async-done | bytes 6291488 | tf_op jit(solution)/shard_map/all_to_all | solution.py:330
  748.4 886.1 %while.46 = (s32[]{:T(128)}, f32[8,64,64]{2,1,0:T(8,128)S(1)}, f32[16,8,64,64]{3,2,1,0:T(8,128)}, f32[16,8,64,64]{3,2,1,0:T(8,128)}, f32[16,8,64]{2,1,0:T(8,128)...) while((s32[]{:T(128)}, f32[8,64,64]{2,1,0:T(8,128)S(1)}, ...), condition=%wide.region_8.10_spmd.clone, body=%wide.region_6.9_spmd.clone.sunk | while | flops 305363520 | bytes 9064910 | solution.py:144
  1877.6 1194.5 %while.47 = (s32[]{:T(128)}, f32[8,64,64]{2,1,0:T(8,128)S(1)}, f32[16,8,64,64]{3,2,1,0:T(8,128)}, f32[16,8,64,64]{3,2,1,0:T(8,128)}, f32[16,8,64,64]{3,2,1,0:T(8...) while((s32[]{:T(128)}, f32[8,64,64]{2,1,0:T(8,128)S(1)}, ...), condition=%wide.region_24.27_spmd.clone, body=%wide.region_18.26_spmd.clone.sunk | while | flops 812939328 | bytes 26438880 | solution.py:144
  1890.3 40.7 custom-call.23
  1964.9 40.7 custom-call.23
  2039.6 40.7 custom-call.23
  2114.2 40.7 custom-call.23
  2188.8 40.7 custom-call.23
  2263.5 40.7 custom-call.23
  2338.1 40.7 custom-call.23
  2412.7 40.7 custom-call.23
  2487.4 40.7 custom-call.23
  2562.0 40.7 custom-call.23
  2636.6 40.7 custom-call.23
  2785.9 40.7 custom-call.23
  3167.6 129.5 %all-to-all-done.3 = bf16[1024,8,384]{2,1,0:T(8,128)(2,1)} async-done(((bf16[1024,8,384]{2,1,0:T(8,128)(2,1)}), bf16[1024,8,384]{2,1,0:T(8,128)(2,1)}, u32[]{:S(2)}, u32[]{:S(2)}) %all-to-all-start.3) | async-done | bytes 6291488 | tf_op jit(solution)/shard_map/all_to_all | solution.py:412
  3725.4 66.8 %all_gather.68 = bf16[1024,64]{0,1:T(8,128)(2,1)S(1)} all-gather(bf16[256,64]{0,1:T(8,128)(2,1)} %copy-done.80), channel_id=1, replica_groups=mesh['seq'=8,'row'=4] {'row'}, dimensions={0}, use_global_device_ids=true | all-gather | bytes 163840 | tf_op jit(solution)/shard_map/all_gather | solution.py:527
  4028.1 50.8 %reduce-scatter.26.cloned.1.call-done = f32[64,512]{1,0:T(8,128)} async-done(((f32[512,512]{1,0:T(8,128)}), f32[64,512]{1,0:T(8,128)}) %reduce-scatter.26.cloned.1.call-update) | async-done | bytes 131088
  4078.9 286.0 %reduce-scatter.20.cloned.1.call-done = f32[256,2048]{1,0:T(8,128)} async-done(((f32[2048,2048]{1,0:T(8,128)}), f32[256,2048]{1,0:T(8,128)}) %reduce-scatter.20.cloned.1.call-update) | async-done | bytes 2097168 | tf_op jit(solution)/shard_map/reduce_scatter | solution.py:582
  4364.9 286.5 %reduce-scatter.16.cloned.1.call-done = f32[4,64,2048]{2,1,0:T(8,128)} async-done(((f32[4,512,2048]{2,1,0:T(8,128)}), f32[4,64,2048]{2,1,0:T(8,128)}) %reduce-scatter.16.cloned.1.call-update) | async-done | bytes 2097168 | tf_op jit(solution)/shard_map/reduce_scatter | solution.py:580
  4651.4 286.0 %reduce-scatter.18.cloned.1.call-done = f32[64,8192]{1,0:T(8,128)} async-done(((f32[512,8192]{1,0:T(8,128)}), f32[64,8192]{1,0:T(8,128)}) %reduce-scatter.18.cloned.1.call-update) | async-done | bytes 2097168 | tf_op jit(solution)/shard_map/reduce_scatter | solution.py:581
  (2212 shorter events, 2811.6 us)
Async XLA Ops:
  7.2 62.8 %all-gather.15.cloned.1.call-start = ((), (), s32[]{:S(2)}) async-start(), calls=%async_computation.25 | async-start | bytes 2162688 | tf_op jit(solution)/shard_map/all_gather | solution.py:266
  7.9 120.3 %all-gather.17.cloned.1.call-start = ((), (), s32[]{:S(2)}) async-start(), calls=%async_computation.26 | async-start | bytes 2162688 | tf_op jit(solution)/shard_map/all_gather | solution.py:267
  8.7 316.0 %all-gather.13.cloned.1.call-start = ((), (), s32[]{:S(2)}) async-start(), calls=%async_computation.24 | async-start | bytes 34603008 | tf_op jit(solution)/shard_map/all_gather | solution.py:268
  9.4 1706.4 %all-gather.19.cloned.1.call-start = ((), (), s32[]{:S(2)}) async-start(), calls=%async_computation.27 | async-start | bytes 34603008 | tf_op jit(solution)/shard_map/all_gather | solution.py:379
  412.8 242.7 %all-to-all-start = ((bf16[128,64,384]{0,2,1:T(8,128)(2,1)}), bf16[128,64,384]{0,2,1:T(8,128)(2,1)}, u32[]{:S(2)}, u32[]{:S(2)}) async-start(bf16[128,64,384]{0,2,1:T(8,128)(2,1)} %bitcast.913), calls=%async_computation | async-start | bytes 12582912 | tf_op jit(solution)/shard_map/all_to_all | solution.py:330
  417.6 1316.6 %all-gather.21.cloned.1.call-start = ((), (), s32[]{:S(2)}) async-start(), calls=%async_computation.28 | async-start | bytes 34603008 | tf_op jit(solution)/shard_map/all_gather | solution.py:380
  3155.9 141.2 %all-to-all-start.3 = ((bf16[1024,8,384]{2,1,0:T(8,128)(2,1)}), bf16[1024,8,384]{2,1,0:T(8,128)(2,1)}, u32[]{:S(2)}, u32[]{:S(2)}) async-start(bf16[1024,8,384]{2,1,0:T(8,128)(2,1)} %copy.1471), calls=%async_computation.3 | async-start | bytes 12582912 | tf_op jit(solution)/shard_map/all_to_all | solution.py:412
  3160.8 643.1 %reduce-scatter.14.cloned.1.call-start = ((), (), s32[]{:S(2)}) async-start(), calls=%async_computation.29 | async-start | bytes 122880 | tf_op jit(solution)/shard_map/reduce_scatter | solution.py:566
  3474.5 387.9 %all-gather.33.cloned.1.call-start = ((), (), s32[]{:S(2)}) async-start(), calls=%async_computation.37 | async-start | bytes 5242880 | tf_op jit(solution)/shard_map/all_gather | solution.py:530
  3475.3 469.8 %all-gather.29.cloned.1.call-start = ((), (), s32[]{:S(2)}) async-start(), calls=%async_computation.33 | async-start | bytes 5242880 | tf_op jit(solution)/shard_map/all_gather | solution.py:524
  3476.0 476.0 %all-gather.27.cloned.1.call-start = ((), (), s32[]{:S(2)}) async-start(), calls=%async_computation.32 | async-start | bytes 5242880 | tf_op jit(solution)/shard_map/all_gather | solution.py:523
  3476.7 482.1 %all-gather.25.cloned.1.call-start = ((), (), s32[]{:S(2)}) async-start(), calls=%async_computation.31 | async-start | bytes 5242880 | tf_op jit(solution)/shard_map/all_gather | solution.py:522
  3477.3 488.4 %all-gather.23.cloned.1.call-start = ((), (), s32[]{:S(2)}) async-start(), calls=%async_computation.30 | async-start | bytes 5242880 | tf_op jit(solution)/shard_map/all_gather | solution.py:521
  3479.8 526.3 %all-gather.31.cloned.1.call-start = ((), (), s32[]{:S(2)}) async-start(), calls=%async_computation.35 | async-start | bytes 20971520 | tf_op jit(solution)/shard_map/all_gather | solution.py:529
  3507.7 30.7 all-to-all-start.4
  3559.7 30.3 all-to-all-start.7
  3667.2 53.2 %all-to-all-start.9 = ((bf16[256,4,512]{0,2,1:T(8,128)(2,1)}), bf16[256,4,512]{0,2,1:T(8,128)(2,1)}, u32[]{:S(2)}, u32[]{:S(2)}) async-start(bf16[256,4,512]{0,2,1:T(8,128)(2,1)} %bitcast.974), calls=%async_computation.10 | async-start | bytes 2097152 | tf_op jit(solution)/shard_map/all_to_all | solution.py:510
  3720.3 142.1 %all-to-all-start.16 = ((bf16[256,4,2048]{2,0,1:T(8,128)(2,1)}), bf16[256,4,2048]{2,0,1:T(8,128)(2,1)}, u32[]{:S(2)}, u32[]{:S(2)}) async-start(bf16[256,4,2048]{2,0,1:T(8,128)(2,1)} %all_to_all.268), calls=%async_computation.19 | async-start | bytes 8388608 | tf_op jit(solution)/shard_map/all_to_all | solution.py:506
  3725.3 301.3 %reduce-scatter.22.cloned.1.call-start = ((), (), s32[]{:S(2)}) async-start(), calls=%async_computation.39 | async-start | bytes 294912
  3805.5 222.6 %reduce-scatter.24.cloned.1.call-start = ((), (), s32[]{:S(2)}) async-start(), calls=%async_computation.40 | async-start | bytes 1179648
  3810.2 268.7 %reduce-scatter.26.cloned.1.call-start = ((), (), s32[]{:S(2)}) async-start(), calls=%async_computation.41 | async-start | bytes 1179648
  3862.4 502.5 %reduce-scatter.20.cloned.1.call-start = ((), (), s32[]{:S(2)}) async-start(), calls=%async_computation.38 | async-start | bytes 18874368 | tf_op jit(solution)/shard_map/reduce_scatter | solution.py:582
  3928.3 723.1 %reduce-scatter.16.cloned.1.call-start = ((), (), s32[]{:S(2)}) async-start(), calls=%async_computation.34 | async-start | bytes 18874368 | tf_op jit(solution)/shard_map/reduce_scatter | solution.py:580
  3978.5 958.9 %reduce-scatter.18.cloned.1.call-start = ((), (), s32[]{:S(2)}) async-start(), calls=%async_computation.36 | async-start | bytes 18874368 | tf_op jit(solution)/shard_map/reduce_scatter | solution.py:581
  (210 other events, 4360.3 us)
Sparse Core Ops, SparseCore 0:
  10.9 59.0 all-gather.14
  72.9 55.3 all-gather.16
  131.2 193.4 all-gather.12
  327.4 302.8 all-gather.18
  633.0 195.0 all-gather.20
  3474.6 20.7 reduce-scatter.13
  3497.0 45.7 all-gather.32
  3544.4 47.9 all-gather.28
  3594.6 49.1 all-gather.26
  3645.1 48.8 all-gather.24
  3695.6 39.8 all-gather.22
  3736.9 138.4 all-gather.30
  3878.7 67.3 reduce-scatter.21
  3949.9 62.3 reduce-scatter.23
  4016.5 62.3 reduce-scatter.25
  4083.1 281.7 reduce-scatter.19
  4369.6 281.7 reduce-scatter.15
  4655.6 281.7 reduce-scatter.17
where the time goes:
time: 4970 us; the launch traced here: 4940 us
  waiting for transfers between devices  1700 us (34%)
  other arithmetic  1470 us (30%)
  matrix products  759 us (15%)
  local copies, waits for them, and re-layouts  731 us (15%)
  blocking collectives  186 us (4%)
  starting transfers between devices  80.3 us (2%)
    another operation x96, other arithmetic, block_step(): jax.scipy.linalg.solve_triangular(system, right_hand, lower=True, unit_di...  1280 us
    reduce_scatter x1, waiting for transfers between devices, per_device(): lax.psum_scatter(square_part, 'seq', scatter_dimension=1, tiled=True)  286 us
    reduce_scatter x1, waiting for transfers between devices, per_device(): lax.psum_scatter(key_part, 'seq', scatter_dimension=0, tiled=True)  286 us
    reduce_scatter x1, waiting for transfers between devices, per_device(): lax.psum_scatter(value_part, 'seq', scatter_dimension=0, tiled=True)  286 us
    all_to_all x1, waiting for transfers between devices, per_device(): lax.all_to_all(cotangent_forwarded, 'seq', split_axis=1, concat_axis=0, t...  235 us
    dot_general x368, matrix products, high_outer(): lax.dot_general(left_side, right_side, CONTRACT_COLS, precision=HIGHEST)  223 us
    all_gather x1, waiting for transfers between devices, per_device(): lax.all_gather(square, ('seq', 'row'), axis=1, tiled=True)  177 us
    dot_general x164, matrix products, accurate_multiply(): return jnp.dot(left_side, right_side, precision=HIGHEST)  149 us
  transfers between devices with their start and end apart: 38, of which 23 were waited for; matrix products, arithmetic and copies ran while one was open for 29% of the time, Pallas kernels for 0%

commit v1 on v0

v1 whole, which is shorter than its diff:
```python
import jax
import jax.numpy as jnp
from jax import lax
from jax.experimental import pallas as pl
from jax.experimental.pallas import tpu as pltpu
from jax.sharding import Mesh, PartitionSpec as P

DECAY_INNER = 96
LA = 96
LV = 64

BF=jnp.bfloat16; F32=jnp.float32
SD=64; BLK=64
NN=(((1,),(0,)),((),())); NT=(((1,),(1,)),((),())); TN=(((0,),(0,)),((),()))

def mm(a,b,d): return lax.dot_general(a,b,d,preferred_element_type=F32)

class Geo:
    def __init__(s, gc):
        s.gc=gc; s.gh=gc//SD
        lane=lax.broadcasted_iota(jnp.int32,(1,gc),1)
        s.head=lane//SD
        s.lm=[(s.head==h).astype(BF) for h in range(s.gh)]
        row=lax.broadcasted_iota(jnp.int32,(BLK,gc),0)
        col=lax.broadcasted_iota(jnp.int32,(BLK,gc),1)%SD
        s.below=row>col; s.upto=row>=col
    def blk(s,x):
        return jnp.concatenate([x*m for m in s.lm],axis=0) if s.gh>1 else x
    def ext(s,x):
        out=x[:BLK]
        for h in range(1,s.gh):
            out=jnp.where(s.head==h,x[h*BLK:(h+1)*BLK],out)
        return out

def headsum(x,ones):
    hi=x.astype(BF); lo=(x-hi.astype(F32)).astype(BF)
    return mm(hi,ones,NN)+mm(lo,ones,NN)

def decayed(geo,ws,tri):
    w=ws.astype(F32)
    cum=mm(tri,ws,NN)
    return w,cum,jnp.exp(cum-w),jnp.exp(cum),jnp.exp(-cum)

def first_kernel(rp,kp,vp,uw,ua,uv,fl,vec,meta,segrow,tri,ones,rs,ws,ks,vs,qs,as_,ab):
    C=rp.shape[1]; gc=min(C,256); geo=Geo(gc)
    same=meta[:,0:1]==segrow[0]
    strict=geo.below&same
    for g in range(C//gc):
        sl=slice(g*gc,(g+1)*gc)
        V=lambda i: vec[i:i+1,sl]
        k0=kp[:,sl]; v0=vp[:,sl]
        lw=-0.606531*jax.nn.sigmoid(V(0)+uw[:,sl])
        al=jax.nn.sigmoid(V(1)+ua[:,sl])
        vm=jax.nn.sigmoid(V(2)+uv[:,sl])
        v=v0+(fl[:,sl].astype(F32)-v0)*vm
        kn=k0*V(3)
        kk=kn*lax.rsqrt(headsum(kn*kn,ones[...])+1e-6)
        km=k0*(1.0+(al-1.0)*V(4))
        q_=kk.astype(BF); w_=lw.astype(BF); a_=al.astype(BF)
        rs[:,sl]=rp[:,sl].astype(BF); ws[:,sl]=w_; ks[:,sl]=km.astype(BF)
        vs[:,sl]=v.astype(BF); qs[:,sl]=q_; as_[:,sl]=a_
        w,cum,eP,eC,eN=decayed(geo,w_,tri[...])
        q=q_.astype(F32)
        qu=(q*eP).astype(BF); bb=(q*a_.astype(F32)*eN).astype(BF)
        ab[:,sl]=jnp.where(strict,mm(qu,geo.blk(bb),NT),0.0)

def solve_kernel(a,t):
    n=a.shape[0]
    t[...]=jnp.zeros_like(t)
    cidx=lax.broadcasted_iota(jnp.int32,t.shape[1:],0)
    def outer(i,_):
        def inner(jb,acc):
            for jj in range(8):
                j=jb*8+jj
                acc=acc-a[i,pl.ds(j,1),:]*t[j]
            return acc
        acc=lax.fori_loop(0,i//8+1,inner,(cidx==i).astype(F32))
        t[i]=acc
        return 0
    lax.fori_loop(0,n,outer,0)

def forward_kernel(rs,ws,ks,vs,qs,as_,tt,vec,meta,segrow,tri,ones,y,o_out,u_out,s_out,state):
    C=rs.shape[1]; gc=min(C,256); geo=Geo(gc)
    @pl.when(pl.program_id(0)==0)
    def _(): state[...]=jnp.zeros_like(state)
    same=meta[:,0:1]==segrow[0]
    carried=meta[:,1:2]; live=meta[:,2:3]; last=meta[BLK-1:BLK,1:2]
    strict=geo.below&same; incl=geo.upto&same
    for g in range(C//gc):
        sl=slice(g*gc,(g+1)*gc)
        V=lambda i: vec[i:i+1,sl]
        w,cum,eP,eC,eN=decayed(geo,ws[:,sl],tri[...])
        q=qs[:,sl].astype(F32); r=rs[:,sl].astype(F32); k=ks[:,sl].astype(F32)
        vb=vs[:,sl]; v=vb.astype(F32); a=as_[:,sl].astype(F32)
        qq=jnp.concatenate([(q*eP).astype(BF),(r*eC).astype(BF)],axis=0)
        kb=(k*eN).astype(BF); bb=(q*a*eN).astype(BF)
        mk=mm(qq,geo.blk(kb),NT)
        al=jnp.concatenate([jnp.where(strict,mk[:BLK],0.0).astype(BF),jnp.where(incl,mk[BLK:],0.0).astype(BF)],axis=0)
        lb=jnp.where(incl,mm(qq[BLK:],geo.blk(bb),NT),0.0).astype(BF)
        s0=state[g]; sb=s0.astype(BF)
        s_out[0,g]=sb
        qst=mm(qq,sb,NT)
        av=mm(al,geo.blk(vb),NN)
        rhs=carried*qst[:BLK]+av[:BLK]
        u=mm(tt[:,sl],geo.blk(rhs.astype(BF)),NN)
        ub=u.astype(BF)
        u_out[:,sl]=ub
        o=carried*qst[BLK:]+av[BLK:]-mm(lb,geo.blk(ub),NN)
        vu=jnp.concatenate([(v*live).astype(BF),(u*(-live)).astype(BF)],axis=0)
        ds=mm(vu,jnp.concatenate([kb,bb],axis=0),TN)
        tail=eC[BLK-1:BLK]
        state[g]=(last*s0+ds*ones[...].astype(F32))*tail
        o_out[:,sl]=o
        mean=headsum(o,ones[...])*(1.0/SD)
        cen=o-mean
        var=headsum(cen*cen,ones[...])*(1.0/SD)
        extra=headsum(r*k*V(5),ones[...])
        y[:,sl]=(cen*lax.rsqrt(var+1.0)*V(6)+V(7)+extra*v).astype(BF)

def backward_kernel(dy,o_in,rs,ws,ks,vs,qs,as_,tt,u_in,s_in,rp,kp,vp,uw,ua,uv,fl,vec,meta,segrow,tri,tru,ones,
                    drp,dkp,dvp,duw,dua,duv,dfl,dvec,state):
    C=rs.shape[1]; gc=min(C,256); geo=Geo(gc)
    @pl.when(pl.program_id(0)==0)
    def _():
        state[...]=jnp.zeros_like(state)
        dvec[...]=jnp.zeros_like(dvec)
    same=meta[:,0:1]==segrow[0]
    carried=meta[:,1:2]; live=meta[:,2:3]; last=meta[BLK-1:BLK,1:2]
    strict=geo.below&same; incl=geo.upto&same
    cat=lambda *x: jnp.concatenate(x,axis=0)
    rsum=lambda x: jnp.sum(x,axis=0,keepdims=True)
    for g in range(C//gc):
        sl=slice(g*gc,(g+1)*gc)
        V=lambda i: vec[i:i+1,sl]
        on=ones[...]
        w,cum,eP,eC,eN=decayed(geo,ws[:,sl],tri[...])
        q=qs[:,sl].astype(F32); r=rs[:,sl].astype(F32); k=ks[:,sl].astype(F32)
        vb=vs[:,sl]; v=vb.astype(F32); a=as_[:,sl].astype(F32)
        d=dy[:,sl].astype(F32); o=o_in[:,sl]
        mean=headsum(o,on)*(1.0/SD); cen=o-mean
        rstd=lax.rsqrt(headsum(cen*cen,on)*(1.0/SD)+1.0)
        nrm=cen*rstd
        extra=headsum(r*k*V(5),on)
        de=headsum(d*v,on)
        dn=d*V(6)
        do=rstd*(dn-headsum(dn,on)*(1.0/SD)-nrm*(headsum(dn*nrm,on)*(1.0/SD)))
        g17=rsum(d); g16=rsum(d*nrm); g15=rsum(de*r*k)
        dr=de*k*V(5); dk=de*r*V(5); dv=d*extra
        qq=cat((q*eP).astype(BF),(r*eC).astype(BF))
        kb=(k*eN).astype(BF); bb=(q*a*eN).astype(BF)
        kblk=geo.blk(kb); bblk=geo.blk(bb)
        mk=mm(qq,kblk,NT)
        al=cat(jnp.where(strict,mk[:BLK],0.0).astype(BF),jnp.where(incl,mk[BLK:],0.0).astype(BF))
        lb=jnp.where(incl,mm(qq[BLK:],bblk,NT),0.0).astype(BF)
        ub=u_in[:,sl]; s0=s_in[0,g]
        tail=eC[BLK-1:BLK]
        ds1=state[g]*tail; dsb=ds1.astype(BF)
        kbs=mm(cat(kb,bb),dsb,NT)
        dob=do.astype(BF)
        du=-geo.ext(mm(lb,dob,TN))-live*kbs[BLK:]
        yy=geo.ext(mm(tt[:,sl],du.astype(BF),TN))
        yo=cat(yy.astype(BF),dob)
        cyo=cat((carried*yy).astype(BF),(carried*do).astype(BF))
        mv=mm(yo,geo.blk(vb),NT); mu=mm(yo,geo.blk(ub),NT)
        dkm=cat(jnp.where(strict,mv[:BLK],0.0).astype(BF),jnp.where(incl,mv[BLK:],0.0).astype(BF))
        dbm=cat(jnp.where(strict,-mu[:BLK],0.0).astype(BF),jnp.where(incl,-mu[BLK:],0.0).astype(BF))
        dqq=mm(cyo,s0,NN)+mm(dkm,kblk,NN)+mm(dbm,bblk,NN)
        vus=mm(cat(vb,ub),dsb,NN)
        kst=live*vus[:BLK]; bst=-(live*vus[BLK:])
        dkb=geo.ext(mm(dkm,qq,TN))+kst
        dbb=geo.ext(mm(dbm,qq,TN))+bst
        dv=dv+geo.ext(mm(al,yo,TN))+live*kbs[:BLK]
        kf=kb.astype(F32); bf=bb.astype(F32); qf=qq.astype(F32)
        dlast=last*rsum(ds1*s0.astype(F32))+rsum(kf*kst+bf*bst)
        state[g]=mm(cyo,qq,TN)*on.astype(F32)+last*ds1
        dqu=dqq[:BLK]*qf[:BLK]
        dcum=dqu+dqq[BLK:]*qf[BLK:]-dkb*kf-dbb*bf
        hi=dcum.astype(BF); rest=dcum-hi.astype(F32); lo=rest.astype(BF)
        lo2=(rest-lo.astype(F32)).astype(BF)
        dw=mm(tru[...],hi,NN)+mm(tru[...],lo,NN)+mm(tru[...],lo2,NN)+dlast-dqu
        dben=dbb*eN
        dq=dqq[:BLK]*eP+dben*a
        da=dben*q
        dr=dr+dqq[BLK:]*eC
        dk=dk+dkb*eN
        k0=kp[:,sl]; v0=vp[:,sl]
        sg=jax.nn.sigmoid(V(0)+uw[:,sl]); af=jax.nn.sigmoid(V(1)+ua[:,sl]); vm=jax.nn.sigmoid(V(2)+uv[:,sl])
        kn=k0*V(3)
        ri=lax.rsqrt(headsum(kn*kn,on)+1e-6)
        kk=kn*ri
        gw=(-0.606531)*dw*sg*(1.0-sg)
        gv=dv*(fl[:,sl].astype(F32)-v0)*vm*(1.0-vm)
        da=da+dk*k0*V(4)
        ga=da*af*(1.0-af)
        dkn=ri*(dq-kk*headsum(dq*kk,on))
        drp[:,sl]=dr.astype(BF)
        dkp[:,sl]=(dk*(1.0+(af-1.0)*V(4))+dkn*V(3)).astype(BF)
        dvp[:,sl]=(dv*(1.0-vm)).astype(BF)
        duw[:,sl]=gw.astype(BF); dua[:,sl]=ga.astype(BF); duv[:,sl]=gv.astype(BF)
        dfl[:,sl]=(dv*vm).astype(BF)
        dvec[:,sl]+=cat(rsum(gw),rsum(ga),rsum(gv),rsum(dkn*k0),rsum(dk*k0*(af-1.0)),g15,g16,g17)

def consts(C):
    gc=min(C,256)
    i=jnp.arange(BLK); tri=(i[:,None]>=i[None,:]).astype(BF); tru=(i[:,None]<=i[None,:]).astype(BF)
    j=jnp.arange(gc)//SD; ones=(j[:,None]==j[None,:]).astype(BF)
    return tri,tru,ones

VM=60*2**20
def params(): return pltpu.CompilerParams(vmem_limit_bytes=VM)

def recurrence_forward(ins,vec,meta,segrow):
    L,C=ins[0].shape; NB=L//BLK; gc=min(C,256); G=C//gc; H=C//SD
    tri,tru,ones=consts(C)
    rowb=pl.BlockSpec((BLK,C),lambda i:(i,0)); fix=lambda s: pl.BlockSpec(s,lambda i:(0,)*len(s))
    metab=pl.BlockSpec((BLK,meta.shape[1]),lambda i:(i,0)); segb=pl.BlockSpec((1,1,gc),lambda i:(i,0,0))
    sd=lambda dt: jax.ShapeDtypeStruct((L,C),dt)
    *six,ab=pl.pallas_call(first_kernel,grid=(NB,),
        in_specs=[rowb]*7+[fix((8,C)),metab,segb,fix((BLK,BLK)),fix((gc,gc))],
        out_specs=[rowb]*7,out_shape=[sd(BF)]*6+[sd(F32)],compiler_params=params())(*ins,vec,meta,segrow,tri,ones)
    at=ab.reshape(NB,BLK,H,SD).transpose(1,3,0,2).reshape(BLK,SD,NB*H)
    t=pl.pallas_call(solve_kernel,out_shape=jax.ShapeDtypeStruct(at.shape,F32),compiler_params=params())(at)
    tt=t.astype(BF).reshape(BLK,SD,NB,H).transpose(2,0,3,1).reshape(L,C)
    y,o,u,s=pl.pallas_call(forward_kernel,grid=(NB,),
        in_specs=[rowb]*7+[fix((8,C)),metab,segb,fix((BLK,BLK)),fix((gc,gc))],
        out_specs=[rowb]*3+[pl.BlockSpec((1,G,gc,gc),lambda i:(i,0,0,0))],
        out_shape=[sd(BF),sd(F32),sd(BF),jax.ShapeDtypeStruct((NB,G,gc,gc),BF)],
        scratch_shapes=[pltpu.VMEM((G,gc,gc),F32)],compiler_params=params())(*six,tt,vec,meta,segrow,tri,ones)
    return y,(o,*six,tt,u,s)

def recurrence_backward(dy,saved,ins,vec,meta,segrow):
    L,C=ins[0].shape; NB=L//BLK; gc=min(C,256); G=C//gc
    tri,tru,ones=consts(C)
    rev=lambda i: NB-1-i
    rowb=pl.BlockSpec((BLK,C),lambda i:(rev(i),0)); fix=lambda s: pl.BlockSpec(s,lambda i:(0,)*len(s))
    metab=pl.BlockSpec((BLK,meta.shape[1]),lambda i:(rev(i),0)); segb=pl.BlockSpec((1,1,gc),lambda i:(rev(i),0,0))
    sb=pl.BlockSpec((1,G,gc,gc),lambda i:(rev(i),0,0,0))
    return pl.pallas_call(backward_kernel,grid=(NB,),
        in_specs=[rowb]*10+[sb]+[rowb]*7+[fix((8,C)),metab,segb,fix((BLK,BLK)),fix((BLK,BLK)),fix((gc,gc))],
        out_specs=[rowb]*7+[fix((8,C))],
        out_shape=[jax.ShapeDtypeStruct((L,C),BF)]*7+[jax.ShapeDtypeStruct((8,C),F32)],
        scratch_shapes=[pltpu.VMEM((G,gc,gc),F32)],compiler_params=params())(dy,*saved,*ins,vec,meta,segrow,tri,tru,ones)


def mix_tile(x, vec, first_row, keep):
    cen = x - jnp.mean(x, axis=-1, keepdims=True)
    hat = cen * lax.rsqrt(jnp.mean(cen * cen, axis=-1, keepdims=True) + 1e-05)
    h = hat * vec[0:1] + vec[1:2]
    row = lax.broadcasted_iota(jnp.int32, h.shape, 0)
    shifted = jnp.where(row == 0, first_row, pltpu.roll(h, 1, 0))
    return hat, h, shifted * keep - h


def mix_forward_kernel(x, meta, vec, sq, low, up, *refs):
    xm, (rp, kp, vp, uw, ua, uv, ug, mid, midb, carry) = refs[:6], refs[6:]

    @pl.when(pl.program_id(0) == 0)
    def _():
        carry[...] = jnp.zeros_like(carry)

    _, h, delta = mix_tile(x[...].astype(F32), vec, carry[0:1], meta[:, 3:4])
    carry[0:1] = h[h.shape[0] - 1 :]
    m = []
    for i in range(6):
        m.append((h + delta * vec[4 + i : 5 + i]).astype(BF))
        xm[i][...] = m[i]
    rp[...] = mm(m[0], sq[0], NN)
    kp[...] = mm(m[2], sq[1], NN)
    vp[...] = mm(m[3], sq[2], NN)
    for out, i, lo, hi, act in ((uw, 1, 0, 128, jnp.tanh), (ua, 4, 128, 256, None), (uv, 3, 256, 384, None), (ug, 5, 384, 640, jax.nn.sigmoid)):
        d = mm(m[i], low[:, lo:hi], NN)
        if act is not None:
            d = act(d)
        b = d.astype(BF)
        mid[:, lo:hi] = d
        midb[:, lo:hi] = b
        out[...] = mm(b, up[:, lo:hi], NT)


def mix_backward_kernel(drp, dkp, dvp, duw, dua, duv, dug, x, above, meta, mid, vec, sq, low, up, dh, dd, gv, carry, hat_s):
    n, D = x.shape
    step = min(D, 512)

    @pl.when(pl.program_id(0) == 0)
    def _():
        carry[...] = jnp.zeros_like(carry)
        gv[...] = jnp.zeros_like(gv)

    def normalized(v):
        v = v.astype(F32)
        cen = v - jnp.mean(v, axis=-1, keepdims=True)
        return cen * lax.rsqrt(jnp.mean(cen * cen, axis=-1, keepdims=True) + 1e-05)

    hat_s[...] = normalized(x[...])
    prev = normalized(above[...])[above.shape[0] - 1 :]
    keep = meta[:, 3:4]
    dw = (mm(duw[...], up[:, 0:128], NN) * (1.0 - mid[:, 0:128] * mid[:, 0:128])).astype(BF)
    da = mm(dua[...], up[:, 128:256], NN).astype(BF)
    dv = mm(duv[...], up[:, 256:384], NN).astype(BF)
    s = mid[:, 384:640]
    dg = (mm(dug[...], up[:, 384:640], NN) * s * (1.0 - s)).astype(BF)
    dd[:, 0:128] = dw
    dd[:, 128:256] = da
    dd[:, 256:384] = dv
    dd[:, 384:640] = dg
    row = lax.broadcasted_iota(jnp.int32, (n, step), 0)
    for k in range(D // step):
        sl = slice(k * step, (k + 1) * step)
        gain, bias = vec[0:1, sl], vec[1:2, sl]
        hat = hat_s[:, sl]
        h = hat * gain + bias
        delta = jnp.where(row == 0, prev[:, sl] * gain + bias, pltpu.roll(h, 1, 0)) * keep - h
        total = ds = None
        for i in range(6):
            if i == 0:
                d = mm(drp[...], sq[0, sl], NT)
            elif i == 1:
                d = mm(dw, low[sl, 0:128], NT)
            elif i == 2:
                d = mm(dkp[...], sq[1, sl], NT)
            elif i == 3:
                d = mm(dvp[...], sq[2, sl], NT) + mm(dv, low[sl, 256:384], NT)
            elif i == 4:
                d = mm(da, low[sl, 128:256], NT)
            else:
                d = mm(dg, low[sl, 384:640], NT)
            gv[i : i + 1, sl] += jnp.sum(d * delta, axis=0, keepdims=True)
            scaled = d * vec[4 + i : 5 + i, sl]
            total = d if total is None else total + d
            ds = scaled if ds is None else ds + scaled
        back = ds * keep
        moved = jnp.where(row == n - 1, carry[0:1, sl], pltpu.roll(back, n - 1, 0))
        carry[0:1, sl] = back[0:1]
        g = total - ds + moved
        dh[:, sl] = g.astype(BF)
        gv[6:7, sl] += jnp.sum(g * hat, axis=0, keepdims=True)
        gv[7:8, sl] += jnp.sum(g, axis=0, keepdims=True)


def weight_kernel(x0, x1, x2, x3, x4, x5, drp, dkp, dvp, dd, duw, dua, duv, dug, mid, z, dt, sq, down, up, sq3):
    sq[0] = mm(x0[...], drp[...], TN).astype(BF)
    sq[1] = mm(x2[...], dkp[...], TN).astype(BF)
    sq[2] = mm(x3[...], dvp[...], TN).astype(BF)
    for x, lo, hi in ((x1, 0, 128), (x4, 128, 256), (x3, 256, 384), (x5, 384, 640)):
        down[:, lo:hi] = mm(x[...], dd[:, lo:hi], TN).astype(BF)
    sq3[...] = mm(z[...], dt[...], TN).astype(BF)

    @pl.when(pl.program_id(0) == 0)
    def _():
        for d, lo, hi in ((duw, 0, 128), (dua, 128, 256), (duv, 256, 384), (dug, 384, 640)):
            up[:, lo:hi] = mm(d[...], mid[:, lo:hi], TN).astype(BF)


def weight_grads(xm, grads, dd, mid, z, dt):
    L, D = xm[0].shape
    C, wide = z.shape[1], mid.shape[1]
    n = 256 if L <= 1024 else 128
    feat = pl.BlockSpec((L, n), lambda i: (0, i))
    fix = lambda m: pl.BlockSpec((L, m), lambda i: (0, 0))
    sd = jax.ShapeDtypeStruct
    return pl.pallas_call(
        weight_kernel,
        grid=(D // n,),
        in_specs=[feat] * 6 + [fix(C)] * 3 + [fix(wide)] + [fix(C)] * 4 + [fix(wide), fix(C), feat],
        out_specs=[
            pl.BlockSpec((3, n, C), lambda i: (0, i, 0)),
            pl.BlockSpec((n, wide), lambda i: (i, 0)),
            pl.BlockSpec((C, wide), lambda i: (0, 0)),
            pl.BlockSpec((C, n), lambda i: (0, i)),
        ],
        out_shape=[sd((3, D, C), BF), sd((D, wide), BF), sd((C, wide), BF), sd((C, D), BF)],
        compiler_params=params(),
    )(*xm, *grads[:3], dd, *grads[3:], mid, z, dt)


TILE = 128


def mix_forward(x, meta, vec, sq, low, up):
    L, D = x.shape
    C = up.shape[0]
    wide = low.shape[1]
    tok = lambda n: pl.BlockSpec((TILE, n), lambda i: (i, 0))
    fix = lambda s: pl.BlockSpec(s, lambda i: (0,) * len(s))
    sd = jax.ShapeDtypeStruct
    out = pl.pallas_call(
        mix_forward_kernel,
        grid=(L // TILE,),
        in_specs=[tok(D), tok(meta.shape[1]), fix(vec.shape), fix(sq.shape), fix(low.shape), fix(up.shape)],
        out_specs=[tok(D)] * 6 + [tok(C)] * 7 + [tok(wide)] * 2,
        out_shape=[sd((L, D), BF)] * 6 + [sd((L, C), F32)] * 7 + [sd((L, wide), F32), sd((L, wide), BF)],
        scratch_shapes=[pltpu.VMEM((8, D), F32)],
        compiler_params=params(),
    )(x, meta, vec, sq, low, up)
    return out[:6], out[6:13], out[13], out[14]


def mix_backward(grads, x, meta, mid, vec, sq, low, up):
    L, D = x.shape
    C = up.shape[0]
    wide = low.shape[1]
    n = L // TILE
    rev = lambda i: n - 1 - i
    tok = lambda m: pl.BlockSpec((TILE, m), lambda i: (rev(i), 0))
    fix = lambda s: pl.BlockSpec(s, lambda i: (0,) * len(s))
    above = pl.BlockSpec((16, D), lambda i: (jnp.maximum(rev(i) * (TILE // 16) - 1, 0), 0))
    sd = jax.ShapeDtypeStruct
    return pl.pallas_call(
        mix_backward_kernel,
        grid=(n,),
        in_specs=[tok(C)] * 7
        + [tok(D), above, tok(meta.shape[1]), tok(wide), fix(vec.shape), fix(sq.shape), fix(low.shape), fix(up.shape)],
        out_specs=[tok(D), tok(wide), fix((8, D))],
        out_shape=[sd((L, D), BF), sd((L, wide), BF), sd((8, D), F32)],
        scratch_shapes=[pltpu.VMEM((8, D), F32), pltpu.VMEM((TILE, D), F32)],
        compiler_params=params(),
    )(*grads, x, x, meta, mid, vec, sq, low, up)


AXES = ("sa", "sb", "ra", "rc")
PLANE = ("sb", "ra", "rc")
MESH = pl.DeviceIdType.MESH
HBM = pl.BlockSpec(memory_space=pl.ANY)


class Net:
    def __init__(self, local_sem, send_sem, recv_sem):
        self.sems = local_sem, send_sem, recv_sem
        self.size = tuple(lax.axis_size(k) for k in AXES)
        self.me = tuple(lax.axis_index(k) for k in AXES)
        self.locals, self.n, self.k = [], 0, 0

    def at(self, shift):
        return tuple(lax.rem(m + d, n) if d else m for m, d, n in zip(self.me, shift, self.size))

    def greet(self, shifts):
        bar = pltpu.get_barrier_semaphore()
        for s in shifts:
            pl.semaphore_signal(bar, inc=1, device_id=self.at(s), device_id_type=MESH)
        pl.semaphore_wait(bar, len(shifts))

    def keep(self, src, dst):
        copy = pltpu.make_async_copy(src, dst, self.sems[0].at[self.k])
        self.k += 1
        copy.start()
        self.locals.append(copy)

    def send(self, src, dst, shift):
        copy = pltpu.make_async_remote_copy(
            src, dst, self.sems[1].at[self.n], self.sems[2].at[self.n], device_id=self.at(shift), device_id_type=MESH
        )
        self.n += 1
        copy.start()
        return copy

    def settle(self):
        for copy in self.locals:
            copy.wait()


def call_net(body, arrays, out_shapes, cid, n_local, n_send, scratch=()):
    n = len(arrays)
    m = n + len(out_shapes)

    def kernel(*refs):
        body(refs[:n], refs[n:m], refs[m + 3 :], Net(*refs[m : m + 3]))

    return pl.pallas_call(
        kernel,
        out_shape=out_shapes,
        in_specs=[HBM] * n,
        out_specs=[HBM] * len(out_shapes),
        scratch_shapes=[
            pltpu.SemaphoreType.DMA((max(n_local, 1),)),
            pltpu.SemaphoreType.DMA((n_send,)),
            pltpu.SemaphoreType.DMA((n_send,)),
            *scratch,
        ],
        compiler_params=pltpu.CompilerParams(collective_id=cid, has_side_effects=True, vmem_limit_bytes=VM),
    )(*arrays)


def line_shifts():
    return [(d, 0, 0, 0) for d in range(1, lax.axis_size("sa"))]


def seq_shifts():
    A, B = lax.axis_size("sa"), lax.axis_size("sb")
    return [(i // B, i % B, 0, 0) for i in range(1, A * B)]


CHIPS = [(0, 1, 0, 0), (0, 0, 1, 0), (0, 1, 1, 0)]
OTHER_CORE = (0, 0, 0, 1)


def plane_gather_first(net, src, view):
    slot = net.me[1:]
    net.keep(src, view(*slot))
    far = [net.send(src, view(*slot), s) for s in CHIPS]
    return far, [net.send(src, view(*slot), OTHER_CORE)]


def plane_gather_second(net, view, far, near):
    for s, copy in zip(CHIPS, far):
        copy.wait_recv()
        slot = net.at(s)[1:]
        near.append(net.send(view(*slot), view(*slot), OTHER_CORE))


def plane_gather_end(far, near):
    for copy in far:
        copy.wait_send()
    for copy in near:
        copy.wait()


def line_exchange(arrays, cid):
    def body(ins, outs, _, net):
        shifts = line_shifts()
        net.greet(shifts)
        a = net.me[0]
        open_ = []
        for x, o in zip(ins, outs):
            open_ += [net.send(x.at[net.at(s)[0]], o.at[a], s) for s in shifts]
            net.keep(x.at[a], o.at[a])
        for copy in open_:
            copy.wait()
        net.settle()

    shapes = [jax.ShapeDtypeStruct(x.shape, x.dtype) for x in arrays]
    return call_net(body, arrays, shapes, cid, len(arrays), (lax.axis_size("sa") - 1) * len(arrays))


def swap_first(net, x, o):
    b = net.me[1]
    net.keep(x.at[b], o.at[b])
    return [net.send(x.at[net.at(CHIPS[0])[1]], o.at[b], CHIPS[0])]


def plane_gather(x, cid):
    def body(ins, outs, _, net):
        (x,), (o,) = ins, outs
        view = lambda i, j, k: o.at[i, j, k]
        net.greet(CHIPS + [OTHER_CORE])
        far, near = plane_gather_first(net, x, view)
        plane_gather_second(net, view, far, near)
        plane_gather_end(far, near)
        net.settle()

    sizes = tuple(lax.axis_size(k) for k in PLANE)
    return call_net(body, [x], [jax.ShapeDtypeStruct(sizes + x.shape, x.dtype)], cid, 1, 7)[0]


def plane_shifts():
    return [(0, i // 4, i // 2 % 2, i % 2) for i in range(1, 8)]


def start_exchange(tokens, first_sliced, out_grad, sq, low, up, key, cid):
    A, B = lax.axis_size("sa"), lax.axis_size("sb")
    S = A * B
    sizes = tuple(lax.axis_size(k) for k in PLANE)

    def body(ins, outs, scratch, net):
        x, f, g, q, lo, u, ke = ins
        xo, fo, go, qo, loo, uo, ko, q_line, lo_line = outs
        q_view = lambda i, j, k: qo.at[:, :, i, j, k]
        lo_view = lambda i, j, k: loo.at[:, i, j, k]
        u_view = lambda i, j, k: uo.at[i, j, k]
        g_view = lambda i, j, k: go.at[i, j, k]
        line, seq = line_shifts(), seq_shifts()
        net.greet(seq + [s for s in plane_shifts() if s != CHIPS[0]])
        a, b = net.me[:2]
        me = a * B + b
        first = []
        for s in line:
            first.append(net.send(q.at[net.at(s)[0]], q_line.at[:, a], s))
            first.append(net.send(lo, lo_line.at[a], s))
        net.keep(q.at[a], q_line.at[:, a])
        net.keep(lo, lo_line.at[a])
        rest = []
        for s in seq:
            rest.append(net.send(x.at[net.at(s)[1]], xo.at[me], s))
        for s in seq:
            to = net.at(s)
            rest.append(net.send(f.at[to[1], to[0]], fo.at[me], s))
        for copy in first:
            copy.wait()
        net.settle()
        net.locals = []
        net.keep(x.at[b], xo.at[me])
        net.keep(f.at[b, a], fo.at[me])
        q_open = plane_gather_first(net, q_line, q_view)
        lo_open = plane_gather_first(net, lo_line, lo_view)
        u_open = plane_gather_first(net, u, u_view)
        g_open = plane_gather_first(net, g, g_view)
        slot = net.me[1:]
        rest += [net.send(ke.at[net.at(s)[1:]], ko.at[slot], s) for s in plane_shifts()]
        net.keep(ke.at[slot], ko.at[slot])
        plane_gather_second(net, q_view, *q_open)
        plane_gather_second(net, lo_view, *lo_open)
        plane_gather_second(net, u_view, *u_open)
        plane_gather_second(net, g_view, *g_open)
        for o in (u_open, q_open, lo_open, g_open):
            plane_gather_end(*o)
        for copy in rest:
            copy.wait()
        net.settle()

    sd = lambda shape, like: jax.ShapeDtypeStruct(shape, like.dtype)
    shapes = [
        sd((S,) + tokens.shape[1:], tokens),
        sd((S,) + first_sliced.shape[2:], first_sliced),
        sd(sizes + out_grad.shape, out_grad),
        sd(sq.shape[1:2] + (A,) + sizes + sq.shape[2:], sq),
        sd((A,) + sizes + low.shape, low),
        sd(sizes + up.shape, up),
        sd(key.shape, key),
        sd(sq.shape[1:2] + (A,) + sq.shape[2:], sq),
        sd((A,) + low.shape, low),
    ]
    n_send = 2 * (A - 1) + 2 * (S - 1) + 5 * 7
    return call_net(body, [tokens, first_sliced, out_grad, sq, low, up, key], shapes, cid, 9, n_send)[:7]


def tail_exchange(dh, dfl, sq, down, wide, up, sq3, narrow, ffn, cid):
    A, B = lax.axis_size("sa"), lax.axis_size("sb")
    leads = [2, 1, 1, 0, 0, 0, 0]
    arrays = [sq, down, wide, up, sq3, narrow, ffn]
    blocks = [x.shape[:n] + x.shape[n + 3 :] for x, n in zip(arrays, leads)]
    n = len(arrays)

    def body(ins, outs, scratch, net):
        d, f, ps = ins[0], ins[1], ins[2:]
        do, fo, pos = outs[0], outs[1], outs[2:]
        own, other, chips = scratch[:n], scratch[n : 2 * n], scratch[2 * n :]
        seq = seq_shifts()
        net.greet(seq + CHIPS[1:] + [OTHER_CORE])
        a, b, y, c = net.me
        there = net.at(OTHER_CORE)[3]
        pairs = [(i // 2, i % 2) for i in range(4)]

        def block(t, i, j, k):
            return ps[t].at[(slice(None),) * leads[t] + (i, j, k)]

        cores, mine = [], []
        for t in range(n):
            cores.append([net.send(block(t, i, j, there), other[t].at[2 * i + j], OTHER_CORE) for i, j in pairs])
            for i, j in pairs:
                net.keep(block(t, i, j, c), own[t].at[2 * i + j])
            mine.append(net.locals)
            net.locals = []
        open_ = [net.send(d.at[net.at(s)[0]], do.at[a], s) for s in line_shifts()]
        net.keep(d.at[a], do.at[a])
        net.keep(f.at[a * B + b], fo.at[b, a])

        def add(t, k, terms):
            shape = blocks[t]
            step = min(shape[-2], 16)
            per = shape[-2] // step
            count = per
            for size in shape[:-2]:
                count = count * size

            @pl.loop(0, count)
            def _(r):
                index = []
                rest = r // per
                for size in reversed(shape[:-2]):
                    index.insert(0, rest % size)
                    rest = rest // size
                at = (*index, pl.ds(pl.multiple_of(r % per * step, step), step))
                total = own[t][(k, *at)].astype(F32)
                for ref, i in terms:
                    total = total + ref[(i, *at)].astype(F32)
                own[t][(k, *at)] = total.astype(BF)

        sent = []
        for t in range(n):
            for copy in cores[t] + mine[t]:
                copy.wait()
            for k, s in enumerate(CHIPS):
                to = net.at(s)
                slot = 2 * to[1] + to[2]
                add(t, slot, [(other[t], slot)])
                sent.append(net.send(own[t].at[slot], chips[t].at[k], s))
        for s in seq:
            to = net.at(s)
            open_.append(net.send(f.at[to[0] * B + to[1]], fo.at[b, a], s))
        me = 2 * b + y
        for t in range(n):
            for copy in sent[3 * t : 3 * t + 3]:
                copy.wait_recv()
            add(t, me, [(other[t], me)] + [(chips[t], k) for k in range(3)])
            net.keep(own[t].at[me], pos[t])
        for copy in sent:
            copy.wait_send()
        for copy in open_:
            copy.wait()
        net.settle()

    sd = jax.ShapeDtypeStruct
    shapes = [sd(dh.shape, dh.dtype), sd((B, A) + dfl.shape[1:], dfl.dtype)] + [sd(s, BF) for s in blocks]
    scratch = [pltpu.VMEM((m,) + s, BF) for m in (4, 4, 3) for s in blocks]
    n_send = (A - 1) + (A * B - 1) + 7 * n
    return call_net(body, [dh, dfl, *arrays], shapes, cid, 2 + 5 * n, n_send, scratch)


def last_exchange(swaps, sq, lines, cid):
    m = len(swaps)

    def body(ins, outs, _, net):
        net.greet(line_shifts() + [CHIPS[0]])
        a = net.me[0]
        open_ = []
        for i, (x, o) in enumerate(zip(ins, outs)):
            if i < m:
                open_ += swap_first(net, x, o)
                continue
            view = (lambda x, k: x.at[:, k]) if i == m else (lambda x, k: x.at[k])
            open_ += [net.send(view(x, net.at(s)[0]), o.at[a], s) for s in line_shifts()]
            net.keep(view(x, a), o.at[a])
        for copy in open_:
            copy.wait()
        net.settle()

    sd = jax.ShapeDtypeStruct
    arrays = [*swaps, sq, *lines]
    shapes = [sd(x.shape, x.dtype) for x in arrays]
    shapes[m] = sd((sq.shape[1], sq.shape[0]) + sq.shape[2:], sq.dtype)
    n_send = m + (1 + len(lines)) * (lax.axis_size("sa") - 1)
    return call_net(body, arrays, shapes, cid, len(arrays), n_send)


def layer_norm(x, gain, bias):
    cen = x - jnp.mean(x, axis=-1, keepdims=True)
    var = jnp.mean(cen * cen, axis=-1, keepdims=True)
    return cen * lax.rsqrt(var + 1e-05) * gain + bias


def next_line(value, steps):
    count = lax.axis_size("sa")
    first, last = max(0, -steps), min(count, count - steps)
    return lax.ppermute(value, "sa", [(i, i + steps) for i in range(first, last)])


def after(value, *others):
    return lax.optimization_barrier((value, *others))[0]


def per_device(tokens, first_values, lengths, vectors, down, up, square, key_w, value_w, out_grad):
    rows_here, seg, D = tokens.shape
    SA, SB, RA, RC = (lax.axis_size(k) for k in AXES)
    a, b = lax.axis_index("sa"), lax.axis_index("sb")
    S, F = SA * SB, SB * RA * RC
    L = seg * S
    C = D // SA
    NB = L // BLK
    gc = min(C, 256)
    T = SB * seg
    w = square.shape[1]
    n_low, n_vec = down.shape[1], vectors.shape[0]
    FS = key_w.shape[1] // (S * RA * RC)

    lens = lax.dynamic_index_in_dim(lengths, b, 0, keepdims=False)
    count = lens.shape[0]
    lower = jnp.arange(count)[:, None] > jnp.arange(count)[None, :]
    starts = jnp.sum(jnp.where(lower, lens[None, :], 0), axis=1)
    pos = jnp.arange(L, dtype=jnp.int32)
    reset = jnp.any(pos[:, None] == starts[None, :], axis=1).astype(F32)
    segid = jnp.sum((pos[:, None] >= starts[None, :]).astype(F32), axis=1) - 1.0
    blocks = segid.reshape(NB, BLK)
    before = blocks[:, :1] - reset.reshape(NB, BLK)[:, :1]
    carried = (blocks == before).astype(F32).reshape(L)
    live = (blocks == blocks[:, -1:]).astype(F32).reshape(L)
    meta = jnp.stack([segid, carried, live, 1.0 - reset], axis=1)
    segrow = jnp.tile(blocks.reshape(NB, 1, BLK), (1, 1, gc // SD))
    keep_row = (1.0 - reset)[:, None]
    keep_own = lax.dynamic_slice(keep_row, (a * T, 0), (T, 1))

    sq3 = lax.all_gather(square[3], AXES, axis=0, tiled=True)
    first_sliced = first_values.reshape(rows_here, seg, SA, C).transpose(0, 2, 1, 3)
    cuts = [0, DECAY_INNER, DECAY_INNER + LA, DECAY_INNER + LA + LV, n_low]

    def widen(m):
        pieces = [m[:, i:j] for i, j in zip(cuts[:-1], cuts[1:])]
        return jnp.concatenate([jnp.pad(p, ((0, 0), (0, -p.shape[1] % 128))) for p in pieces], axis=1)

    wide_at = [0, 128, 256, 384]
    low_mine = jnp.concatenate([widen(down), jnp.pad(vectors.T, ((0, 0), (0, 128 - n_vec)))], axis=1)
    sq_mine = square[:3].reshape(3, w, SA, C).transpose(2, 0, 1, 3)
    half = SA * FS
    key_mine = key_w.reshape(w, SA, F, FS).transpose(2, 0, 1, 3).reshape(SB, RA, RC, w, half)
    x_row, first_row, g_plane, sq, low, up_heads, key_line = start_exchange(
        tokens, first_sliced, out_grad, sq_mine, low_mine, widen(up.T), key_mine, 1
    )
    x_row = x_row.reshape(L, D)
    first_row = first_row.reshape(L, C)
    sq = sq.reshape(3, D, C)
    low = low.reshape(D, 768)
    low_w = low[:, :640]
    up_w = up_heads.reshape(C, 640)
    vec = low[:, 640 : 640 + n_vec].astype(F32).T
    vec_heads = lax.dynamic_slice(vec, (10, a * C), (8, C))
    FW = F * w
    halves = [slice(i * half, (i + 1) * half) for i in range(D // half)]
    kv = jnp.concatenate([key_line.reshape(FW, half), *(value_w[:, s] for s in halves)], axis=0)
    kv_all = lax.all_gather(kv, "sa", axis=0)
    key_all = kv_all[:, :FW].reshape(D, half)
    value_all = jnp.concatenate(
        [kv_all[:, FW + i * FS : FW + (i + 1) * FS].reshape(half, half) for i in range(D // half)], axis=1
    )
    g_all = g_plane.transpose(3, 1, 2, 0, 4, 5).reshape(F * T, D)
    slot = (b * RA + lax.axis_index("ra")) * RC + lax.axis_index("rc")
    g_own = lax.dynamic_slice(g_all, (slot * T, 0), (T, D)).astype(F32)

    xm, (rp, kp, vp, uw, ua, uv, ug), mid, mid_low = mix_forward(x_row, meta, vec, sq, low_w, up_w)
    ins = (rp, kp, vp, uw, ua, uv, first_row)
    y, saved = recurrence_forward(ins, vec_heads, meta, segrow)
    z = (y.astype(F32) * ug).astype(BF)
    (z_own,) = line_exchange([z.reshape(SA, T, C)], 2)
    z_own = z_own.transpose(1, 0, 2).reshape(T, D)

    x_own = lax.dynamic_slice(x_row, (a * T, 0), (T, D)).astype(F32)
    x1 = x_own + mm(z_own, sq3, NN)
    h2, norm2_pull = jax.vjp(layer_norm, x1, vec[2], vec[3])
    edge2 = next_line(h2[-1:], 1)

    def channel_mix(h, edge, mix):
        s = jnp.concatenate([edge, h[:-1]], axis=0) * keep_own
        return h + (s - h) * mix

    xc, cmix_pull = jax.vjp(channel_mix, h2, edge2, vec[18])
    xc_all = plane_gather(xc.astype(BF), 3).reshape(F * T, D)
    kc = jax.nn.relu(mm(xc_all, key_all, NN))
    q = (kc * kc).astype(BF)
    dkc = (mm(g_all, value_all, NT) * 2.0 * kc).astype(BF)
    dxc = lax.psum_scatter(mm(dkc, key_all, NT).astype(BF), PLANE, scatter_dimension=0, tiled=True)
    ffn_part = mm(q, value_all, NN).astype(BF)
    value_part = mm(q, g_all, TN).astype(BF).reshape(SA, FS, D)
    key_part = mm(xc_all, dkc, TN).astype(BF).reshape(SA, FW, half)
    kv_part = jnp.concatenate([key_part, *(value_part[:, :, s] for s in halves)], axis=1)
    dxc, kv_part, ffn_part = lax.optimization_barrier((dxc, kv_part, ffn_part))

    dh2, dedge2, g18 = cmix_pull(dxc.astype(F32))
    dh2 = dh2.at[-1:].add(next_line(dedge2, -1))
    dx1n, g2, g3 = norm2_pull(dh2)
    dx1 = g_own + dx1n
    dt = dx1.astype(BF)
    dz = mm(dt, sq3, NT).astype(BF)
    (dz_row,) = line_exchange([dz.reshape(T, SA, C).transpose(1, 0, 2)], 4)
    dt_row = lax.all_gather(dt, "sa", axis=0, tiled=True)
    kv_grad = lax.psum_scatter(after(kv_part, dz).reshape(-1, half), "sa", scatter_dimension=0, tiled=True)
    dz_row = dz_row.reshape(L, C).astype(F32)

    dy = (dz_row * ug).astype(BF)
    dug = (dz_row * y.astype(F32)).astype(BF)
    drp, dkp, dvp, duw, dua, duv, dfl, dvec = recurrence_backward(dy, saved, ins, vec_heads, meta, segrow)
    dh1, dd, gmix = mix_backward((drp, dkp, dvp, duw, dua, duv, dug), x_row, meta, mid, vec, sq, low_w, up_w)
    g0, g1 = gmix[6], gmix[7]

    sq_part, down_part, up_part, sq3_part = weight_grads(xm, (drp, dkp, dvp, duw, dua, duv, dug), dd, mid_low, z, dt_row)
    wide = jnp.stack([g0, g1, g2, g3, *(gmix[i] for i in range(6)), g18] + [jnp.zeros_like(g0)] * 5).astype(BF)
    wide = jnp.pad(wide.T, ((0, 0), (0, 112)))
    narrow = jnp.pad(dvec.astype(BF).T, ((0, 0), (0, 120)))
    plane = (SB, RA, RC, w)
    dh1_own, dfl_own, sq_sum, down_sum, wide_sum, up_sum, sq3_sum, narrow_sum, ffn = tail_exchange(
        dh1.reshape(SA, T, D),
        dfl.reshape(S, seg, C),
        sq_part.reshape((3, SA) + plane + (C,)),
        down_part.reshape((SA,) + plane + (640,)),
        wide.reshape((SA,) + plane + (128,)),
        up_part.reshape(plane + (640,)),
        sq3_part.reshape(plane + (D,)),
        narrow.reshape(plane + (128,)),
        ffn_part.reshape(SB, RA, RC, T, D),
        5,
    )
    dh1_own = jnp.sum(dh1_own.astype(F32), axis=0)
    _, norm1_pull = jax.vjp(lambda x: layer_norm(x, vec[0], vec[1]), x_own)
    (dx0,) = norm1_pull(dh1_own)
    mixed = (x1 + ffn.astype(F32)).astype(BF)
    tokens_grad, mixed_out, sq_sum, down_sum, wide_sum = last_exchange(
        [(dx1 + dx0).astype(BF).reshape(SB, seg, D), mixed.reshape(SB, seg, D)], sq_sum, [down_sum, wide_sum], 6
    )
    first_grad = dfl_own.transpose(0, 2, 1, 3).reshape(rows_here, seg, D)
    square_grad = jnp.concatenate([sq_sum.transpose(1, 2, 0, 3).reshape(3, w, D), sq3_sum[None]], axis=0).astype(F32)
    narrow_pieces = lambda m: [m[:, i : i + q - p] for i, p, q in zip(wide_at, cuts[:-1], cuts[1:])]
    down_grad = jnp.concatenate(narrow_pieces(jnp.sum(down_sum.astype(F32), axis=0)), axis=1)
    up_grad = jnp.concatenate(narrow_pieces(up_sum.astype(F32)), axis=1).T
    wide_t = jnp.sum(wide_sum.astype(F32), axis=0)[:, :16].T
    narrow_t = narrow_sum[:, :8].astype(F32).T
    vectors_gradient = jnp.concatenate([wide_t[:10], narrow_t, wide_t[10:11]], axis=0)
    value_grad = jnp.concatenate([kv_grad[FW + i * FS : FW + (i + 1) * FS] for i in range(D // half)], axis=1)
    value_grad = value_grad.astype(F32)
    key_grad = lax.all_to_all(kv_grad[:FW].reshape(F, w, half), PLANE, split_axis=0, concat_axis=0, tiled=True)
    key_grad = key_grad.reshape(F, w, SA, FS).transpose(1, 2, 0, 3).reshape(w, -1).astype(F32)
    return (
        mixed_out,
        tokens_grad,
        first_grad,
        vectors_gradient,
        down_grad,
        up_grad,
        square_grad,
        key_grad,
        value_grad,
    )


def solution(mesh):
    seq, row = mesh.shape["seq"], mesh.shape["row"]
    fine = Mesh(mesh.devices.reshape(seq // 2, 2, row // 2, 2), AXES)
    S, R = ("sa", "sb"), ("ra", "rc")
    in_specs = (
        P(R, S, None),
        P(R, S, None),
        P(R, None),
        P(None, S + R),
        P(S + R, None),
        P(None, S + R),
        P(None, S + R, None),
        P(S + R, None),
        P(S + R, None),
        P(R, S, None),
    )
    out_specs = (
        P(R, S, None),
        P(R, S, None),
        P(R, S, None),
        P(None, S + R),
        P(S + R, None),
        P(None, S + R),
        P(None, S + R, None),
        P(S + R, None),
        P(S + R, None),
    )
    return jax.shard_map(per_device, mesh=fine, in_specs=in_specs, out_specs=out_specs, check_vma=False)
```

time: 4970 us -> 1110 us (0.22)
  waiting for transfers between devices: 1700 us -> 38.3 us
  other arithmetic: 1470 us -> 50.8 us
  Pallas kernels: 0 us -> 805 us
  matrix products: 759 us -> 89.6 us
  local copies, waits for them, and re-layouts: 731 us -> 90.5 us
  blocking collectives: 186 us -> 0 us
  starting transfers between devices: 80.3 us -> 13.3 us
    another operation x164 -> x2, other arithmetic: 1300 us -> 0.87 us  [the longest x96 1280 us: block_step(): jax.scipy.linalg.solve_triangular(system, right_hand, lower=True, unit_di...]
    reduce_scatter x4 -> x2, waiting for transfers between devices: 859 us -> 23.8 us  [the longest x1 23.8 us: per_device(): lax.psum_scatter(mm(dkc, key_all, NT).astype(BF), PLANE, scatter_dimensio...]
    pallas_call x0 -> x13, Pallas kernels: none -> 805 us  [the longest x6 590 us: call_net(): pl.pallas_call(kernel, out_shape=out_shapes, in_specs=[HBM] * n, out_spec...]
    dot_general x689 -> x8, matrix products: 711 us -> 89.6 us  [mm(): return lax.dot_general(a, b, d, preferred_element_type=F32)]
    all_to_all x16 -> x1, waiting for transfers between devices: 541 us -> 10.7 us  [per_device(): lax.all_to_all(kv_grad[:FW].reshape(F, w, half), PLANE, split_axis=0, con...]
    all_gather x11 -> x3, waiting for transfers between devices: 237 us -> 0.02 us  [the longest x1 0.02 us: per_device(): kv_all = lax.all_gather(kv, 'sa', axis=0)]
    all_gather x9 -> x0, blocking collectives: 169 us -> none  [the longest x1 66.8 us: per_device(): lax.all_gather(grad_down_low[2], 'row', axis=0, tiled=True)]
    another operation x56 -> x7, local copies, waits for them, and re-layouts: 118 us -> 2.11 us  [the longest x1 1.08 us: per_device(): meta = jnp.stack([segid, carried, live, 1.0 - reset], axis=1)]
  transfers between devices with their start and end apart: 38 -> 8, of which waited for: 23 -> 3; matrix products, arithmetic and copies ran while one was open for 29% -> 14% of each run, Pallas kernels for 0% -> 68%
where the time goes in v1:
time: 1110 us; the launch traced here: 1100 us
  Pallas kernels  805 us (73%)
  local copies, waits for them, and re-layouts  90.5 us (8%)
  matrix products  89.6 us (8%)
  other arithmetic  50.8 us (5%)
  waiting for transfers between devices  38.3 us (3%)
  between operations  14.8 us (1%)
  starting transfers between devices  13.3 us (1%)
    pallas_call x6, Pallas kernels, call_net(): pl.pallas_call(kernel, out_shape=out_shapes, in_specs=[HBM] * n, out_spec...  590 us
    dot_general x8, matrix products, mm(): return lax.dot_general(a, b, d, preferred_element_type=F32)  89.6 us
    pallas_call x1, Pallas kernels, recurrence_backward(): pl.pallas_call(backward_kernel, grid=(NB,), in_specs=[rowb] * 10 + [sb] +...  58.6 us
    pallas_call x1, Pallas kernels, recurrence_forward(): pl.pallas_call(forward_kernel, grid=(NB,), in_specs=[rowb] * 7 + [fix((8,...  37.3 us
    pallas_call x1, Pallas kernels, mix_backward(): pl.pallas_call(mix_backward_kernel, grid=(n,), in_specs=[tok(C)] * 7 + [t...  35.2 us
    pallas_call x1, Pallas kernels, mix_forward(): pl.pallas_call(mix_forward_kernel, grid=(L // TILE,), in_specs=[tok(D), t...  31 us
    pallas_call x1, Pallas kernels, weight_grads(): pl.pallas_call(weight_kernel, grid=(D // n,), in_specs=[feat] * 6 + [fix(...  25.7 us
    reduce_scatter x1, waiting for transfers between devices, per_device(): lax.psum_scatter(mm(dkc, key_all, NT).astype(BF), PLANE, scatter_dimensio...  23.8 us
  transfers between devices with their start and end apart: 8, of which 3 were waited for; matrix products, arithmetic and copies ran while one was open for 14% of the time, Pallas kernels for 68%

profile of v1, /device:TPU:0, one launch (start us, length us, event | category | flops | bytes accessed | tf_op | source)
XLA Modules:
  0.0 1102.6 jit_solution(7252177389768548973)
XLA Ops:
  19.9 209.9 %shard_map.169 = (bf16[8,128,2048]{2,1,0:T(8,128)(2,1)}, bf16[8,128,512]{2,1,0:T(8,128)(2,1)}, bf16[2,2,2,2,128,2048]{5,4,3,2,1,0:T(8,128)(2,1)}, bf16[3,4,2,2,2...) custom-call(bf16[2,128,2048]{2,1,0:T(8,128)(2,1)} %refs_0_.1, ...), custom_call_target="tpu_custom_call" | custom-call | tf_op jit(solution)/shard_map/pallas_call | solution.py:468
  235.7 8.4 copy.163
  248.8 31.0 %shard_map.170 = (bf16[1024,2048]{1,0:T(8,128)(2,1)}, bf16[1024,2048]{1,0:T(8,128)(2,1)}, bf16[1024,2048]{1,0:T(8,128)(2,1)}, bf16[1024,2048]{1,0:T(8,128)(2,1)}...) custom-call(bf16[1024,2048]{1,0:T(8,128)(2,1)} %bitcast.115, ...), custom_call_target="tpu_custom_call" | custom-call | tf_op jit(solution)/shard_map/pallas_call | solution.py:386
  281.2 17.0 %shard_map.171 = (bf16[1024,512]{1,0:T(8,128)(2,1)}, bf16[1024,512]{1,0:T(8,128)(2,1)}, bf16[1024,512]{1,0:T(8,128)(2,1)}, bf16[1024,512]{1,0:T(8,128)(2,1)}, bf...) custom-call(f32[1024,512]{1,0:T(8,128)} %get-tuple-element.93.rp, ...), custom_call_target="tpu_custom_call" | custom-call | tf_op jit(solution)/shard_map/pallas_call | solution.py:218
  311.2 10.2 shard_map.172
  332.2 37.3 %shard_map.173 = (bf16[1024,512]{1,0:T(8,128)(2,1)}, f32[1024,512]{1,0:T(8,128)}, bf16[1024,512]{1,0:T(8,128)(2,1)}, bf16[16,2,256,256]{3,2,1,0:T(8,128)(2,1)}) custom-call(bf16[1024,512]{1,0:T(8,128)(2,1)} %get-tuple-element.100.rs, bf16[1024,512]{1,0:T(8,128)(2,1)} %get-tuple-element.101.ws, bf16[1024,512]{1,0:T(8,128)(2,1)} %get-tuple-element.102.ks, ...), custom_call_target="tpu_custom_call" | custom-call | tf_op jit(solution)/shard_map/pallas_call | solution.py:224
  372.2 61.8 %shard_map.174 = bf16[4,256,512]{2,1,0:T(8,128)(2,1)} custom-call(bf16[4,256,512]{2,1,0:T(8,128)(2,1)} %bitcast.133), custom_call_target="tpu_custom_call" | custom-call | tf_op jit(solution)/shard_map/pallas_call | solution.py:468
  446.0 7.9 collective-permute-start
  464.7 51.8 %shard_map.175 = bf16[2,2,2,256,2048]{4,3,2,1,0:T(8,128)(2,1)} custom-call(bf16[256,2048]{1,0:T(8,128)(2,1)} %add_convert_fusion.2.refs_0_), custom_call_target="tpu_custom_call" | custom-call | tf_op jit(solution)/shard_map/pallas_call | solution.py:468
  516.5 15.0 %fusion.51 = f32[2048,1024]{1,0:T(8,128)} fusion(bf16[2048,2048]{1,0:T(8,128)(2,1)} %bitcast.135, bf16[2048,1024]{1,0:T(8,128)(2,1)} %bitcast.146), kind=kOutput, calls=%fused_computation.135 | convolution fusion | flops 8589934592 | bytes 20971520 | tf_op jit(solution)/shard_map/dot_general | solution.py:16
  531.5 12.7 %multiply_convert_fusion.1 = bf16[2048,1024]{1,0:T(8,128)(2,1)S(1)} fusion(f32[2048,1024]{1,0:T(8,128)} %fusion.51, bf16[2048,2048]{1,0:T(8,128)(2,1)} %bitcast.129, bf16[1024,1024]{1,0:T(8,128)(2,1)S(1)} %bitcast.174, bf16[1024,1024]{1,0:T(8,128)(2,1)S(1)} %bitcast.172), kind=kOutput, calls=%fused_computation.7 | convolution fusion | flops 8606711808 | bytes 25165824 | tf_op jit(solution)/shard_map/dot_general | solution.py:16
  546.2 10.9 convolution_convert_fusion.1
  557.2 14.8 %convolution_convert_fusion.2 = bf16[1024,2048]{1,0:T(8,128)(2,1)S(1)} fusion(bf16[2048,2048]{1,0:T(8,128)(2,1)} %bitcast.130, f32[2048,1024]{1,0:T(8,128)} %fusion.51), kind=kOutput, calls=%fused_computation.12 | convolution fusion | flops 8598323200 | bytes 20971520 | tf_op jit(solution)/shard_map/dot_general | solution.py:16
  574.2 11.9 %convolution_convert_fusion.3 = bf16[2048,1024]{1,0:T(8,128)(2,1)S(1)} fusion(bf16[2048,2048]{1,0:T(8,128)(2,1)} %bitcast.136, bf16[2048,1024]{1,0:T(8,128)(2,1)S(1)} %copy-done.38), kind=kOutput, calls=%fused_computation.13 | convolution fusion | flops 8592031744 | bytes 16777216 | tf_op jit(solution)/shard_map/dot_general | solution.py:16
  591.3 11.2 %convolution_convert_fusion = bf16[2048,2048]{1,0:T(8,128)(2,1)} fusion(bf16[1024,1024]{1,0:T(8,128)(2,1)S(1)} %bitcast.175, bf16[1024,1024]{1,0:T(8,128)(2,1)S(1)} %bitcast.173, f32[2048,1024]{1,0:T(8,128)S(1)} %bitcast.196), kind=kOutput, calls=%fused_computation.8 | convolution fusion | flops 8608808960 | bytes 20971520 | tf_op jit(solution)/shard_map/dot_general | solution.py:16
  602.5 23.8 %reduce-scatter.3.cloned.1.call-done = bf16[256,2048]{1,0:T(8,128)(2,1)} async-done(((bf16[2048,2048]{1,0:T(8,128)(2,1)}), bf16[256,2048]{1,0:T(8,128)(2,1)}) %reduce-scatter.3.cloned.1.call-update) | async-done | bytes 1048592 | tf_op jit(solution)/shard_map/reduce_scatter | solution.py:837
  644.4 7.1 fusion.9
  655.9 37.0 %shard_map.176 = bf16[4,256,512]{2,1,0:T(8,128)(2,1)} custom-call(bf16[4,256,512]{2,1,0:T(8,128)(2,1)} %bitcast.153), custom_call_target="tpu_custom_call" | custom-call | tf_op jit(solution)/shard_map/pallas_call | solution.py:468
  696.7 58.6 %shard_map.177 = (bf16[1024,512]{1,0:T(8,128)(2,1)}, bf16[1024,512]{1,0:T(8,128)(2,1)}, bf16[1024,512]{1,0:T(8,128)(2,1)}, bf16[1024,512]{1,0:T(8,128)(2,1)}, bf...) custom-call(bf16[1024,512]{1,0:T(8,128)(2,1)} %get-tuple-element.222.dy, ...), custom_call_target="tpu_custom_call" | custom-call | tf_op jit(solution)/shard_map/pallas_call | solution.py:238
  755.3 35.2 %shard_map.178 = (bf16[1024,2048]{1,0:T(8,128)(2,1)}, bf16[1024,640]{1,0:T(8,128)(2,1)}, f32[8,2048]{1,0:T(8,128)}) custom-call(bf16[1024,512]{1,0:T(8,128)(2,1)} %get-tuple-element.113.drp, bf16[1024,512]{1,0:T(8,128)(2,1)} %get-tuple-element.114.dkp, bf16[1024,512]{1,0:T(8,128)(2,1)} %get-tuple-element.115.dvp, bf16[1024,512]{1,0:T(8,128)(2,1)} %get-tuple-element.116.duw, ...), custom_call_target="tpu_custom_call" | custom-call | tf_op jit(solution)/shard_map/pallas_call | solution.py:408
  793.8 25.7 %shard_map.179 = (bf16[3,2048,512]{2,1,0:T(8,128)(2,1)}, bf16[2048,640]{1,0:T(8,128)(2,1)}, bf16[512,640]{1,0:T(8,128)(2,1)}, bf16[512,2048]{1,0:T(8,128)(2,1)}) custom-call(bf16[1024,2048]{1,0:T(8,128)(2,1)} %get-tuple-element.122.x0, bf16[1024,2048]{1,0:T(8,128)(2,1)} %get-tuple-element.123.x1, bf16[1024,2048]{1,0:T(8,128)(2,1)} %get-tuple-element.124.x2, ...), custom_call_target="tpu_custom_call" | custom-call | tf_op jit(solution)/shard_map/pallas_call | solution.py:361
  819.4 181.4 %shard_map.180 = (bf16[4,256,2048]{2,1,0:T(8,128)(2,1)}, bf16[2,4,128,512]{3,2,1,0:T(8,128)(2,1)}, bf16[3,4,64,512]{3,2,1,0:T(8,128)(2,1)}, bf16[4,64,640]{2,1,0...) custom-call(bf16[4,256,2048]{2,1,0:T(8,128)(2,1)} %bitcast.144, ...), custom_call_target="tpu_custom_call" | custom-call | tf_op jit(solution)/shard_map/pallas_call | solution.py:468
  1012.8 48.4 %shard_map.181 = (bf16[2,128,2048]{2,1,0:T(8,128)(2,1)}, bf16[2,128,2048]{2,1,0:T(8,128)(2,1)}, bf16[4,3,64,512]{3,2,1,0:T(8,128)(2,1)}, bf16[4,64,640]{2,1,0:T(8,128)(2,1)}, bf16[4,64,128]{2,1,0:T(8,128)(2,1)}) custom-call(bf16[2,128,2048]{2,1,0:T(8,128)(2,1)} %bitcast.150, bf16[2,128,2048]{2,1,0:T(8,128)(2,1)} %bitcast.149, ...), custom_call_target="tpu_custom_call" | custom-call | tf_op jit(solution)/shard_map/pallas_call | solution.py:468
  1078.0 10.7 all-to-all-done
  (237 shorter events, 148.1 us)
Async XLA Ops:
  7.2 225.6 %copy-start = (s32[2,4]{1,0:T(2,128)S(1)}, s32[2,4]{1,0:T(2,128)}, u32[]{:S(2)}) copy-start(s32[2,4]{1,0:T(2,128)} %param.14) | copy-start | bytes 100
  7.2 6.1 slice-start
  7.2 7.0 copy-start.20
  7.2 430.5 %all-gather.10.cloned.1.call-start = ((), (), s32[]{:S(2)}) async-start(), calls=%async_computation.7 | async-start | bytes 8650752 | tf_op jit(solution)/shard_map/all_gather | solution.py:780
  9.1 444.8 %all-gather.8.cloned.1.call-start = ((), (), s32[]{:S(2)}) async-start(), calls=%async_computation.6 | async-start | bytes 10485760 | tf_op jit(solution)/shard_map/all_gather | solution.py:807
  19.9 209.9 %copy-start.22 = (bf16[256,2048]{1,0:T(8,128)(2,1)S(1)}, bf16[256,2048]{1,0:T(8,128)(2,1)}, u32[]{:S(2)}) copy-start(bf16[256,2048]{1,0:T(8,128)(2,1)} %param.20) | copy-start | bytes 3145732
  232.5 393.8 %reduce-scatter.3.cloned.1.call-start = ((), (), s32[]{:S(2)}) async-start(), calls=%async_computation.3 | async-start | bytes 9437184 | tf_op jit(solution)/shard_map/reduce_scatter | solution.py:837
  235.7 8.4 copy-start.14
  332.2 37.3 %copy-start.9 = (f32[1024,512]{1,0:T(8,128)S(1)}, f32[1024,512]{1,0:T(8,128)}, u32[]{:S(2)}) copy-start(f32[1024,512]{1,0:T(8,128)} %get-tuple-element.108) | copy-start | bytes 6291460
  446.0 16.6 %collective-permute-start = (f32[1,2048]{1,0:T(1,128)S(1)}, f32[1,2048]{1,0:T(1,128)S(1)}, u32[]{:S(2)}, u32[]{:S(2)}) collective-permute-start(f32[1,2048]{1,0:T(1,128)S(1)} %slice.229), channel_id=1, source_target_pairs={{0,8},{8,16},{16,24},{1,9},{9,17},{17,25},{2,10},{10,18},{18,26},{... | collective-permute-start | bytes 24584 | tf_op jit(solution)/shard_map/ppermute | solution.py:743
  453.9 6.2 copy-start.10
  516.4 15.0 %copy-start.16 = (bf16[4,256,1024]{2,1,0:T(8,128)(2,1)S(1)}, bf16[4,256,1024]{2,1,0:T(8,128)(2,1)}, u32[]{:S(2)}) copy-start(bf16[4,256,1024]{2,1,0:T(8,128)(2,1)} %get-tuple-element.211) | copy-start | bytes 6291460
  516.4 15.0 %copy-start.18 = (bf16[4,256,1024]{2,1,0:T(8,128)(2,1)S(1)}, bf16[4,256,1024]{2,1,0:T(8,128)(2,1)}, u32[]{:S(2)}) copy-start(bf16[4,256,1024]{2,1,0:T(8,128)(2,1)} %get-tuple-element.212) | copy-start | bytes 6291460
  531.5 14.7 %copy-start.11 = (bf16[4,512,1024]{2,1,0:T(8,128)(2,1)S(1)}, bf16[4,512,1024]{2,1,0:T(8,128)(2,1)}, u32[]{:S(2)}) copy-start(bf16[4,512,1024]{2,1,0:T(8,128)(2,1)} %slice.232) | copy-start | bytes 12582916
  557.1 236.6 %all-gather.6.cloned.1.call-start = ((), (), s32[]{:S(2)}) async-start(), calls=%async_computation.4 | async-start | bytes 5242880 | tf_op jit(solution)/shard_map/all_gather | solution.py:851
  572.0 18.5 %slice-start.1 = ((s8[8388608]{0:T(1024)(128)(4,1)}), s8[4194304]{0:T(1024)(128)(4,1)S(1)}, s32[]{:S(2)}) async-start(s8[8388608]{0:T(1024)(128)(4,1)} %bitcast.195), calls=%async_computation.9 | async-start | bytes 8388608
  574.2 16.2 %slice-start.2 = ((s8[8388608]{0:T(1024)(128)(4,1)}), s8[4194304]{0:T(1024)(128)(4,1)S(1)}, s32[]{:S(2)}) async-start(s8[8388608]{0:T(1024)(128)(4,1)} %bitcast.195), calls=%async_computation.10 | async-start | bytes 8388608
  630.1 5.7 collective-permute-start.1
  644.4 424.0 %reduce-scatter.5.cloned.1.call-start = ((), (), s32[]{:S(2)}) async-start(), calls=%async_computation.5 | async-start | bytes 10485760 | tf_op jit(solution)/shard_map/reduce_scatter | solution.py:852
  655.9 37.0 %copy-start.13 = (bf16[1024,512]{1,0:T(8,128)(2,1)S(1)}, bf16[1024,512]{1,0:T(8,128)(2,1)}, u32[]{:S(2)}) copy-start(bf16[1024,512]{1,0:T(8,128)(2,1)} %get-tuple-element.107) | copy-start | bytes 3145732
  755.3 36.1 %copy-start.34 = (f32[8,512]{1,0:T(8,128)S(1)}, f32[8,512]{1,0:T(8,128)}, u32[]{:S(2)}) copy-start(f32[8,512]{1,0:T(8,128)} %get-tuple-element.135) | copy-start | bytes 49156
  1012.8 50.7 %copy-start.33 = (bf16[64,128]{1,0:T(8,128)(2,1)S(1)}, bf16[64,128]{1,0:T(8,128)(2,1)}, u32[]{:S(2)}) copy-start(bf16[64,128]{1,0:T(8,128)(2,1)} %get-tuple-element.146) | copy-start | bytes 49156
  1068.4 6.5 copy-start.29
  1070.7 17.9 %all-to-all-start = ((bf16[8,64,1024]{2,1,0:T(8,128)(2,1)}), bf16[8,64,1024]{2,1,0:T(8,128)(2,1)S(1)}, u32[]{:S(2)}, u32[]{:S(2)}) async-start(bf16[8,64,1024]{2,1,0:T(8,128)(2,1)} %bitcast.59), calls=%async_computation.2 | async-start | bytes 2097152 | tf_op jit(solution)/shard_map/all_to_all | solution.py:895
  (26 other events, 65.1 us)
Sparse Core Ops, SparseCore 0:
  10.9 173.7 all-gather.9
  232.7 198.8 all-gather.7
  557.2 69.0 reduce-scatter.2
  644.5 101.8 all-gather.5
  748.7 211.6 reduce-scatter.4

commit v2 on v1

--- a/solution.py
+++ b/solution.py
@@ -1,3 +1,5 @@
+import functools
+
 import jax
 import jax.numpy as jnp
 from jax import lax
@@ -32,16 +34,19 @@
             out=jnp.where(s.head==h,x[h*BLK:(h+1)*BLK],out)
         return out
 
-def headsum(x,ones):
-    hi=x.astype(BF); lo=(x-hi.astype(F32)).astype(BF)
-    return mm(hi,ones,NN)+mm(lo,ones,NN)
+def headsums(ones, *xs):
+    hi = [x.astype(BF) for x in xs]
+    lo = [(x - h.astype(F32)).astype(BF) for x, h in zip(xs, hi)]
+    s = mm(jnp.concatenate(hi + lo, axis=0), ones, NN)
+    n = len(xs) * BLK
+    return [s[i * BLK : (i + 1) * BLK] + s[n + i * BLK : n + (i + 1) * BLK] for i in range(len(xs))]
 
 def decayed(geo,ws,tri):
     w=ws.astype(F32)
     cum=mm(tri,ws,NN)
     return w,cum,jnp.exp(cum-w),jnp.exp(cum),jnp.exp(-cum)
 
-def first_kernel(rp,kp,vp,uw,ua,uv,fl,vec,meta,segrow,tri,ones,rs,ws,ks,vs,qs,as_,ab):
+def first_block(rp,kp,vp,uw,ua,uv,fl,vec,meta,segrow,tri,ones,rs,ws,ks,vs,qs,as_,ri_out,ab):
     C=rp.shape[1]; gc=min(C,256); geo=Geo(gc)
     same=meta[:,0:1]==segrow[0]
     strict=geo.below&same
@@ -54,7 +59,9 @@
         vm=jax.nn.sigmoid(V(2)+uv[:,sl])
         v=v0+(fl[:,sl].astype(F32)-v0)*vm
         kn=k0*V(3)
-        kk=kn*lax.rsqrt(headsum(kn*kn,ones[...])+1e-6)
+        ri=lax.rsqrt(headsums(ones[...],kn*kn)[0]+1e-6)
+        ri_out[:,sl]=ri
+        kk=kn*ri
         km=k0*(1.0+(al-1.0)*V(4))
         q_=kk.astype(BF); w_=lw.astype(BF); a_=al.astype(BF)
         rs[:,sl]=rp[:,sl].astype(BF); ws[:,sl]=w_; ks[:,sl]=km.astype(BF)
@@ -62,27 +69,55 @@
         w,cum,eP,eC,eN=decayed(geo,w_,tri[...])
         q=q_.astype(F32)
         qu=(q*eP).astype(BF); bb=(q*a_.astype(F32)*eN).astype(BF)
-        ab[:,sl]=jnp.where(strict,mm(qu,geo.blk(bb),NT),0.0)
-
-def solve_kernel(a,t):
-    n=a.shape[0]
-    t[...]=jnp.zeros_like(t)
-    cidx=lax.broadcasted_iota(jnp.int32,t.shape[1:],0)
-    def outer(i,_):
-        def inner(jb,acc):
+        put128(ab,g,jnp.where(strict,mm(qu,geo.blk(bb),NT),0.0))
+
+def put128(ref, g, x):
+    if x.shape[1] < 128:
+        x = jnp.concatenate([x, jnp.zeros_like(x)], axis=1)
+    n = x.shape[1] // 128
+    for k in range(n):
+        ref[g * n + k] = x[:, k * 128 : (k + 1) * 128]
+
+
+def get128(ref, g, gc):
+    n = max(gc // 128, 1)
+    x = jnp.concatenate([ref[g * n + k] for k in range(n)], axis=1) if n > 1 else ref[g]
+    return x[:, :gc].astype(BF)
+
+
+def solve_kernel(ab, tt, a, t):
+    G, L, _ = ab.shape
+    NB = L // BLK
+    B = NB * G * 2
+
+    @pl.loop(0, BLK, unroll=8)
+    def _(i):
+        rows = [ab[g, pl.ds(i, NB, stride=BLK), :] for g in range(G)]
+        a[i] = jnp.concatenate([r[:, k * SD : (k + 1) * SD] for r in rows for k in range(2)], axis=0).T
+
+    t[...] = jnp.zeros_like(t)
+    cidx = lax.broadcasted_iota(jnp.int32, (SD, B), 0)
+
+    @pl.loop(0, BLK)
+    def _(i):
+        def inner(jb, acc):
             for jj in range(8):
-                j=jb*8+jj
-                acc=acc-a[i,pl.ds(j,1),:]*t[j]
+                j = jb * 8 + jj
+                acc = acc - a[i, pl.ds(j, 1), :] * t[j]
             return acc
-        acc=lax.fori_loop(0,i//8+1,inner,(cidx==i).astype(F32))
-        t[i]=acc
-        return 0
-    lax.fori_loop(0,n,outer,0)
-
-def forward_kernel(rs,ws,ks,vs,qs,as_,tt,vec,meta,segrow,tri,ones,y,o_out,u_out,s_out,state):
+
+        t[i] = lax.fori_loop(0, i // 8 + 1, inner, (cidx == i).astype(F32))
+
+    @pl.loop(0, BLK, unroll=8)
+    def _(i):
+        rows = t[i].T
+        for g in range(G):
+            pair = [rows[(2 * g + k) * NB : (2 * g + k + 1) * NB] for k in range(2)]
+            tt[g, pl.ds(i, NB, stride=BLK), :] = jnp.concatenate(pair, axis=1)
+
+
+def forward_block(rs,ws,ks,vs,qs,as_,tt,vec,meta,segrow,tri,ones,y,nrm_out,rstd_out,extra_out,u_out,al_out,lb_out,s_out,state):
     C=rs.shape[1]; gc=min(C,256); geo=Geo(gc)
-    @pl.when(pl.program_id(0)==0)
-    def _(): state[...]=jnp.zeros_like(state)
     same=meta[:,0:1]==segrow[0]
     carried=meta[:,1:2]; live=meta[:,2:3]; last=meta[BLK-1:BLK,1:2]
     strict=geo.below&same; incl=geo.upto&same
@@ -102,7 +137,7 @@
         qst=mm(qq,sb,NT)
         av=mm(al,geo.blk(vb),NN)
         rhs=carried*qst[:BLK]+av[:BLK]
-        u=mm(tt[:,sl],geo.blk(rhs.astype(BF)),NN)
+        u=mm(get128(tt,g,gc),geo.blk(rhs.astype(BF)),NN)
         ub=u.astype(BF)
         u_out[:,sl]=ub
         o=carried*qst[BLK:]+av[BLK:]-mm(lb,geo.blk(ub),NN)
@@ -110,20 +145,17 @@
         ds=mm(vu,jnp.concatenate([kb,bb],axis=0),TN)
         tail=eC[BLK-1:BLK]
         state[g]=(last*s0+ds*ones[...].astype(F32))*tail
-        o_out[:,sl]=o
-        mean=headsum(o,ones[...])*(1.0/SD)
-        cen=o-mean
-        var=headsum(cen*cen,ones[...])*(1.0/SD)
-        extra=headsum(r*k*V(5),ones[...])
-        y[:,sl]=(cen*lax.rsqrt(var+1.0)*V(6)+V(7)+extra*v).astype(BF)
-
-def backward_kernel(dy,o_in,rs,ws,ks,vs,qs,as_,tt,u_in,s_in,rp,kp,vp,uw,ua,uv,fl,vec,meta,segrow,tri,tru,ones,
+        al_out[:,sl]=al; lb_out[:,sl]=lb
+        mean,extra=headsums(ones[...],o,r*k*V(5))
+        cen=o-mean*(1.0/SD)
+        rstd=lax.rsqrt(headsums(ones[...],cen*cen)[0]*(1.0/SD)+1.0)
+        nrm=cen*rstd
+        nrm_out[:,sl]=nrm; rstd_out[:,sl]=rstd; extra_out[:,sl]=extra
+        y[:,sl]=(nrm*V(6)+V(7)+extra*v).astype(BF)
+
+def backward_block(dy,nrm_in,rstd_in,extra_in,rs,ws,ks,vs,qs,as_,tt,u_in,al_in,lb_in,s_in,ri_in,rp,kp,vp,uw,ua,uv,fl,vec,meta,segrow,tri,tru,ones,
                     drp,dkp,dvp,duw,dua,duv,dfl,dvec,state):
     C=rs.shape[1]; gc=min(C,256); geo=Geo(gc)
-    @pl.when(pl.program_id(0)==0)
-    def _():
-        state[...]=jnp.zeros_like(state)
-        dvec[...]=jnp.zeros_like(dvec)
     same=meta[:,0:1]==segrow[0]
     carried=meta[:,1:2]; live=meta[:,2:3]; last=meta[BLK-1:BLK,1:2]
     strict=geo.below&same; incl=geo.upto&same
@@ -136,29 +168,23 @@
         w,cum,eP,eC,eN=decayed(geo,ws[:,sl],tri[...])
         q=qs[:,sl].astype(F32); r=rs[:,sl].astype(F32); k=ks[:,sl].astype(F32)
         vb=vs[:,sl]; v=vb.astype(F32); a=as_[:,sl].astype(F32)
-        d=dy[:,sl].astype(F32); o=o_in[:,sl]
-        mean=headsum(o,on)*(1.0/SD); cen=o-mean
-        rstd=lax.rsqrt(headsum(cen*cen,on)*(1.0/SD)+1.0)
-        nrm=cen*rstd
-        extra=headsum(r*k*V(5),on)
-        de=headsum(d*v,on)
+        d=dy[:,sl].astype(F32); nrm=nrm_in[:,sl]; extra=extra_in[:,sl]
         dn=d*V(6)
-        do=rstd*(dn-headsum(dn,on)*(1.0/SD)-nrm*(headsum(dn*nrm,on)*(1.0/SD)))
+        de,dn1,dn2=headsums(on,d*v,dn,dn*nrm)
+        do=rstd_in[:,sl]*(dn-dn1*(1.0/SD)-nrm*(dn2*(1.0/SD)))
         g17=rsum(d); g16=rsum(d*nrm); g15=rsum(de*r*k)
         dr=de*k*V(5); dk=de*r*V(5); dv=d*extra
         qq=cat((q*eP).astype(BF),(r*eC).astype(BF))
         kb=(k*eN).astype(BF); bb=(q*a*eN).astype(BF)
         kblk=geo.blk(kb); bblk=geo.blk(bb)
-        mk=mm(qq,kblk,NT)
-        al=cat(jnp.where(strict,mk[:BLK],0.0).astype(BF),jnp.where(incl,mk[BLK:],0.0).astype(BF))
-        lb=jnp.where(incl,mm(qq[BLK:],bblk,NT),0.0).astype(BF)
+        al=al_in[:,sl]; lb=lb_in[:,sl]
         ub=u_in[:,sl]; s0=s_in[0,g]
         tail=eC[BLK-1:BLK]
         ds1=state[g]*tail; dsb=ds1.astype(BF)
         kbs=mm(cat(kb,bb),dsb,NT)
         dob=do.astype(BF)
         du=-geo.ext(mm(lb,dob,TN))-live*kbs[BLK:]
-        yy=geo.ext(mm(tt[:,sl],du.astype(BF),TN))
+        yy=geo.ext(mm(get128(tt,g,gc),du.astype(BF),TN))
         yo=cat(yy.astype(BF),dob)
         cyo=cat((carried*yy).astype(BF),(carried*do).astype(BF))
         mv=mm(yo,geo.blk(vb),NT); mu=mm(yo,geo.blk(ub),NT)
@@ -186,13 +212,13 @@
         k0=kp[:,sl]; v0=vp[:,sl]
         sg=jax.nn.sigmoid(V(0)+uw[:,sl]); af=jax.nn.sigmoid(V(1)+ua[:,sl]); vm=jax.nn.sigmoid(V(2)+uv[:,sl])
         kn=k0*V(3)
-        ri=lax.rsqrt(headsum(kn*kn,on)+1e-6)
+        ri=ri_in[:,sl]
         kk=kn*ri
         gw=(-0.606531)*dw*sg*(1.0-sg)
         gv=dv*(fl[:,sl].astype(F32)-v0)*vm*(1.0-vm)
         da=da+dk*k0*V(4)
         ga=da*af*(1.0-af)
-        dkn=ri*(dq-kk*headsum(dq*kk,on))
+        dkn=ri*(dq-kk*headsums(on,dq*kk)[0])
         drp[:,sl]=dr.astype(BF)
         dkp[:,sl]=(dk*(1.0+(af-1.0)*V(4))+dkn*V(3)).astype(BF)
         dvp[:,sl]=(dv*(1.0-vm)).astype(BF)
@@ -200,6 +226,24 @@
         dfl[:,sl]=(dv*vm).astype(BF)
         dvec[:,sl]+=cat(rsum(gw),rsum(ga),rsum(gv),rsum(dkn*k0),rsum(dk*k0*(af-1.0)),g15,g16,g17)
 
+def per_block(ref, kind, i):
+    if kind is None:
+        return ref
+    size = {"n": 1, "pair": 2 * BLK}.get(kind, BLK)
+    at = pl.ds(i * size, size)
+    return ref.at[:, at] if kind == "inv" else ref.at[at]
+
+
+def blocks_kernel(body, kinds, order, zeroed, *refs):
+    @pl.when(pl.program_id(0) == 0)
+    def _():
+        for i in zeroed:
+            refs[i][...] = jnp.zeros_like(refs[i])
+
+    for i in order:
+        body(*(per_block(r, k, i) for r, k in zip(refs, kinds)))
+
+
 def consts(C):
     gc=min(C,256)
     i=jnp.arange(BLK); tri=(i[:,None]>=i[None,:]).astype(BF); tru=(i[:,None]<=i[None,:]).astype(BF)
@@ -207,39 +251,78 @@
     return tri,tru,ones
 
 VM=60*2**20
+def takes(us): return pl.CostEstimate(flops=int(us*6e8), bytes_accessed=1<<20, transcendentals=0)
+UNROLL=2
 def params(): return pltpu.CompilerParams(vmem_limit_bytes=VM)
 
-def recurrence_forward(ins,vec,meta,segrow):
-    L,C=ins[0].shape; NB=L//BLK; gc=min(C,256); G=C//gc; H=C//SD
-    tri,tru,ones=consts(C)
-    rowb=pl.BlockSpec((BLK,C),lambda i:(i,0)); fix=lambda s: pl.BlockSpec(s,lambda i:(0,)*len(s))
-    metab=pl.BlockSpec((BLK,meta.shape[1]),lambda i:(i,0)); segb=pl.BlockSpec((1,1,gc),lambda i:(i,0,0))
-    sd=lambda dt: jax.ShapeDtypeStruct((L,C),dt)
-    *six,ab=pl.pallas_call(first_kernel,grid=(NB,),
-        in_specs=[rowb]*7+[fix((8,C)),metab,segb,fix((BLK,BLK)),fix((gc,gc))],
-        out_specs=[rowb]*7,out_shape=[sd(BF)]*6+[sd(F32)],compiler_params=params())(*ins,vec,meta,segrow,tri,ones)
-    at=ab.reshape(NB,BLK,H,SD).transpose(1,3,0,2).reshape(BLK,SD,NB*H)
-    t=pl.pallas_call(solve_kernel,out_shape=jax.ShapeDtypeStruct(at.shape,F32),compiler_params=params())(at)
-    tt=t.astype(BF).reshape(BLK,SD,NB,H).transpose(2,0,3,1).reshape(L,C)
-    y,o,u,s=pl.pallas_call(forward_kernel,grid=(NB,),
-        in_specs=[rowb]*7+[fix((8,C)),metab,segb,fix((BLK,BLK)),fix((gc,gc))],
-        out_specs=[rowb]*3+[pl.BlockSpec((1,G,gc,gc),lambda i:(i,0,0,0))],
-        out_shape=[sd(BF),sd(F32),sd(BF),jax.ShapeDtypeStruct((NB,G,gc,gc),BF)],
-        scratch_shapes=[pltpu.VMEM((G,gc,gc),F32)],compiler_params=params())(*six,tt,vec,meta,segrow,tri,ones)
-    return y,(o,*six,tt,u,s)
-
-def recurrence_backward(dy,saved,ins,vec,meta,segrow):
-    L,C=ins[0].shape; NB=L//BLK; gc=min(C,256); G=C//gc
-    tri,tru,ones=consts(C)
-    rev=lambda i: NB-1-i
-    rowb=pl.BlockSpec((BLK,C),lambda i:(rev(i),0)); fix=lambda s: pl.BlockSpec(s,lambda i:(0,)*len(s))
-    metab=pl.BlockSpec((BLK,meta.shape[1]),lambda i:(rev(i),0)); segb=pl.BlockSpec((1,1,gc),lambda i:(rev(i),0,0))
-    sb=pl.BlockSpec((1,G,gc,gc),lambda i:(rev(i),0,0,0))
-    return pl.pallas_call(backward_kernel,grid=(NB,),
-        in_specs=[rowb]*10+[sb]+[rowb]*7+[fix((8,C)),metab,segb,fix((BLK,BLK)),fix((BLK,BLK)),fix((gc,gc))],
-        out_specs=[rowb]*7+[fix((8,C))],
-        out_shape=[jax.ShapeDtypeStruct((L,C),BF)]*7+[jax.ShapeDtypeStruct((8,C),F32)],
-        scratch_shapes=[pltpu.VMEM((G,gc,gc),F32)],compiler_params=params())(dy,*saved,*ins,vec,meta,segrow,tri,tru,ones)
+def recurrence_forward(ins, vec, meta, segrow):
+    L, C = ins[0].shape
+    NB, gc = L // BLK, min(C, 256)
+    G = C // gc
+    tri, tru, ones = consts(C)
+    inv = jax.ShapeDtypeStruct((-(-C // 128), L, 128), F32)
+    n = UNROLL
+    rowb = pl.BlockSpec((n * BLK, C), lambda i: (i, 0))
+    fix = lambda s: pl.BlockSpec(s, lambda i: (0,) * len(s))
+    metab = pl.BlockSpec((n * BLK, meta.shape[1]), lambda i: (i, 0))
+    segb = pl.BlockSpec((n, 1, gc), lambda i: (i, 0, 0))
+    invb = pl.BlockSpec((inv.shape[0], n * BLK, 128), lambda i: (0, i, 0))
+    sd = lambda dt: jax.ShapeDtypeStruct((L, C), dt)
+    tail = [fix((8, C)), metab, segb, fix((BLK, BLK)), fix((gc, gc))]
+    tail_kinds = [None, "row", "n", None, None]
+    *six, ri, ab = pl.pallas_call(
+        functools.partial(blocks_kernel, first_block, ["row"] * 7 + tail_kinds + ["row"] * 7 + ["inv"], range(n), ()),
+        grid=(NB // n,),
+        in_specs=[rowb] * 7 + tail,
+        out_specs=[rowb] * 7 + [invb],
+        out_shape=[sd(BF)] * 6 + [sd(F32), inv],
+        compiler_params=params(),
+    )(*ins, vec, meta, segrow, tri, ones)
+    lanes = inv.shape[0] * 2 * NB
+    tt = pl.pallas_call(
+        solve_kernel, out_shape=inv, scratch_shapes=[pltpu.VMEM((BLK, SD, lanes), F32)] * 2, compiler_params=params()
+    )(ab)
+    kinds = ["row"] * 6 + ["inv"] + tail_kinds + ["row"] * 5 + ["pair", "row", "n", None]
+    pairb = pl.BlockSpec((2 * n * BLK, C), lambda i: (i, 0))
+    y, nrm, rstd, extra, u, al, lb, s = pl.pallas_call(
+        functools.partial(blocks_kernel, forward_block, kinds, range(n), (len(kinds) - 1,)),
+        grid=(NB // n,),
+        in_specs=[rowb] * 6 + [invb] + tail,
+        out_specs=[rowb] * 5 + [pairb, rowb, pl.BlockSpec((n, G, gc, gc), lambda i: (i, 0, 0, 0))],
+        out_shape=[sd(BF)] + [sd(F32)] * 3 + [sd(BF), jax.ShapeDtypeStruct((2 * L, C), BF), sd(BF), jax.ShapeDtypeStruct((NB, G, gc, gc), BF)],
+        scratch_shapes=[pltpu.VMEM((G, gc, gc), F32)],
+        compiler_params=params(),
+    )(*six, tt, vec, meta, segrow, tri, ones)
+    return y, (nrm, rstd, extra, *six, tt, u, al, lb, s, ri)
+
+
+def recurrence_backward(dy, saved, ins, vec, meta, segrow):
+    L, C = ins[0].shape
+    NB, gc = L // BLK, min(C, 256)
+    G = C // gc
+    tri, tru, ones = consts(C)
+    n = UNROLL
+    rev = lambda i: NB // n - 1 - i
+    rowb = pl.BlockSpec((n * BLK, C), lambda i: (rev(i), 0))
+    fix = lambda s: pl.BlockSpec(s, lambda i: (0,) * len(s))
+    metab = pl.BlockSpec((n * BLK, meta.shape[1]), lambda i: (rev(i), 0))
+    segb = pl.BlockSpec((n, 1, gc), lambda i: (rev(i), 0, 0))
+    sb = pl.BlockSpec((n, G, gc, gc), lambda i: (rev(i), 0, 0, 0))
+    invb = pl.BlockSpec((-(-C // 128), n * BLK, 128), lambda i: (0, rev(i), 0))
+    kinds = ["row"] * 10 + ["inv", "row", "pair", "row", "n"] + ["row"] * 8 + [None, "row", "n", None, None, None] + ["row"] * 7 + [None] * 2
+    last = len(kinds) - 1
+    return pl.pallas_call(
+        functools.partial(blocks_kernel, backward_block, kinds, range(n - 1, -1, -1), (last - 1, last)),
+        grid=(NB // n,),
+        in_specs=[rowb] * 10
+        + [invb, rowb, pl.BlockSpec((2 * n * BLK, C), lambda i: (rev(i), 0)), rowb, sb]
+        + [rowb] * 8
+        + [fix((8, C)), metab, segb, fix((BLK, BLK)), fix((BLK, BLK)), fix((gc, gc))],
+        out_specs=[rowb] * 7 + [fix((8, C))],
+        out_shape=[jax.ShapeDtypeStruct((L, C), BF)] * 7 + [jax.ShapeDtypeStruct((8, C), F32)],
+        scratch_shapes=[pltpu.VMEM((G, gc, gc), F32)],
+        compiler_params=params(),
+    )(dy, *saved, *ins, vec, meta, segrow, tri, tru, ones)
 
 
 def mix_tile(x, vec, first_row, keep):
@@ -353,22 +436,24 @@
 
 def weight_grads(xm, grads, dd, mid, z, dt):
     L, D = xm[0].shape
-    C, wide = z.shape[1], mid.shape[1]
+    C, wide = grads[0].shape[1], mid.shape[1]
     n = 256 if L <= 1024 else 128
+    tok, own = z.shape
     feat = pl.BlockSpec((L, n), lambda i: (0, i))
     fix = lambda m: pl.BlockSpec((L, m), lambda i: (0, 0))
     sd = jax.ShapeDtypeStruct
     return pl.pallas_call(
         weight_kernel,
         grid=(D // n,),
-        in_specs=[feat] * 6 + [fix(C)] * 3 + [fix(wide)] + [fix(C)] * 4 + [fix(wide), fix(C), feat],
+        in_specs=[feat] * 6 + [fix(C)] * 3 + [fix(wide)] + [fix(C)] * 4 + [fix(wide), pl.BlockSpec((tok, own), lambda i: (0, 0)), pl.BlockSpec((tok, n), lambda i: (0, i))],
         out_specs=[
             pl.BlockSpec((3, n, C), lambda i: (0, i, 0)),
             pl.BlockSpec((n, wide), lambda i: (i, 0)),
             pl.BlockSpec((C, wide), lambda i: (0, 0)),
-            pl.BlockSpec((C, n), lambda i: (0, i)),
+            pl.BlockSpec((own, n), lambda i: (0, i)),
         ],
-        out_shape=[sd((3, D, C), BF), sd((D, wide), BF), sd((C, wide), BF), sd((C, D), BF)],
+        out_shape=[sd((3, D, C), BF), sd((D, wide), BF), sd((C, wide), BF), sd((own, D), BF)],
+        cost_estimate=takes(26),
         compiler_params=params(),
     )(*xm, *grads[:3], dd, *grads[3:], mid, z, dt)
 
@@ -379,17 +464,18 @@
 def mix_forward(x, meta, vec, sq, low, up):
     L, D = x.shape
     C = up.shape[0]
-    wide = low.shape[1]
+    wide = up.shape[1]
     tok = lambda n: pl.BlockSpec((TILE, n), lambda i: (i, 0))
     fix = lambda s: pl.BlockSpec(s, lambda i: (0,) * len(s))
     sd = jax.ShapeDtypeStruct
     out = pl.pallas_call(
         mix_forward_kernel,
         grid=(L // TILE,),
-        in_specs=[tok(D), tok(meta.shape[1]), fix(vec.shape), fix(sq.shape), fix(low.shape), fix(up.shape)],
+        in_specs=[tok(D), tok(meta.shape[1]), fix(vec.shape), fix(sq.shape), fix((D, wide)), fix(up.shape)],
         out_specs=[tok(D)] * 6 + [tok(C)] * 7 + [tok(wide)] * 2,
         out_shape=[sd((L, D), BF)] * 6 + [sd((L, C), F32)] * 7 + [sd((L, wide), F32), sd((L, wide), BF)],
         scratch_shapes=[pltpu.VMEM((8, D), F32)],
+        cost_estimate=takes(30),
         compiler_params=params(),
     )(x, meta, vec, sq, low, up)
     return out[:6], out[6:13], out[13], out[14]
@@ -398,7 +484,7 @@
 def mix_backward(grads, x, meta, mid, vec, sq, low, up):
     L, D = x.shape
     C = up.shape[0]
-    wide = low.shape[1]
+    wide = up.shape[1]
     n = L // TILE
     rev = lambda i: n - 1 - i
     tok = lambda m: pl.BlockSpec((TILE, m), lambda i: (rev(i), 0))
@@ -409,10 +495,11 @@
         mix_backward_kernel,
         grid=(n,),
         in_specs=[tok(C)] * 7
-        + [tok(D), above, tok(meta.shape[1]), tok(wide), fix(vec.shape), fix(sq.shape), fix(low.shape), fix(up.shape)],
+        + [tok(D), above, tok(meta.shape[1]), tok(wide), fix(vec.shape), fix(sq.shape), fix((D, wide)), fix(up.shape)],
         out_specs=[tok(D), tok(wide), fix((8, D))],
         out_shape=[sd((L, D), BF), sd((L, wide), BF), sd((8, D), F32)],
         scratch_shapes=[pltpu.VMEM((8, D), F32), pltpu.VMEM((TILE, D), F32)],
+        cost_estimate=takes(35),
         compiler_params=params(),
     )(*grads, x, x, meta, mid, vec, sq, low, up)
 
@@ -484,51 +571,104 @@
     return [(d, 0, 0, 0) for d in range(1, lax.axis_size("sa"))]
 
 
-def seq_shifts():
-    A, B = lax.axis_size("sa"), lax.axis_size("sb")
-    return [(i // B, i % B, 0, 0) for i in range(1, A * B)]
-
-
 CHIPS = [(0, 1, 0, 0), (0, 0, 1, 0), (0, 1, 1, 0)]
 OTHER_CORE = (0, 0, 0, 1)
 
 
-def plane_gather_first(net, src, view):
-    slot = net.me[1:]
-    net.keep(src, view(*slot))
-    far = [net.send(src, view(*slot), s) for s in CHIPS]
-    return far, [net.send(src, view(*slot), OTHER_CORE)]
-
-
-def plane_gather_second(net, view, far, near):
-    for s, copy in zip(CHIPS, far):
-        copy.wait_recv()
-        slot = net.at(s)[1:]
-        near.append(net.send(view(*slot), view(*slot), OTHER_CORE))
-
-
-def plane_gather_end(far, near):
-    for copy in far:
-        copy.wait_send()
-    for copy in near:
-        copy.wait()
-
-
-def line_exchange(arrays, cid):
+class Gather:
+    def __init__(self, net, src, view, half=None):
+        self.net, self.src, self.view, self.half = net, src, view, half
+
+    def slot(self, shift):
+        return self.net.at(shift)[1:]
+
+    def hand(self, view, shift):
+        copy = self.net.send(view, view, shift)
+        self.out.append(copy)
+        return copy
+
+    def first(self):
+        net = self.net
+        here = self.view(*net.me[1:])
+        net.keep(self.src, here)
+        self.near = [net.send(self.src, here, s) for s in CHIPS[:2]]
+        self.far = [] if self.half else [net.send(self.src, here, CHIPS[2])]
+        self.out = self.near + self.far
+        self.core = [net.send(self.src, here, OTHER_CORE)]
+
+    def to_core(self, shift):
+        view = self.view(*self.slot(shift))
+        self.core.append(self.net.send(view, view, OTHER_CORE))
+
+    def second(self):
+        for h, copy in enumerate(self.near):
+            copy.wait_recv()
+            if self.half:
+                self.far.append(self.hand(self.half(*self.slot(CHIPS[h]), h), CHIPS[1 - h]))
+            self.to_core(CHIPS[h])
+
+    def third(self):
+        for copy in self.far:
+            copy.wait_recv()
+        self.to_core(CHIPS[2])
+
+    def end(self):
+        for copy in self.out:
+            copy.wait_send()
+        for copy in self.core:
+            copy.wait()
+
+
+def gather_body(net, gathers):
+    for step in ("second", "third", "end"):
+        for g in gathers:
+            getattr(g, step)()
+
+
+def line_exchange(arrays, gathers, cid, shares=()):
+    m = len(arrays)
+    n = m + len(gathers)
+
     def body(ins, outs, _, net):
         shifts = line_shifts()
-        net.greet(shifts)
+        net.greet(shifts + (plane_shifts() if shares else CHIPS[:2] + [OTHER_CORE] if gathers else []))
         a = net.me[0]
         open_ = []
-        for x, o in zip(ins, outs):
+        for x, o in zip(ins[:m], outs):
             open_ += [net.send(x.at[net.at(s)[0]], o.at[a], s) for s in shifts]
             net.keep(x.at[a], o.at[a])
+        planes = [
+            Gather(net, x, functools.partial(g[2], o), functools.partial(g[3], o))
+            for x, o, g in zip(ins[m:], outs[m:], gathers)
+        ]
+        for g in planes:
+            g.first()
+        mine = net.me[1:]
+        for x, o in zip(ins[n:], outs[n:]):
+            open_ += [net.send(x.at[net.at(s)[1:]], o.at[mine], s) for s in plane_shifts()]
+            net.keep(x.at[mine], o.at[mine])
+        gather_body(net, planes)
         for copy in open_:
             copy.wait()
         net.settle()
 
-    shapes = [jax.ShapeDtypeStruct(x.shape, x.dtype) for x in arrays]
-    return call_net(body, arrays, shapes, cid, len(arrays), (lax.axis_size("sa") - 1) * len(arrays))
+    sd = jax.ShapeDtypeStruct
+    shapes = [sd(x.shape, x.dtype) for x in arrays] + [sd(g[1], g[0].dtype) for g in gathers]
+    shapes += [sd(x.shape, x.dtype) for x in shares]
+    n_send = (lax.axis_size("sa") - 1) * m + 8 * len(gathers) + 7 * len(shares)
+    operands = [*arrays, *(g[0] for g in gathers), *shares]
+    return call_net(body, operands, shapes, cid, len(operands), n_send)
+
+
+def rows_gather(x):
+    sizes = tuple(lax.axis_size(k) for k in PLANE)
+    half = x.shape[0] // 2
+    return (
+        x,
+        sizes + x.shape,
+        lambda o, b, y, c: o.at[b, y, c],
+        lambda o, b, y, c, h: o.at[b, y, c, pl.ds(h * half, half)],
+    )
 
 
 def swap_first(net, x, o):
@@ -537,71 +677,113 @@
     return [net.send(x.at[net.at(CHIPS[0])[1]], o.at[b], CHIPS[0])]
 
 
-def plane_gather(x, cid):
-    def body(ins, outs, _, net):
-        (x,), (o,) = ins, outs
-        view = lambda i, j, k: o.at[i, j, k]
-        net.greet(CHIPS + [OTHER_CORE])
-        far, near = plane_gather_first(net, x, view)
-        plane_gather_second(net, view, far, near)
-        plane_gather_end(far, near)
-        net.settle()
-
-    sizes = tuple(lax.axis_size(k) for k in PLANE)
-    return call_net(body, [x], [jax.ShapeDtypeStruct(sizes + x.shape, x.dtype)], cid, 1, 7)[0]
-
-
 def plane_shifts():
     return [(0, i // 4, i // 2 % 2, i % 2) for i in range(1, 8)]
 
 
-def start_exchange(tokens, first_sliced, out_grad, sq, low, up, key, cid):
+def start_exchange(tokens, sq, low, up, key, cid):
     A, B = lax.axis_size("sa"), lax.axis_size("sb")
-    S = A * B
+    S, hops = A * B, A - 1
     sizes = tuple(lax.axis_size(k) for k in PLANE)
+    n_fixed = 2 * hops + 8 + 8 + 7 + 7 + 1
 
     def body(ins, outs, scratch, net):
-        x, f, g, q, lo, u, ke = ins
-        xo, fo, go, qo, loo, uo, ko, q_line, lo_line = outs
-        q_view = lambda i, j, k: qo.at[:, :, i, j, k]
-        lo_view = lambda i, j, k: loo.at[:, i, j, k]
-        u_view = lambda i, j, k: uo.at[i, j, k]
-        g_view = lambda i, j, k: go.at[i, j, k]
-        line, seq = line_shifts(), seq_shifts()
-        net.greet(seq + [s for s in plane_shifts() if s != CHIPS[0]])
-        a, b = net.me[:2]
+        x, q, lo, u, ke = ins
+        xo, qo, loo, uo, ko, q_line, lo_line = outs
+        line = line_shifts()
+        net.greet(line + plane_shifts())
+        a, b, y, c = net.me
         me = a * B + b
+        ssem, rsem = net.sems[1:]
+
+        def block(i, k):
+            return xo.at[i * B + (b if k == 0 else 1 - b)]
+
+        def index(way, t, k):
+            return n_fixed + (way * hops + t) * 2 + k
+
+        def origin(way, t):
+            return a - t if way == 0 else a + t
+
+        def have(way, t):
+            return a >= t if way == 0 else a <= A - 1 - t
+
+        def can(way):
+            return a < A - 1 if way == 0 else a > 0
+
+        def relay(way, t, k):
+            dst = block(origin(way, t), k)
+            i = index(way, t, k)
+            to = (a + 1 if way == 0 else a - 1, b, y, c)
+            src = x.at[b] if t == 0 and k == 0 else dst
+            return pltpu.make_async_remote_copy(src, dst, ssem.at[i], rsem.at[i], device_id=to, device_id_type=MESH)
+
+        def relay_start(t, k):
+            for way in range(2):
+
+                @pl.when(have(way, t) & can(way))
+                def _(way=way):
+                    relay(way, t, k).start()
+
+        def relay_arrived(t, k):
+            for way in range(2):
+
+                @pl.when(have(way, t))
+                def _(way=way):
+                    dst, i = block(origin(way, t), k), index(way, t - 1, k)
+                    pltpu.make_async_remote_copy(
+                        dst, dst, ssem.at[i], rsem.at[i], device_id=net.at(OTHER_CORE), device_id_type=MESH
+                    ).wait_recv()
+
         first = []
         for s in line:
             first.append(net.send(q.at[net.at(s)[0]], q_line.at[:, a], s))
             first.append(net.send(lo, lo_line.at[a], s))
+        relay_start(0, 0)
+        across = net.send(x.at[1 - b], xo.at[me], CHIPS[0])
         net.keep(q.at[a], q_line.at[:, a])
         net.keep(lo, lo_line.at[a])
-        rest = []
-        for s in seq:
-            rest.append(net.send(x.at[net.at(s)[1]], xo.at[me], s))
-        for s in seq:
-            to = net.at(s)
-            rest.append(net.send(f.at[to[1], to[0]], fo.at[me], s))
+        planes = [Gather(net, u, lambda i, j, k: uo.at[i, j, k])]
+        planes[0].first()
+        across.wait_recv()
+        relay_start(0, 1)
         for copy in first:
             copy.wait()
         net.settle()
         net.locals = []
         net.keep(x.at[b], xo.at[me])
-        net.keep(f.at[b, a], fo.at[me])
-        q_open = plane_gather_first(net, q_line, q_view)
-        lo_open = plane_gather_first(net, lo_line, lo_view)
-        u_open = plane_gather_first(net, u, u_view)
-        g_open = plane_gather_first(net, g, g_view)
-        slot = net.me[1:]
-        rest += [net.send(ke.at[net.at(s)[1:]], ko.at[slot], s) for s in plane_shifts()]
-        net.keep(ke.at[slot], ko.at[slot])
-        plane_gather_second(net, q_view, *q_open)
-        plane_gather_second(net, lo_view, *lo_open)
-        plane_gather_second(net, u_view, *u_open)
-        plane_gather_second(net, g_view, *g_open)
-        for o in (u_open, q_open, lo_open, g_open):
-            plane_gather_end(*o)
+        h = A // 2
+        planes.append(
+            Gather(net, q_line, lambda i, j, k: qo.at[:, :, i, j, k], lambda i, j, k, p: qo.at[:, pl.ds(p * h, h), i, j, k])
+        )
+        planes.append(Gather(net, lo_line, lambda i, j, k: loo.at[:, i, j, k], lambda i, j, k, p: loo.at[pl.ds(p * h, h), i, j, k]))
+        planes[1].first()
+        planes[2].first()
+        mine = net.me[1:]
+        rest = [net.send(ke.at[net.at(s)[1:]], ko.at[mine], s) for s in plane_shifts()]
+        net.keep(ke.at[mine], ko.at[mine])
+        for t in range(1, hops):
+            for k in range(2):
+                relay_arrived(t, k)
+                relay_start(t, k)
+            if t == 1:
+                for g in planes:
+                    g.second()
+        for g in planes:
+            g.third()
+        for k in range(2):
+            relay_arrived(hops, k)
+        for t in range(hops):
+            for k in range(2):
+                for way in range(2):
+
+                    @pl.when(have(way, t) & can(way))
+                    def _(way=way, t=t, k=k):
+                        relay(way, t, k).wait_send()
+
+        across.wait_send()
+        for g in planes:
+            g.end()
         for copy in rest:
             copy.wait()
         net.settle()
@@ -609,8 +791,6 @@
     sd = lambda shape, like: jax.ShapeDtypeStruct(shape, like.dtype)
     shapes = [
         sd((S,) + tokens.shape[1:], tokens),
-        sd((S,) + first_sliced.shape[2:], first_sliced),
-        sd(sizes + out_grad.shape, out_grad),
         sd(sq.shape[1:2] + (A,) + sizes + sq.shape[2:], sq),
         sd((A,) + sizes + low.shape, low),
         sd(sizes + up.shape, up),
@@ -618,23 +798,21 @@
         sd(sq.shape[1:2] + (A,) + sq.shape[2:], sq),
         sd((A,) + low.shape, low),
     ]
-    n_send = 2 * (A - 1) + 2 * (S - 1) + 5 * 7
-    return call_net(body, [tokens, first_sliced, out_grad, sq, low, up, key], shapes, cid, 9, n_send)[:7]
-
-
-def tail_exchange(dh, dfl, sq, down, wide, up, sq3, narrow, ffn, cid):
-    A, B = lax.axis_size("sa"), lax.axis_size("sb")
-    leads = [2, 1, 1, 0, 0, 0, 0]
-    arrays = [sq, down, wide, up, sq3, narrow, ffn]
+    return call_net(body, [tokens, sq, low, up, key], shapes, cid, 9, n_fixed + 4 * hops)[:5]
+
+
+def tail_exchange(dh, sq3, sq, down, wide, up, narrow, ffn, cid):
+    A = lax.axis_size("sa")
+    leads = [2, 1, 1, 0, 0, 0]
+    arrays = [sq, down, wide, up, narrow, ffn]
     blocks = [x.shape[:n] + x.shape[n + 3 :] for x, n in zip(arrays, leads)]
     n = len(arrays)
 
     def body(ins, outs, scratch, net):
-        d, f, ps = ins[0], ins[1], ins[2:]
-        do, fo, pos = outs[0], outs[1], outs[2:]
+        ps, pos = ins[2:], outs[2:]
         own, other, chips = scratch[:n], scratch[n : 2 * n], scratch[2 * n :]
-        seq = seq_shifts()
-        net.greet(seq + CHIPS[1:] + [OTHER_CORE])
+        line = line_shifts()
+        net.greet(line + CHIPS + [OTHER_CORE])
         a, b, y, c = net.me
         there = net.at(OTHER_CORE)[3]
         pairs = [(i // 2, i % 2) for i in range(4)]
@@ -649,9 +827,10 @@
                 net.keep(block(t, i, j, c), own[t].at[2 * i + j])
             mine.append(net.locals)
             net.locals = []
-        open_ = [net.send(d.at[net.at(s)[0]], do.at[a], s) for s in line_shifts()]
-        net.keep(d.at[a], do.at[a])
-        net.keep(f.at[a * B + b], fo.at[b, a])
+        open_ = []
+        for x, o in zip(ins[:2], outs[:2]):
+            open_ += [net.send(x.at[net.at(s)[0]], o.at[a], s) for s in line]
+            net.keep(x.at[a], o.at[a])
 
         def add(t, k, terms):
             shape = blocks[t]
@@ -683,9 +862,6 @@
                 slot = 2 * to[1] + to[2]
                 add(t, slot, [(other[t], slot)])
                 sent.append(net.send(own[t].at[slot], chips[t].at[k], s))
-        for s in seq:
-            to = net.at(s)
-            open_.append(net.send(f.at[to[0] * B + to[1]], fo.at[b, a], s))
         me = 2 * b + y
         for t in range(n):
             for copy in sent[3 * t : 3 * t + 3]:
@@ -699,35 +875,40 @@
         net.settle()
 
     sd = jax.ShapeDtypeStruct
-    shapes = [sd(dh.shape, dh.dtype), sd((B, A) + dfl.shape[1:], dfl.dtype)] + [sd(s, BF) for s in blocks]
+    shapes = [sd(dh.shape, BF), sd(sq3.shape, BF)] + [sd(s, BF) for s in blocks]
     scratch = [pltpu.VMEM((m,) + s, BF) for m in (4, 4, 3) for s in blocks]
-    n_send = (A - 1) + (A * B - 1) + 7 * n
-    return call_net(body, [dh, dfl, *arrays], shapes, cid, 2 + 5 * n, n_send, scratch)
-
-
-def last_exchange(swaps, sq, lines, cid):
+    n_send = 2 * (A - 1) + 7 * n
+    return call_net(body, [dh, sq3, *arrays], shapes, cid, 2 + 5 * n, n_send, scratch)
+
+
+def last_exchange(swaps, sq, lines, key, cid):
     m = len(swaps)
+    n = m + 1 + len(lines)
 
     def body(ins, outs, _, net):
-        net.greet(line_shifts() + [CHIPS[0]])
+        line, plane = line_shifts(), plane_shifts()
+        net.greet(line + plane)
         a = net.me[0]
+        mine = net.me[1:]
         open_ = []
-        for i, (x, o) in enumerate(zip(ins, outs)):
+        for i, (x, o) in enumerate(zip(ins[:n], outs)):
             if i < m:
                 open_ += swap_first(net, x, o)
                 continue
             view = (lambda x, k: x.at[:, k]) if i == m else (lambda x, k: x.at[k])
-            open_ += [net.send(view(x, net.at(s)[0]), o.at[a], s) for s in line_shifts()]
+            open_ += [net.send(view(x, net.at(s)[0]), o.at[a], s) for s in line]
             net.keep(view(x, a), o.at[a])
+        open_ += [net.send(ins[n].at[net.at(s)[1:]], outs[n].at[mine], s) for s in plane]
+        net.keep(ins[n].at[mine], outs[n].at[mine])
         for copy in open_:
             copy.wait()
         net.settle()
 
     sd = jax.ShapeDtypeStruct
-    arrays = [*swaps, sq, *lines]
+    arrays = [*swaps, sq, *lines, key]
     shapes = [sd(x.shape, x.dtype) for x in arrays]
     shapes[m] = sd((sq.shape[1], sq.shape[0]) + sq.shape[2:], sq.dtype)
-    n_send = m + (1 + len(lines)) * (lax.axis_size("sa") - 1)
+    n_send = m + (1 + len(lines)) * (lax.axis_size("sa") - 1) + 7
     return call_net(body, arrays, shapes, cid, len(arrays), n_send)
 
 
@@ -778,7 +959,8 @@
     keep_own = lax.dynamic_slice(keep_row, (a * T, 0), (T, 1))
 
     sq3 = lax.all_gather(square[3], AXES, axis=0, tiled=True)
-    first_sliced = first_values.reshape(rows_here, seg, SA, C).transpose(0, 2, 1, 3)
+    first_sliced = first_values.reshape(rows_here, seg, SA, C).transpose(2, 0, 1, 3).reshape(S, seg, C)
+    first_row = lax.all_to_all(first_sliced, ("sa", "sb"), split_axis=0, concat_axis=0, tiled=True).reshape(L, C)
     cuts = [0, DECAY_INNER, DECAY_INNER + LA, DECAY_INNER + LA + LV, n_low]
 
     def widen(m):
@@ -790,14 +972,10 @@
     sq_mine = square[:3].reshape(3, w, SA, C).transpose(2, 0, 1, 3)
     half = SA * FS
     key_mine = key_w.reshape(w, SA, F, FS).transpose(2, 0, 1, 3).reshape(SB, RA, RC, w, half)
-    x_row, first_row, g_plane, sq, low, up_heads, key_line = start_exchange(
-        tokens, first_sliced, out_grad, sq_mine, low_mine, widen(up.T), key_mine, 1
-    )
+    x_row, sq, low, up_heads, key_line = start_exchange(tokens, sq_mine, low_mine, widen(up.T), key_mine, 1)
     x_row = x_row.reshape(L, D)
-    first_row = first_row.reshape(L, C)
     sq = sq.reshape(3, D, C)
     low = low.reshape(D, 768)
-    low_w = low[:, :640]
     up_w = up_heads.reshape(C, 640)
     vec = low[:, 640 : 640 + n_vec].astype(F32).T
     vec_heads = lax.dynamic_slice(vec, (10, a * C), (8, C))
@@ -809,16 +987,21 @@
     value_all = jnp.concatenate(
         [kv_all[:, FW + i * FS : FW + (i + 1) * FS].reshape(half, half) for i in range(D // half)], axis=1
     )
-    g_all = g_plane.transpose(3, 1, 2, 0, 4, 5).reshape(F * T, D)
-    slot = (b * RA + lax.axis_index("ra")) * RC + lax.axis_index("rc")
-    g_own = lax.dynamic_slice(g_all, (slot * T, 0), (T, D)).astype(F32)
-
-    xm, (rp, kp, vp, uw, ua, uv, ug), mid, mid_low = mix_forward(x_row, meta, vec, sq, low_w, up_w)
+
+    xm, (rp, kp, vp, uw, ua, uv, ug), mid, mid_low = mix_forward(x_row, meta, vec, sq, low, up_w)
     ins = (rp, kp, vp, uw, ua, uv, first_row)
     y, saved = recurrence_forward(ins, vec_heads, meta, segrow)
     z = (y.astype(F32) * ug).astype(BF)
-    (z_own,) = line_exchange([z.reshape(SA, T, C)], 2)
+    gather_g = (
+        out_grad,
+        (SB, RA, RC, SB, seg, D),
+        lambda o, i, j, k: o.at[:, j, k, i],
+        lambda o, i, j, k, h: o.at[h, j, k, i],
+    )
+    z_own, g_all = line_exchange([z.reshape(SA, T, C)], [gather_g], 2)
+    g_all = g_all.reshape(F * T, D)
     z_own = z_own.transpose(1, 0, 2).reshape(T, D)
+    z_share = z_own.reshape(T, SA, F, w).transpose(2, 0, 1, 3).reshape(SB, RA, RC, T, SA * w)
 
     x_own = lax.dynamic_slice(x_row, (a * T, 0), (T, D)).astype(F32)
     x1 = x_own + mm(z_own, sq3, NN)
@@ -830,7 +1013,8 @@
         return h + (s - h) * mix
 
     xc, cmix_pull = jax.vjp(channel_mix, h2, edge2, vec[18])
-    xc_all = plane_gather(xc.astype(BF), 3).reshape(F * T, D)
+    (xc_all,) = line_exchange([], [rows_gather(xc.astype(BF))], 3)
+    xc_all = xc_all.reshape(F * T, D)
     kc = jax.nn.relu(mm(xc_all, key_all, NN))
     q = (kc * kc).astype(BF)
     dkc = (mm(g_all, value_all, NT) * 2.0 * kc).astype(BF)
@@ -844,33 +1028,39 @@
     dh2, dedge2, g18 = cmix_pull(dxc.astype(F32))
     dh2 = dh2.at[-1:].add(next_line(dedge2, -1))
     dx1n, g2, g3 = norm2_pull(dh2)
-    dx1 = g_own + dx1n
+    slot = (b * RA + lax.axis_index("ra")) * RC + lax.axis_index("rc")
+    dx1 = lax.dynamic_slice(g_all, (slot * T, 0), (T, D)).astype(F32) + dx1n
     dt = dx1.astype(BF)
     dz = mm(dt, sq3, NT).astype(BF)
-    (dz_row,) = line_exchange([dz.reshape(T, SA, C).transpose(1, 0, 2)], 4)
-    dt_row = lax.all_gather(dt, "sa", axis=0, tiled=True)
+    dz_row, dt_all, z_share = line_exchange(
+        [dz.reshape(T, SA, C).transpose(1, 0, 2)], [rows_gather(dt)], 4, [z_share]
+    )
     kv_grad = lax.psum_scatter(after(kv_part, dz).reshape(-1, half), "sa", scatter_dimension=0, tiled=True)
     dz_row = dz_row.reshape(L, C).astype(F32)
 
     dy = (dz_row * ug).astype(BF)
     dug = (dz_row * y.astype(F32)).astype(BF)
     drp, dkp, dvp, duw, dua, duv, dfl, dvec = recurrence_backward(dy, saved, ins, vec_heads, meta, segrow)
-    dh1, dd, gmix = mix_backward((drp, dkp, dvp, duw, dua, duv, dug), x_row, meta, mid, vec, sq, low_w, up_w)
+    dfl = lax.all_to_all(dfl.reshape(S, seg, C), ("sa", "sb"), split_axis=0, concat_axis=0, tiled=True)
+    dh1, dd, gmix = mix_backward((drp, dkp, dvp, duw, dua, duv, dug), x_row, meta, mid, vec, sq, low, up_w)
     g0, g1 = gmix[6], gmix[7]
 
-    sq_part, down_part, up_part, sq3_part = weight_grads(xm, (drp, dkp, dvp, duw, dua, duv, dug), dd, mid_low, z, dt_row)
+    sq_part, down_part, up_part, sq3_part = weight_grads(
+        xm, (drp, dkp, dvp, duw, dua, duv, dug), dd, mid_low, z_share.reshape(F * T, SA * w), dt_all.reshape(F * T, D)
+    )
+    dfl, sq_part = lax.optimization_barrier((dfl, sq_part))
+    first_grad = dfl.reshape(SA, SB, seg, C).transpose(1, 2, 0, 3).reshape(rows_here, seg, D)
     wide = jnp.stack([g0, g1, g2, g3, *(gmix[i] for i in range(6)), g18] + [jnp.zeros_like(g0)] * 5).astype(BF)
     wide = jnp.pad(wide.T, ((0, 0), (0, 112)))
     narrow = jnp.pad(dvec.astype(BF).T, ((0, 0), (0, 120)))
     plane = (SB, RA, RC, w)
-    dh1_own, dfl_own, sq_sum, down_sum, wide_sum, up_sum, sq3_sum, narrow_sum, ffn = tail_exchange(
+    dh1_own, sq3_sum, sq_sum, down_sum, wide_sum, up_sum, narrow_sum, ffn = tail_exchange(
         dh1.reshape(SA, T, D),
-        dfl.reshape(S, seg, C),
+        sq3_part.reshape(SA, w, D),
         sq_part.reshape((3, SA) + plane + (C,)),
         down_part.reshape((SA,) + plane + (640,)),
         wide.reshape((SA,) + plane + (128,)),
         up_part.reshape(plane + (640,)),
-        sq3_part.reshape(plane + (D,)),
         narrow.reshape(plane + (128,)),
         ffn_part.reshape(SB, RA, RC, T, D),
         5,
@@ -879,11 +1069,15 @@
     _, norm1_pull = jax.vjp(lambda x: layer_norm(x, vec[0], vec[1]), x_own)
     (dx0,) = norm1_pull(dh1_own)
     mixed = (x1 + ffn.astype(F32)).astype(BF)
-    tokens_grad, mixed_out, sq_sum, down_sum, wide_sum = last_exchange(
-        [(dx1 + dx0).astype(BF).reshape(SB, seg, D), mixed.reshape(SB, seg, D)], sq_sum, [down_sum, wide_sum], 6
+    tokens_grad, mixed_out, sq_sum, down_sum, wide_sum, key_grad = last_exchange(
+        [(dx1 + dx0).astype(BF).reshape(SB, seg, D), mixed.reshape(SB, seg, D)],
+        sq_sum,
+        [down_sum, wide_sum],
+        kv_grad[:FW].reshape(SB, RA, RC, w, half),
+        6,
     )
-    first_grad = dfl_own.transpose(0, 2, 1, 3).reshape(rows_here, seg, D)
-    square_grad = jnp.concatenate([sq_sum.transpose(1, 2, 0, 3).reshape(3, w, D), sq3_sum[None]], axis=0).astype(F32)
+    sq3_sum = jnp.sum(sq3_sum.astype(F32), axis=0)
+    square_grad = jnp.concatenate([sq_sum.transpose(1, 2, 0, 3).reshape(3, w, D).astype(F32), sq3_sum[None]], axis=0)
     narrow_pieces = lambda m: [m[:, i : i + q - p] for i, p, q in zip(wide_at, cuts[:-1], cuts[1:])]
     down_grad = jnp.concatenate(narrow_pieces(jnp.sum(down_sum.astype(F32), axis=0)), axis=1)
     up_grad = jnp.concatenate(narrow_pieces(up_sum.astype(F32)), axis=1).T
@@ -892,7 +1086,6 @@
     vectors_gradient = jnp.concatenate([wide_t[:10], narrow_t, wide_t[10:11]], axis=0)
     value_grad = jnp.concatenate([kv_grad[FW + i * FS : FW + (i + 1) * FS] for i in range(D // half)], axis=1)
     value_grad = value_grad.astype(F32)
-    key_grad = lax.all_to_all(kv_grad[:FW].reshape(F, w, half), PLANE, split_axis=0, concat_axis=0, tiled=True)
     key_grad = key_grad.reshape(F, w, SA, FS).transpose(1, 2, 0, 3).reshape(w, -1).astype(F32)
     return (
         mixed_out,

time: 1110 us -> 936 us (0.84)
  Pallas kernels: 805 us -> 640 us
  local copies, waits for them, and re-layouts: 90.5 us -> 70 us
    pallas_call x6, Pallas kernels: 590 us -> 437 us  [call_net(): pl.pallas_call(kernel, out_shape=out_shapes, in_specs=[HBM] * n, out_spec...]
    pallas_call x4, Pallas kernels: 123 us -> 110 us  [the longest x1 44.9 us: recurrence_backward(): pl.pallas_call(functools.partial(blocks_kernel, backward_block, kinds, ra...]
    reshape x7 -> x5, local copies, waits for them, and re-layouts: 20.9 us -> 8.89 us  [the longest x2 4.52 us: per_device(): dfl.reshape(SA, SB, seg, C).transpose(1, 2, 0, 3).reshape(rows_here, seg, D)]
  transfers between devices with their start and end apart: 8 -> 8, of which waited for: 3 -> 3; matrix products, arithmetic and copies ran while one was open for 14% -> 13% of each run, Pallas kernels for 68% -> 59%
where the time goes in v2:
time: 936 us; the launch traced here: 929 us
  Pallas kernels  640 us (68%)
  matrix products  88.5 us (9%)
  local copies, waits for them, and re-layouts  70 us (7%)
  other arithmetic  49.7 us (5%)
  waiting for transfers between devices  41.8 us (4%)
  starting transfers between devices  24.1 us (3%)
  between operations  14.8 us (2%)
    pallas_call x6, Pallas kernels, call_net(): pl.pallas_call(kernel, out_shape=out_shapes, in_specs=[HBM] * n, out_spec...  437 us
    dot_general x8, matrix products, mm(): return lax.dot_general(a, b, d, preferred_element_type=F32)  88.5 us
    pallas_call x1, Pallas kernels, recurrence_backward(): pl.pallas_call(functools.partial(blocks_kernel, backward_block, kinds, ra...  44.9 us
    pallas_call x1, Pallas kernels, recurrence_forward(): pl.pallas_call(functools.partial(blocks_kernel, forward_block, kinds, ran...  35.9 us
    pallas_call x1, Pallas kernels, mix_backward(): pl.pallas_call(mix_backward_kernel, grid=(n,), in_specs=[tok(C)] * 7 + [t...  35.2 us
    pallas_call x1, Pallas kernels, mix_forward(): pl.pallas_call(mix_forward_kernel, grid=(L // TILE,), in_specs=[tok(D), t...  31.5 us
    pallas_call x1, Pallas kernels, weight_grads(): pl.pallas_call(weight_kernel, grid=(D // n,), in_specs=[feat] * 6 + [fix(...  26.4 us
    reduce_scatter x1, waiting for transfers between devices, per_device(): lax.psum_scatter(mm(dkc, key_all, NT).astype(BF), PLANE, scatter_dimensio...  26.1 us
  transfers between devices with their start and end apart: 8, of which 3 were waited for; matrix products, arithmetic and copies ran while one was open for 13% of the time, Pallas kernels for 59%

profile of v2, /device:TPU:0, one launch (start us, length us, event | category | flops | bytes accessed | tf_op | source)
XLA Modules:
  0.0 928.8 jit_solution(2177448115183519451)
XLA Ops:
  18.1 133.6 %shard_map.169 = (bf16[8,128,2048]{2,1,0:T(8,128)(2,1)}, bf16[3,4,2,2,2,64,512]{6,5,4,3,2,1,0:T(8,128)(2,1)}, bf16[4,2,2,2,64,768]{5,4,3,2,1,0:T(8,128)(2,1)}, b...) custom-call(bf16[2,128,2048]{2,1,0:T(8,128)(2,1)} %refs_0_.1, ...), custom_call_target="tpu_custom_call" | custom-call | tf_op jit(solution)/shard_map/pallas_call | solution.py:555
  170.8 31.5 %shard_map.170 = (bf16[1024,2048]{1,0:T(8,128)(2,1)}, bf16[1024,2048]{1,0:T(8,128)(2,1)}, bf16[1024,2048]{1,0:T(8,128)(2,1)}, bf16[1024,2048]{1,0:T(8,128)(2,1)}...) custom-call(bf16[1024,2048]{1,0:T(8,128)(2,1)} %bitcast.129, ...), custom_call_target="tpu_custom_call" | custom-call | flops 17999998976 | bytes 1048576 | tf_op jit(solution)/shard_map/pallas_call | solution.py:471
  202.2 11.9 %all-to-all-done = bf16[8,128,512]{2,1,0:T(8,128)(2,1)S(1)} async-done(((bf16[8,128,512]{2,1,0:T(8,128)(2,1)}), bf16[8,128,512]{2,1,0:T(8,128)(2,1)S(1)}, u32[]{:S(2)}, u32[]{:S(2)}) %all-to-all-start) | async-done | bytes 1048608 | tf_op jit(solution)/shard_map/all_to_all | solution.py:963
  215.1 12.8 %shard_map.171 = (bf16[1024,512]{1,0:T(8,128)(2,1)}, bf16[1024,512]{1,0:T(8,128)(2,1)}, bf16[1024,512]{1,0:T(8,128)(2,1)}, bf16[1024,512]{1,0:T(8,128)(2,1)}, bf...) custom-call(f32[1024,512]{1,0:T(8,128)} %get-tuple-element.101.refs_0_.refs_, ...), custom_call_target="tpu_custom_call" | custom-call | tf_op jit(solution)/shard_map/pallas_call | solution.py:273
  227.9 16.3 %shard_map.172.refs_6_.refs_10_ = f32[4,1024,128]{2,1,0:T(8,128)} custom-call(f32[4,1024,128]{2,1,0:T(8,128)} %get-tuple-element.113.ab), custom_call_target="tpu_custom_call" | custom-call | tf_op jit(solution)/shard_map/pallas_call | solution.py:282
  244.2 35.9 %shard_map.173 = (bf16[1024,512]{1,0:T(8,128)(2,1)}, f32[1024,512]{1,0:T(8,128)}, f32[1024,512]{1,0:T(8,128)}, f32[1024,512]{1,0:T(8,128)}, bf16[1024,512]{1,0:T...) custom-call(bf16[1024,512]{1,0:T(8,128)(2,1)} %get-tuple-element.107.refs_0_.r, ...), custom_call_target="tpu_custom_call" | custom-call | tf_op jit(solution)/shard_map/pallas_call | solution.py:287
  282.7 43.6 %shard_map.174 = (bf16[4,256,512]{2,1,0:T(8,128)(2,1)}, bf16[2,2,2,2,128,2048]{5,4,3,2,1,0:T(8,128)(2,1)}) custom-call(bf16[4,256,512]{2,1,0:T(8,128)(2,1)} %bitcast.151, bf16[2,128,2048]{2,1,0:T(8,128)(2,1)} %refs_1_.1), custom_call_target="tpu_custom_call" | custom-call | tf_op jit(solution)/shard_map/pallas_call | solution.py:555
  336.1 11.6 %collective-permute-start = (f32[1,2048]{1,0:T(1,128)S(1)}, f32[1,2048]{1,0:T(1,128)S(1)}, u32[]{:S(2)}, u32[]{:S(2)}) collective-permute-start(f32[1,2048]{1,0:T(1,128)S(1)} %slice.224), channel_id=1, source_target_pairs={{0,8},{8,16},{16,24},{1,9},{9,17},{17,25},{2,10},{10,18},{18,26},{... | collective-permute-start | bytes 24584 | tf_op jit(solution)/shard_map/ppermute | solution.py:924
  358.4 40.8 %shard_map.175 = bf16[2,2,2,256,2048]{4,3,2,1,0:T(8,128)(2,1)} custom-call(bf16[256,2048]{1,0:T(8,128)(2,1)} %add_convert_fusion.2.refs_0_), custom_call_target="tpu_custom_call" | custom-call | tf_op jit(solution)/shard_map/pallas_call | solution.py:555
  399.3 14.6 %fusion.51 = f32[2048,1024]{1,0:T(8,128)} fusion(bf16[2048,2048]{1,0:T(8,128)(2,1)} %bitcast.123, bf16[2048,1024]{1,0:T(8,128)(2,1)} %bitcast.140), kind=kOutput, calls=%fused_computation.137 | convolution fusion | flops 8589934592 | bytes 20971520 | tf_op jit(solution)/shard_map/dot_general | solution.py:18
  413.9 12.7 %multiply_convert_fusion.1 = bf16[2048,1024]{1,0:T(8,128)(2,1)S(1)} fusion(f32[2048,1024]{1,0:T(8,128)} %fusion.51, bf16[2048,2048]{1,0:T(8,128)(2,1)} %bitcast.173, bf16[1024,1024]{1,0:T(8,128)(2,1)S(1)} %bitcast.163, bf16[1024,1024]{1,0:T(8,128)(2,1)S(1)} %bitcast.161), kind=kOutput, calls=%fused_computation.7 | convolution fusion | flops 8606711808 | bytes 25165824 | tf_op jit(solution)/shard_map/dot_general | solution.py:18
  428.6 10.9 %convolution_convert_fusion.1 = bf16[2048,2048]{1,0:T(8,128)(2,1)} fusion(bf16[2048,1024]{1,0:T(8,128)(2,1)S(1)} %multiply_convert_fusion.1, bf16[2048,1024]{1,0:T(8,128)(2,1)S(1)} %bitcast.141), kind=kOutput, calls=%fused_computation.9 | convolution fusion | flops 8594128896 | bytes 16777216 | tf_op jit(solution)/shard_map/dot_general | solution.py:18
  439.8 14.0 %convolution_convert_fusion.2 = bf16[1024,2048]{1,0:T(8,128)(2,1)S(1)} fusion(bf16[2048,2048]{1,0:T(8,128)(2,1)} %bitcast.174, f32[2048,1024]{1,0:T(8,128)} %fusion.51), kind=kOutput, calls=%fused_computation.11 | convolution fusion | flops 8598323200 | bytes 20971520 | tf_op jit(solution)/shard_map/dot_general | solution.py:18
  456.2 12.0 %convolution_convert_fusion.3 = bf16[2048,1024]{1,0:T(8,128)(2,1)S(1)} fusion(bf16[2048,2048]{1,0:T(8,128)(2,1)} %bitcast.124, bf16[2048,1024]{1,0:T(8,128)(2,1)S(1)} %copy-done.39), kind=kOutput, calls=%fused_computation.12 | convolution fusion | flops 8592031744 | bytes 16777216 | tf_op jit(solution)/shard_map/dot_general | solution.py:18
  473.0 11.1 %convolution_convert_fusion = bf16[2048,2048]{1,0:T(8,128)(2,1)} fusion(bf16[1024,1024]{1,0:T(8,128)(2,1)S(1)} %bitcast.164, bf16[1024,1024]{1,0:T(8,128)(2,1)S(1)} %bitcast.162, f32[2048,1024]{1,0:T(8,128)S(1)} %bitcast.198), kind=kOutput, calls=%fused_computation.8 | convolution fusion | flops 8608808960 | bytes 20971520 | tf_op jit(solution)/shard_map/dot_general | solution.py:18
  484.1 26.1 %reduce-scatter.3.cloned.1.call-done = bf16[256,2048]{1,0:T(8,128)(2,1)} async-done(((bf16[2048,2048]{1,0:T(8,128)(2,1)}), bf16[256,2048]{1,0:T(8,128)(2,1)}) %reduce-scatter.3.cloned.1.call-update) | async-done | bytes 1048592 | tf_op jit(solution)/shard_map/reduce_scatter | solution.py:1021
  527.4 7.1 fusion.9
  542.3 52.2 %shard_map.176 = (bf16[4,256,512]{2,1,0:T(8,128)(2,1)}, bf16[2,2,2,256,2048]{4,3,2,1,0:T(8,128)(2,1)}, bf16[2,2,2,256,256]{4,3,2,1,0:T(8,128)(2,1)}) custom-call(bf16[4,256,512]{2,1,0:T(8,128)(2,1)} %bitcast.139, bf16[256,2048]{1,0:T(8,128)(2,1)} %copy-done.13, bf16[2,2,2,256,256]{4,3,2,1,0:T(8,128)(2,1)} %copy.157.refs_2_), custom_call_target="tpu_custom_call" | custom-call | tf_op jit(solution)/shard_map/pallas_call | solution.py:555
  598.3 44.9 %shard_map.177 = (bf16[1024,512]{1,0:T(8,128)(2,1)}, bf16[1024,512]{1,0:T(8,128)(2,1)}, bf16[1024,512]{1,0:T(8,128)(2,1)}, bf16[1024,512]{1,0:T(8,128)(2,1)}, bf...) custom-call(bf16[1024,512]{1,0:T(8,128)(2,1)} %get-tuple-element.206.refs_0_,, ...), custom_call_target="tpu_custom_call" | custom-call | tf_op jit(solution)/shard_map/pallas_call | solution.py:314
  643.2 7.0 all-to-all-start.1
  650.2 35.2 %shard_map.178 = (bf16[1024,2048]{1,0:T(8,128)(2,1)}, bf16[1024,640]{1,0:T(8,128)(2,1)}, f32[8,2048]{1,0:T(8,128)}) custom-call(bf16[1024,512]{1,0:T(8,128)(2,1)} %get-tuple-element.129.drp, bf16[1024,512]{1,0:T(8,128)(2,1)} %get-tuple-element.130.dkp, bf16[1024,512]{1,0:T(8,128)(2,1)} %get-tuple-element.131.dvp, bf16[1024,512]{1,0:T(8,128)(2,1)} %get-tuple-element.132.duw, ...), custom_call_target="tpu_custom_call" | custom-call | flops 20999999488 | bytes 1048576 | tf_op jit(solution)/shard_map/pallas_call | solution.py:494
  690.4 26.4 %shard_map.179 = (bf16[3,2048,512]{2,1,0:T(8,128)(2,1)}, bf16[2048,640]{1,0:T(8,128)(2,1)}, bf16[512,640]{1,0:T(8,128)(2,1)}, bf16[256,2048]{1,0:T(8,128)(2,1)}) custom-call(bf16[1024,2048]{1,0:T(8,128)(2,1)} %get-tuple-element.137.x0, bf16[1024,2048]{1,0:T(8,128)(2,1)} %get-tuple-element.138.x1, bf16[1024,2048]{1,0:T(8,128)(2,1)} %get-tuple-element.139.x2, ...), custom_call_target="tpu_custom_call" | custom-call | flops 15600000000 | bytes 1048576 | tf_op jit(solution)/shard_map/pallas_call | solution.py:445
  716.8 117.1 %shard_map.180 = (bf16[4,256,2048]{2,1,0:T(8,128)(2,1)}, bf16[4,64,2048]{2,1,0:T(8,128)(2,1)}, bf16[3,4,64,512]{3,2,1,0:T(8,128)(2,1)}, bf16[4,64,640]{2,1,0:T(8...) custom-call(bf16[4,256,2048]{2,1,0:T(8,128)(2,1)} %bitcast.152, ...), custom_call_target="tpu_custom_call" | custom-call | tf_op jit(solution)/shard_map/pallas_call | solution.py:555
  854.9 49.7 %shard_map.181 = (bf16[2,128,2048]{2,1,0:T(8,128)(2,1)}, bf16[2,128,2048]{2,1,0:T(8,128)(2,1)}, bf16[4,3,64,512]{3,2,1,0:T(8,128)(2,1)}, bf16[4,64,640]{2,1,0:T(...) custom-call(bf16[2,128,2048]{2,1,0:T(8,128)(2,1)} %bitcast.155, ...), custom_call_target="tpu_custom_call" | custom-call | tf_op jit(solution)/shard_map/pallas_call | solution.py:555
  (235 shorter events, 135.2 us)
Async XLA Ops:
  7.2 154.3 %copy-start = (s32[2,4]{1,0:T(2,128)S(1)}, s32[2,4]{1,0:T(2,128)}, u32[]{:S(2)}) copy-start(s32[2,4]{1,0:T(2,128)} %param.14) | copy-start | bytes 100
  7.2 6.1 slice-start
  7.2 6.0 copy-start.36
  7.2 7.0 copy-start.22
  7.2 320.6 %all-gather.7.cloned.1.call-start = ((), (), s32[]{:S(2)}) async-start(), calls=%async_computation.7 | async-start | bytes 8650752 | tf_op jit(solution)/shard_map/all_gather | solution.py:961
  9.1 338.6 %all-gather.5.cloned.1.call-start = ((), (), s32[]{:S(2)}) async-start(), calls=%async_computation.6 | async-start | bytes 10485760 | tf_op jit(solution)/shard_map/all_gather | solution.py:985
  16.5 135.2 %copy-start.23 = (bf16[256,2048]{1,0:T(8,128)(2,1)S(1)}, bf16[256,2048]{1,0:T(8,128)(2,1)}, u32[]{:S(2)}) copy-start(bf16[256,2048]{1,0:T(8,128)(2,1)} %param.20) | copy-start | bytes 3145732
  157.6 56.5 %all-to-all-start = ((bf16[8,128,512]{2,1,0:T(8,128)(2,1)}), bf16[8,128,512]{2,1,0:T(8,128)(2,1)S(1)}, u32[]{:S(2)}, u32[]{:S(2)}) async-start(bf16[8,128,512]{2,1,0:T(8,128)(2,1)} %bitcast.13), calls=%async_computation | async-start | bytes 2097152 | tf_op jit(solution)/shard_map/all_to_all | solution.py:963
  161.4 348.8 %reduce-scatter.3.cloned.1.call-start = ((), (), s32[]{:S(2)}) async-start(), calls=%async_computation.4 | async-start | bytes 9437184 | tf_op jit(solution)/shard_map/reduce_scatter | solution.py:1021
  244.2 35.9 %copy-start.9 = (f32[1024,512]{1,0:T(8,128)S(1)}, f32[1024,512]{1,0:T(8,128)}, u32[]{:S(2)}) copy-start(f32[1024,512]{1,0:T(8,128)} %get-tuple-element.115) | copy-start | bytes 6291460
  336.1 20.3 %collective-permute-start = (f32[1,2048]{1,0:T(1,128)S(1)}, f32[1,2048]{1,0:T(1,128)S(1)}, u32[]{:S(2)}, u32[]{:S(2)}) collective-permute-start(f32[1,2048]{1,0:T(1,128)S(1)} %slice.224), channel_id=1, source_target_pairs={{0,8},{8,16},{16,24},{1,9},{9,17},{17,25},{2,10},{10,18},{18,26},{... | collective-permute-start | bytes 24584 | tf_op jit(solution)/shard_map/ppermute | solution.py:924
  347.7 6.2 copy-start.10
  399.3 14.6 %copy-start.18 = (bf16[4,256,1024]{2,1,0:T(8,128)(2,1)S(1)}, bf16[4,256,1024]{2,1,0:T(8,128)(2,1)}, u32[]{:S(2)}) copy-start(bf16[4,256,1024]{2,1,0:T(8,128)(2,1)} %get-tuple-element.195) | copy-start | bytes 6291460
  399.3 14.6 %copy-start.20 = (bf16[4,256,1024]{2,1,0:T(8,128)(2,1)S(1)}, bf16[4,256,1024]{2,1,0:T(8,128)(2,1)}, u32[]{:S(2)}) copy-start(bf16[4,256,1024]{2,1,0:T(8,128)(2,1)} %get-tuple-element.196) | copy-start | bytes 6291460
  413.9 14.7 %copy-start.14 = (bf16[4,512,1024]{2,1,0:T(8,128)(2,1)S(1)}, bf16[4,512,1024]{2,1,0:T(8,128)(2,1)}, u32[]{:S(2)}) copy-start(bf16[4,512,1024]{2,1,0:T(8,128)(2,1)} %slice.227) | copy-start | bytes 12582916
  439.6 413.1 %reduce-scatter.5.cloned.1.call-start = ((), (), s32[]{:S(2)}) async-start(), calls=%async_computation.5 | async-start | bytes 10485760 | tf_op jit(solution)/shard_map/reduce_scatter | solution.py:1038
  453.8 18.6 %slice-start.3 = ((s8[8388608]{0:T(1024)(128)(4,1)}), s8[4194304]{0:T(1024)(128)(4,1)S(1)}, s32[]{:S(2)}) async-start(s8[8388608]{0:T(1024)(128)(4,1)} %bitcast.197), calls=%async_computation.11 | async-start | bytes 8388608
  456.2 16.2 %slice-start.4 = ((s8[8388608]{0:T(1024)(128)(4,1)}), s8[4194304]{0:T(1024)(128)(4,1)S(1)}, s32[]{:S(2)}) async-start(s8[8388608]{0:T(1024)(128)(4,1)} %bitcast.197), calls=%async_computation.12 | async-start | bytes 8388608
  468.2 4.8 copy-start.21
  514.0 5.7 collective-permute-start.1
  527.4 7.1 copy-start.13
  542.3 52.2 %copy-start.16 = (bf16[1024,512]{1,0:T(8,128)(2,1)S(1)}, bf16[1024,512]{1,0:T(8,128)(2,1)}, u32[]{:S(2)}) copy-start(bf16[1024,512]{1,0:T(8,128)(2,1)} %get-tuple-element.114) | copy-start | bytes 3145732
  643.2 73.6 %all-to-all-start.1 = ((bf16[8,128,512]{2,1,0:T(8,128)(2,1)}), bf16[8,128,512]{2,1,0:T(8,128)(2,1)S(1)}, u32[]{:S(2)}, u32[]{:S(2)}) async-start(bf16[8,128,512]{2,1,0:T(8,128)(2,1)} %bitcast.168), calls=%async_computation.2 | async-start | bytes 2097152 | tf_op jit(solution)/shard_map/all_to_all | solution.py:1044
  650.2 36.1 %copy-start.35 = (f32[8,512]{1,0:T(8,128)S(1)}, f32[8,512]{1,0:T(8,128)}, u32[]{:S(2)}) copy-start(f32[8,512]{1,0:T(8,128)} %get-tuple-element.154) | copy-start | bytes 49156
  (29 other events, 68.8 us)
Sparse Core Ops, SparseCore 0:
  10.9 129.8 all-gather.6
  154.6 190.5 all-gather.4
  439.7 70.4 reduce-scatter.2
  534.6 182.3 reduce-scatter.4

commit v3 on v2

--- a/solution.py
+++ b/solution.py
@@ -420,6 +420,31 @@
         gv[7:8, sl] += jnp.sum(g, axis=0, keepdims=True)
 
 
+def hidden_kernel(x, g, key, value, q, dk, dx):
+    k = jnp.maximum(mm(x[...], key[...], NN), 0.0)
+    q[...] = (k * k).astype(BF)
+    d = (mm(g[...], value[...], NT) * (2.0 * k)).astype(BF)
+    dk[...] = d
+    dx[...] = mm(d, key[...], NT).astype(BF)
+
+
+def hidden(x, g, key, value):
+    n, D = x.shape
+    H = key.shape[1]
+    tok = lambda m: pl.BlockSpec((256, m), lambda i: (i, 0))
+    fix = lambda s: pl.BlockSpec(s, lambda i: (0, 0))
+    sd = lambda m: jax.ShapeDtypeStruct((n, m), BF)
+    return pl.pallas_call(
+        hidden_kernel,
+        grid=(n // 256,),
+        in_specs=[tok(D), tok(D), fix(key.shape), fix(value.shape)],
+        out_specs=[tok(H), tok(H), tok(D)],
+        out_shape=[sd(H), sd(H), sd(D)],
+        cost_estimate=takes(30),
+        compiler_params=params(),
+    )(x, g, key, value)
+
+
 def weight_kernel(x0, x1, x2, x3, x4, x5, drp, dkp, dvp, dd, duw, dua, duv, dug, mid, z, dt, sq, down, up, sq3):
     sq[0] = mm(x0[...], drp[...], TN).astype(BF)
     sq[1] = mm(x2[...], dkp[...], TN).astype(BF)
@@ -458,7 +483,7 @@
     )(*xm, *grads[:3], dd, *grads[3:], mid, z, dt)
 
 
-TILE = 128
+TILE = 256
 
 
 def mix_forward(x, meta, vec, sq, low, up):
@@ -804,6 +829,7 @@
 def tail_exchange(dh, sq3, sq, down, wide, up, narrow, ffn, cid):
     A = lax.axis_size("sa")
     leads = [2, 1, 1, 0, 0, 0]
+    halved = [1, 0, 0, None, None, 0]
     arrays = [sq, down, wide, up, narrow, ffn]
     blocks = [x.shape[:n] + x.shape[n + 3 :] for x, n in zip(arrays, leads)]
     n = len(arrays)
@@ -832,8 +858,17 @@
             open_ += [net.send(x.at[net.at(s)[0]], o.at[a], s) for s in line]
             net.keep(x.at[a], o.at[a])
 
-        def add(t, k, terms):
-            shape = blocks[t]
+        def part(t, h):
+            if h is None or halved[t] is None:
+                return ()
+            size = blocks[t][halved[t]] // 2
+            return (slice(None),) * halved[t] + (pl.ds(h * size, size),)
+
+        def add(t, k, terms, h=None):
+            shape, start = list(blocks[t]), [0] * len(blocks[t])
+            if h is not None:
+                shape[halved[t]] //= 2
+                start[halved[t]] = h * shape[halved[t]]
             step = min(shape[-2], 16)
             per = shape[-2] // step
             count = per
@@ -844,32 +879,60 @@
             def _(r):
                 index = []
                 rest = r // per
-                for size in reversed(shape[:-2]):
-                    index.insert(0, rest % size)
+                for size, first in zip(reversed(shape[:-2]), reversed(start[:-2])):
+                    index.insert(0, first + rest % size)
                     rest = rest // size
-                at = (*index, pl.ds(pl.multiple_of(r % per * step, step), step))
+                at = (*index, pl.ds(pl.multiple_of(start[-2] + r % per * step, step), step))
                 total = own[t][(k, *at)].astype(F32)
                 for ref, i in terms:
                     total = total + ref[(i, *at)].astype(F32)
                 own[t][(k, *at)] = total.astype(BF)
 
-        sent = []
+        def slot(i, j):
+            return 2 * i + j
+
+        nb, ny = net.at(CHIPS[0])[1], net.at(CHIPS[1])[2]
+        ways = [
+            (CHIPS[0], CHIPS[1], lambda j: slot(nb, j), lambda j: slot(b, j), slot(b, ny)),
+            (CHIPS[1], CHIPS[0], lambda j: slot(j, ny), lambda j: slot(j, y), slot(nb, y)),
+        ]
+        me = slot(b, y)
+        sent = [[] for _ in range(n)]
         for t in range(n):
             for copy in cores[t] + mine[t]:
                 copy.wait()
-            for k, s in enumerate(CHIPS):
-                to = net.at(s)
-                slot = 2 * to[1] + to[2]
-                add(t, slot, [(other[t], slot)])
-                sent.append(net.send(own[t].at[slot], chips[t].at[k], s))
-        me = 2 * b + y
+            for k in range(4):
+                add(t, k, [(other[t], k)])
+            if halved[t] is None:
+                for k, s in enumerate(CHIPS):
+                    to = net.at(s)
+                    sent[t].append(net.send(own[t].at[slot(to[1], to[2])], chips[t].at[k], s))
+                continue
+            for h, (s, _, theirs, _, _) in enumerate(ways):
+                for j in range(2):
+                    src, dst = own[t].at[(theirs(j), *part(t, h))], chips[t].at[(j, *part(t, h))]
+                    sent[t].append(net.send(src, dst, s))
+        second = [[] for _ in range(n)]
         for t in range(n):
-            for copy in sent[3 * t : 3 * t + 3]:
+            if halved[t] is None:
+                continue
+            for h, (_, s, _, ours, across) in enumerate(ways):
+                for j in range(2):
+                    sent[t][2 * h + j].wait_recv()
+                    add(t, ours(j), [(chips[t], j)], h)
+                src, dst = own[t].at[(across, *part(t, h))], chips[t].at[(2, *part(t, h))]
+                second[t].append(net.send(src, dst, s))
+        for t in range(n):
+            for copy in second[t] if second[t] else sent[t]:
                 copy.wait_recv()
-            add(t, me, [(other[t], me)] + [(chips[t], k) for k in range(3)])
+            if halved[t] is None:
+                add(t, me, [(chips[t], k) for k in range(3)])
+            else:
+                add(t, me, [(chips[t], 2)])
             net.keep(own[t].at[me], pos[t])
-        for copy in sent:
-            copy.wait_send()
+        for t in range(n):
+            for copy in sent[t] + second[t]:
+                copy.wait_send()
         for copy in open_:
             copy.wait()
         net.settle()
@@ -877,7 +940,7 @@
     sd = jax.ShapeDtypeStruct
     shapes = [sd(dh.shape, BF), sd(sq3.shape, BF)] + [sd(s, BF) for s in blocks]
     scratch = [pltpu.VMEM((m,) + s, BF) for m in (4, 4, 3) for s in blocks]
-    n_send = 2 * (A - 1) + 7 * n
+    n_send = 2 * (A - 1) + 10 * n
     return call_net(body, [dh, sq3, *arrays], shapes, cid, 2 + 5 * n, n_send, scratch)
 
 
@@ -958,21 +1021,21 @@
     keep_row = (1.0 - reset)[:, None]
     keep_own = lax.dynamic_slice(keep_row, (a * T, 0), (T, 1))
 
-    sq3 = lax.all_gather(square[3], AXES, axis=0, tiled=True)
     first_sliced = first_values.reshape(rows_here, seg, SA, C).transpose(2, 0, 1, 3).reshape(S, seg, C)
     first_row = lax.all_to_all(first_sliced, ("sa", "sb"), split_axis=0, concat_axis=0, tiled=True).reshape(L, C)
     cuts = [0, DECAY_INNER, DECAY_INNER + LA, DECAY_INNER + LA + LV, n_low]
 
-    def widen(m):
-        pieces = [m[:, i:j] for i, j in zip(cuts[:-1], cuts[1:])]
-        return jnp.concatenate([jnp.pad(p, ((0, 0), (0, -p.shape[1] % 128))) for p in pieces], axis=1)
-
     wide_at = [0, 128, 256, 384]
-    low_mine = jnp.concatenate([widen(down), jnp.pad(vectors.T, ((0, 0), (0, 128 - n_vec)))], axis=1)
+    spot = jnp.concatenate([at + jnp.arange(q - p) for at, p, q in zip(wide_at, cuts[:-1], cuts[1:])])
+    place = (spot[:, None] == jnp.arange(768)[None, :]).astype(BF)
+    place_vec = (640 + jnp.arange(n_vec)[:, None] == jnp.arange(768)[None, :]).astype(BF)
+    low_mine = (mm(down, place, NN) + mm(vectors, place_vec, TN)).astype(BF)
+    up_mine = mm(up, place[:, :640], TN).astype(BF)
     sq_mine = square[:3].reshape(3, w, SA, C).transpose(2, 0, 1, 3)
     half = SA * FS
     key_mine = key_w.reshape(w, SA, F, FS).transpose(2, 0, 1, 3).reshape(SB, RA, RC, w, half)
-    x_row, sq, low, up_heads, key_line = start_exchange(tokens, sq_mine, low_mine, widen(up.T), key_mine, 1)
+    x_row, sq, low, up_heads, key_line = start_exchange(tokens, sq_mine, low_mine, up_mine, key_mine, 1)
+    sq3 = lax.all_gather(after(square[3], x_row), AXES, axis=0, tiled=True)
     x_row = x_row.reshape(L, D)
     sq = sq.reshape(3, D, C)
     low = low.reshape(D, 768)
@@ -982,31 +1045,36 @@
     FW = F * w
     halves = [slice(i * half, (i + 1) * half) for i in range(D // half)]
     kv = jnp.concatenate([key_line.reshape(FW, half), *(value_w[:, s] for s in halves)], axis=0)
-    kv_all = lax.all_gather(kv, "sa", axis=0)
+
+    xm, (rp, kp, vp, uw, ua, uv, ug), mid, mid_low = mix_forward(x_row, meta, vec, sq, low, up_w)
+    ins = (rp, kp, vp, uw, ua, uv, first_row)
+    y, saved = recurrence_forward(ins, vec_heads, meta, segrow)
+    kv_all = lax.all_gather(after(kv, sq3, saved[9]), "sa", axis=0)
     key_all = kv_all[:, :FW].reshape(D, half)
     value_all = jnp.concatenate(
         [kv_all[:, FW + i * FS : FW + (i + 1) * FS].reshape(half, half) for i in range(D // half)], axis=1
     )
-
-    xm, (rp, kp, vp, uw, ua, uv, ug), mid, mid_low = mix_forward(x_row, meta, vec, sq, low, up_w)
-    ins = (rp, kp, vp, uw, ua, uv, first_row)
-    y, saved = recurrence_forward(ins, vec_heads, meta, segrow)
     z = (y.astype(F32) * ug).astype(BF)
+    before = jnp.concatenate([jnp.zeros((1, 16, C), BF), z.reshape(SA, T, C)[:-1, T - 16 :]], axis=0)
+    z_blocks = jnp.concatenate([before, z.reshape(SA, T, C)], axis=1)
     gather_g = (
         out_grad,
         (SB, RA, RC, SB, seg, D),
         lambda o, i, j, k: o.at[:, j, k, i],
         lambda o, i, j, k, h: o.at[h, j, k, i],
     )
-    z_own, g_all = line_exchange([z.reshape(SA, T, C)], [gather_g], 2)
+    z_own, g_all = line_exchange([z_blocks], [gather_g], 2)
     g_all = g_all.reshape(F * T, D)
-    z_own = z_own.transpose(1, 0, 2).reshape(T, D)
+    z_more = z_own.transpose(1, 0, 2).reshape(T + 16, D)
+    z_own = z_more[16:]
     z_share = z_own.reshape(T, SA, F, w).transpose(2, 0, 1, 3).reshape(SB, RA, RC, T, SA * w)
 
     x_own = lax.dynamic_slice(x_row, (a * T, 0), (T, D)).astype(F32)
-    x1 = x_own + mm(z_own, sq3, NN)
+    x_before = lax.dynamic_slice(x_row, (jnp.maximum(a * T - 16, 0), 0), (16, D)).astype(F32)
+    x1_more = jnp.concatenate([x_before, x_own], axis=0) + mm(z_more, sq3, NN)
+    x1 = x1_more[16:]
     h2, norm2_pull = jax.vjp(layer_norm, x1, vec[2], vec[3])
-    edge2 = next_line(h2[-1:], 1)
+    edge2 = layer_norm(x1_more[15:16], vec[2], vec[3])
 
     def channel_mix(h, edge, mix):
         s = jnp.concatenate([edge, h[:-1]], axis=0) * keep_own
@@ -1015,10 +1083,8 @@
     xc, cmix_pull = jax.vjp(channel_mix, h2, edge2, vec[18])
     (xc_all,) = line_exchange([], [rows_gather(xc.astype(BF))], 3)
     xc_all = xc_all.reshape(F * T, D)
-    kc = jax.nn.relu(mm(xc_all, key_all, NN))
-    q = (kc * kc).astype(BF)
-    dkc = (mm(g_all, value_all, NT) * 2.0 * kc).astype(BF)
-    dxc = lax.psum_scatter(mm(dkc, key_all, NT).astype(BF), PLANE, scatter_dimension=0, tiled=True)
+    q, dkc, dxc_part = hidden(xc_all, g_all, key_all, value_all)
+    dxc = lax.psum_scatter(dxc_part, PLANE, scatter_dimension=0, tiled=True)
     ffn_part = mm(q, value_all, NN).astype(BF)
     value_part = mm(q, g_all, TN).astype(BF).reshape(SA, FS, D)
     key_part = mm(xc_all, dkc, TN).astype(BF).reshape(SA, FW, half)
@@ -1035,7 +1101,7 @@
     dz_row, dt_all, z_share = line_exchange(
         [dz.reshape(T, SA, C).transpose(1, 0, 2)], [rows_gather(dt)], 4, [z_share]
     )
-    kv_grad = lax.psum_scatter(after(kv_part, dz).reshape(-1, half), "sa", scatter_dimension=0, tiled=True)
+    kv_grad = lax.psum_scatter(kv_part.reshape(-1, half), "sa", scatter_dimension=0, tiled=True)
     dz_row = dz_row.reshape(L, C).astype(F32)
 
     dy = (dz_row * ug).astype(BF)

time: 936 us -> 910 us (0.972)
  matrix products: 88.5 us -> 50.6 us
  starting transfers between devices: 24.1 us -> 13.5 us
    dot_general x8, matrix products: 88.5 us -> 50.6 us  [mm(): return lax.dot_general(a, b, d, preferred_element_type=F32)]
    pallas_call x0 -> x1, Pallas kernels: none -> 32.8 us  [hidden(): pl.pallas_call(hidden_kernel, grid=(n // 256,), in_specs=[tok(D), tok(D),...]
    all_gather x2, waiting for transfers between devices: 0.04 us -> 20.2 us  [the longest x1 10.2 us: per_device(): kv_all = lax.all_gather(after(kv, sq3, saved[9]), 'sa', axis=0)]
    pallas_call x6, Pallas kernels: 437 us -> 418 us  [call_net(): pl.pallas_call(kernel, out_shape=out_shapes, in_specs=[HBM] * n, out_spec...]
    ppermute x2 -> x1, starting transfers between devices: 13 us -> 1.29 us  [next_line(): lax.ppermute(value, 'sa', [(i, i + steps) for i in range(first, last)])]
    all_to_all x1, waiting for transfers between devices: 11.9 us -> 0.28 us  [per_device(): lax.all_to_all(first_sliced, ('sa', 'sb'), split_axis=0, concat_axis=0, t...]
    unnamed x94 -> x85, local copies, waits for them, and re-layouts: 19.5 us -> 17.8 us
  transfers between devices with their start and end apart: 8 -> 7, of which waited for: 3 -> 5; matrix products, arithmetic and copies ran while one was open for 13% -> 14% of each run, Pallas kernels for 59% -> 52%
where the time goes in v3:
time: 910 us; the launch traced here: 900 us
  Pallas kernels  644 us (71%)
  local copies, waits for them, and re-layouts  67 us (7%)
  other arithmetic  57.4 us (6%)
  waiting for transfers between devices  51.1 us (6%)
  matrix products  50.6 us (6%)
  between operations  16.4 us (2%)
  starting transfers between devices  13.5 us (1%)
    pallas_call x6, Pallas kernels, call_net(): pl.pallas_call(kernel, out_shape=out_shapes, in_specs=[HBM] * n, out_spec...  418 us
    dot_general x8, matrix products, mm(): return lax.dot_general(a, b, d, preferred_element_type=F32)  50.6 us
    pallas_call x1, Pallas kernels, recurrence_backward(): pl.pallas_call(functools.partial(blocks_kernel, backward_block, kinds, ra...  44.8 us
    pallas_call x1, Pallas kernels, recurrence_forward(): pl.pallas_call(functools.partial(blocks_kernel, forward_block, kinds, ran...  35.9 us
    pallas_call x1, Pallas kernels, hidden(): pl.pallas_call(hidden_kernel, grid=(n // 256,), in_specs=[tok(D), tok(D),...  32.8 us
    pallas_call x1, Pallas kernels, mix_forward(): pl.pallas_call(mix_forward_kernel, grid=(L // TILE,), in_specs=[tok(D), t...  28.5 us
    pallas_call x1, Pallas kernels, mix_backward(): pl.pallas_call(mix_backward_kernel, grid=(n,), in_specs=[tok(C)] * 7 + [t...  28 us
    pallas_call x1, Pallas kernels, weight_grads(): pl.pallas_call(weight_kernel, grid=(D // n,), in_specs=[feat] * 6 + [fix(...  26.2 us
  transfers between devices with their start and end apart: 7, of which 5 were waited for; matrix products, arithmetic and copies ran while one was open for 14% of the time, Pallas kernels for 52%

profile of v3, /device:TPU:0, one launch (start us, length us, event | category | flops | bytes accessed | tf_op | source)
XLA Modules:
  0.0 899.9 jit_solution(12712077756088590258)
XLA Ops:
  15.2 94.2 %shard_map.169 = (bf16[8,128,2048]{2,1,0:T(8,128)(2,1)}, bf16[3,4,2,2,2,64,512]{6,5,4,3,2,1,0:T(8,128)(2,1)}, bf16[4,2,2,2,64,768]{5,4,3,2,1,0:T(8,128)(2,1)}, b...) custom-call(bf16[2,128,2048]{2,1,0:T(8,128)(2,1)} %refs_0_.1, ...), custom_call_target="tpu_custom_call" | custom-call | tf_op jit(solution)/shard_map/pallas_call | solution.py:580
  123.6 28.5 %shard_map.170 = (bf16[1024,2048]{1,0:T(8,128)(2,1)}, bf16[1024,2048]{1,0:T(8,128)(2,1)}, bf16[1024,2048]{1,0:T(8,128)(2,1)}, bf16[1024,2048]{1,0:T(8,128)(2,1)}...) custom-call(bf16[1024,2048]{1,0:T(8,128)(2,1)} %bitcast.131, ...), custom_call_target="tpu_custom_call" | custom-call | flops 17999998976 | bytes 1048576 | tf_op jit(solution)/shard_map/pallas_call | solution.py:496
  153.4 13.2 %shard_map.171 = (bf16[1024,512]{1,0:T(8,128)(2,1)}, bf16[1024,512]{1,0:T(8,128)(2,1)}, bf16[1024,512]{1,0:T(8,128)(2,1)}, bf16[1024,512]{1,0:T(8,128)(2,1)}, bf...) custom-call(f32[1024,512]{1,0:T(8,128)} %get-tuple-element.105.refs_0_.refs_, ...), custom_call_target="tpu_custom_call" | custom-call | tf_op jit(solution)/shard_map/pallas_call | solution.py:273
  166.6 16.3 %shard_map.172.refs_6_.refs_10_ = f32[4,1024,128]{2,1,0:T(8,128)} custom-call(f32[4,1024,128]{2,1,0:T(8,128)} %get-tuple-element.117.ab), custom_call_target="tpu_custom_call" | custom-call | tf_op jit(solution)/shard_map/pallas_call | solution.py:282
  182.9 10.0 %all-gather.4.cloned.1.call-done = bf16[2048,2048]{1,0:T(8,128)(2,1)} async-done(((bf16[64,2048]{1,0:T(8,128)(2,1)}), bf16[2048,2048]{1,0:T(8,128)(2,1)}) %all-gather.4.cloned.1.call-update) | async-done | bytes 8388624 | tf_op jit(solution)/shard_map/all_gather | solution.py:1038
  197.0 35.9 %shard_map.173 = (bf16[1024,512]{1,0:T(8,128)(2,1)}, f32[1024,512]{1,0:T(8,128)}, f32[1024,512]{1,0:T(8,128)}, f32[1024,512]{1,0:T(8,128)}, bf16[1024,512]{1,0:T...) custom-call(bf16[1024,512]{1,0:T(8,128)(2,1)} %get-tuple-element.111.refs_0_.r, ...), custom_call_target="tpu_custom_call" | custom-call | tf_op jit(solution)/shard_map/pallas_call | solution.py:287
  235.6 43.5 %shard_map.174 = (bf16[4,272,512]{2,1,0:T(8,128)(2,1)}, bf16[2,2,2,2,128,2048]{5,4,3,2,1,0:T(8,128)(2,1)}) custom-call(bf16[4,272,512]{2,1,0:T(8,128)(2,1)} %fusion.20.refs_0_, bf16[2,128,2048]{2,1,0:T(8,128)(2,1)} %refs_1_.1), custom_call_target="tpu_custom_call" | custom-call | tf_op jit(solution)/shard_map/pallas_call | solution.py:580
  281.1 5.9 convolution_add_fusion
  295.4 60.7 %shard_map.175 = bf16[2,2,2,256,2048]{4,3,2,1,0:T(8,128)(2,1)} custom-call(bf16[256,2048]{1,0:T(8,128)(2,1)} %add_convert_fusion.2.refs_0_), custom_call_target="tpu_custom_call" | custom-call | tf_op jit(solution)/shard_map/pallas_call | solution.py:580
  356.1 10.2 %all-gather.6.cloned.1.call-done = bf16[4096,1024]{1,0:T(8,128)(2,1)} async-done(((bf16[1024,1024]{1,0:T(8,128)(2,1)}), bf16[4096,1024]{1,0:T(8,128)(2,1)}) %all-gather.6.cloned.1.call-update) | async-done | bytes 8388624 | tf_op jit(solution)/shard_map/all_gather | solution.py:1052
  376.2 32.8 %shard_map.176 = (bf16[2048,1024]{1,0:T(8,128)(2,1)}, bf16[2048,1024]{1,0:T(8,128)(2,1)}, bf16[2048,2048]{1,0:T(8,128)(2,1)}) custom-call(bf16[2048,2048]{1,0:T(8,128)(2,1)} %bitcast.121, bf16[2048,2048]{1,0:T(8,128)(2,1)} %bitcast.175, bf16[2048,1024]{1,0:T(8,128)(2,1)} %bitcast.147, bf16[1024,2048]{1,0:T(8,128)(2,1)} %pad_maximum_fusion.1.value), custom_call_target="tpu_custom_call" | custom-call | flops 17999998976 | bytes 1048576 | tf_op jit(solution)/shard_map/pallas_call | solution.py:437
  409.5 12.8 %convolution_convert_fusion.1 = bf16[1024,2048]{1,0:T(8,128)(2,1)S(1)} fusion(bf16[2048,1024]{1,0:T(8,128)(2,1)} %get-tuple-element.127, bf16[2048,2048]{1,0:T(8,128)(2,1)} %bitcast.176), kind=kOutput, calls=%fused_computation.4 | convolution fusion | flops 8592031744 | bytes 16777216 | tf_op jit(solution)/shard_map/dot_general | solution.py:18
  424.7 11.5 %convolution_convert_fusion.2 = bf16[2048,1024]{1,0:T(8,128)(2,1)S(1)} fusion(bf16[2048,2048]{1,0:T(8,128)(2,1)} %bitcast.122, bf16[2048,1024]{1,0:T(8,128)(2,1)S(1)} %copy-done.38), kind=kOutput, calls=%fused_computation.5 | convolution fusion | flops 8592031744 | bytes 16777216 | tf_op jit(solution)/shard_map/dot_general | solution.py:18
  442.9 10.9 %convolution_convert_fusion = bf16[2048,2048]{1,0:T(8,128)(2,1)} fusion(bf16[2048,1024]{1,0:T(8,128)(2,1)S(1)} %copy-done.37, bf16[1024,1024]{1,0:T(8,128)(2,1)S(1)} %bitcast.130, bf16[1024,1024]{1,0:T(8,128)(2,1)S(1)} %bitcast.128), kind=kOutput, calls=%fused_computation.2 | convolution fusion | flops 8602517504 | bytes 16777216 | tf_op jit(solution)/shard_map/dot_general | solution.py:18
  453.8 24.8 %reduce-scatter.3.cloned.1.call-done = bf16[256,2048]{1,0:T(8,128)(2,1)} async-done(((bf16[2048,2048]{1,0:T(8,128)(2,1)}), bf16[256,2048]{1,0:T(8,128)(2,1)}) %reduce-scatter.3.cloned.1.call-update) | async-done | bytes 1048592 | tf_op jit(solution)/shard_map/reduce_scatter | solution.py:1087
  493.9 5.7 collective-permute-done
  507.3 7.2 convolution_convert_fusion.3
  519.0 52.2 %shard_map.177 = (bf16[4,256,512]{2,1,0:T(8,128)(2,1)}, bf16[2,2,2,256,2048]{4,3,2,1,0:T(8,128)(2,1)}, bf16[2,2,2,256,256]{4,3,2,1,0:T(8,128)(2,1)}) custom-call(bf16[4,256,512]{2,1,0:T(8,128)(2,1)} %bitcast.146, bf16[256,2048]{1,0:T(8,128)(2,1)} %copy-done.17, bf16[2,2,2,256,256]{4,3,2,1,0:T(8,128)(2,1)} %copy.131.refs_2_), custom_call_target="tpu_custom_call" | custom-call | tf_op jit(solution)/shard_map/pallas_call | solution.py:580
  575.0 44.8 %shard_map.178 = (bf16[1024,512]{1,0:T(8,128)(2,1)}, bf16[1024,512]{1,0:T(8,128)(2,1)}, bf16[1024,512]{1,0:T(8,128)(2,1)}, bf16[1024,512]{1,0:T(8,128)(2,1)}, bf...) custom-call(bf16[1024,512]{1,0:T(8,128)(2,1)} %get-tuple-element.208.refs_0_,, ...), custom_call_target="tpu_custom_call" | custom-call | tf_op jit(solution)/shard_map/pallas_call | solution.py:314
  619.9 7.7 all-to-all-start.1
  627.6 28.0 %shard_map.179 = (bf16[1024,2048]{1,0:T(8,128)(2,1)}, bf16[1024,640]{1,0:T(8,128)(2,1)}, f32[8,2048]{1,0:T(8,128)}) custom-call(bf16[1024,512]{1,0:T(8,128)(2,1)} %get-tuple-element.138.drp, bf16[1024,512]{1,0:T(8,128)(2,1)} %get-tuple-element.139.dkp, bf16[1024,512]{1,0:T(8,128)(2,1)} %get-tuple-element.140.dvp, bf16[1024,512]{1,0:T(8,128)(2,1)} %get-tuple-element.141.duw, ...), custom_call_target="tpu_custom_call" | custom-call | flops 20999999488 | bytes 1048576 | tf_op jit(solution)/shard_map/pallas_call | solution.py:519
  660.5 26.2 %shard_map.180 = (bf16[3,2048,512]{2,1,0:T(8,128)(2,1)}, bf16[2048,640]{1,0:T(8,128)(2,1)}, bf16[512,640]{1,0:T(8,128)(2,1)}, bf16[256,2048]{1,0:T(8,128)(2,1)}) custom-call(bf16[1024,2048]{1,0:T(8,128)(2,1)} %get-tuple-element.146.x0, bf16[1024,2048]{1,0:T(8,128)(2,1)} %get-tuple-element.147.x1, bf16[1024,2048]{1,0:T(8,128)(2,1)} %get-tuple-element.148.x2, ...), custom_call_target="tpu_custom_call" | custom-call | flops 15600000000 | bytes 1048576 | tf_op jit(solution)/shard_map/pallas_call | solution.py:470
  686.8 115.4 %shard_map.181 = (bf16[4,256,2048]{2,1,0:T(8,128)(2,1)}, bf16[4,64,2048]{2,1,0:T(8,128)(2,1)}, bf16[3,4,64,512]{3,2,1,0:T(8,128)(2,1)}, bf16[4,64,640]{2,1,0:T(8...) custom-call(bf16[4,256,2048]{2,1,0:T(8,128)(2,1)} %bitcast.158, ...), custom_call_target="tpu_custom_call" | custom-call | tf_op jit(solution)/shard_map/pallas_call | solution.py:580
  823.4 52.1 %shard_map.182 = (bf16[2,128,2048]{2,1,0:T(8,128)(2,1)}, bf16[2,128,2048]{2,1,0:T(8,128)(2,1)}, bf16[4,3,64,512]{3,2,1,0:T(8,128)(2,1)}, bf16[4,64,640]{2,1,0:T(...) custom-call(bf16[2,128,2048]{2,1,0:T(8,128)(2,1)} %bitcast.161, ...), custom_call_target="tpu_custom_call" | custom-call | tf_op jit(solution)/shard_map/pallas_call | solution.py:580
  (231 shorter events, 133.0 us)
Async XLA Ops:
  7.2 5.9 copy-start
  7.2 185.6 %all-gather.4.cloned.1.call-start = ((), (), s32[]{:S(2)}) async-start(), calls=%async_computation.4 | async-start | bytes 8650752 | tf_op jit(solution)/shard_map/all_gather | solution.py:1038
  14.2 95.2 %copy-start.23 = (bf16[2,128,2048]{2,1,0:T(8,128)(2,1)S(1)}, bf16[2,128,2048]{2,1,0:T(8,128)(2,1)}, u32[]{:S(2)}) copy-start(bf16[2,128,2048]{2,1,0:T(8,128)(2,1)} %param.13) | copy-start | bytes 3145732
  110.2 5.0 copy-start.36
  111.4 41.1 %all-to-all-start = ((bf16[8,128,512]{2,1,0:T(8,128)(2,1)}), bf16[8,128,512]{2,1,0:T(8,128)(2,1)S(1)}, u32[]{:S(2)}, u32[]{:S(2)}) async-start(bf16[8,128,512]{2,1,0:T(8,128)(2,1)} %bitcast.13), calls=%async_computation | async-start | bytes 2097152 | tf_op jit(solution)/shard_map/all_to_all | solution.py:1025
  115.1 6.9 copy-start.24
  115.1 251.2 %all-gather.6.cloned.1.call-start = ((), (), s32[]{:S(2)}) async-start(), calls=%async_computation.7 | async-start | bytes 10485760 | tf_op jit(solution)/shard_map/all_gather | solution.py:1052
  192.9 285.8 %reduce-scatter.3.cloned.1.call-start = ((), (), s32[]{:S(2)}) async-start(), calls=%async_computation.5 | async-start | bytes 9437184 | tf_op jit(solution)/shard_map/reduce_scatter | solution.py:1087
  197.0 35.9 %copy-start.8 = (f32[1024,512]{1,0:T(8,128)S(1)}, f32[1024,512]{1,0:T(8,128)}, u32[]{:S(2)}) copy-start(f32[1024,512]{1,0:T(8,128)} %get-tuple-element.119) | copy-start | bytes 6291460
  366.3 6.2 copy-start.9
  409.0 412.1 %reduce-scatter.5.cloned.1.call-start = ((), (), s32[]{:S(2)}) async-start(), calls=%async_computation.6 | async-start | bytes 10485760 | tf_op jit(solution)/shard_map/reduce_scatter | solution.py:1104
  436.2 4.4 copy-start.11
  436.2 4.8 copy-start.13
  436.3 6.7 copy-start.37
  483.6 5.1 copy-start.18
  492.1 7.5 collective-permute-start
  493.9 5.8 copy-start.2
  507.2 7.2 copy-start.17
  519.0 52.2 %copy-start.19 = (bf16[1024,512]{1,0:T(8,128)(2,1)S(1)}, bf16[1024,512]{1,0:T(8,128)(2,1)}, u32[]{:S(2)}) copy-start(bf16[1024,512]{1,0:T(8,128)(2,1)} %get-tuple-element.118) | copy-start | bytes 3145732
  619.9 66.9 %all-to-all-start.1 = ((bf16[8,128,512]{2,1,0:T(8,128)(2,1)}), bf16[8,128,512]{2,1,0:T(8,128)(2,1)S(1)}, u32[]{:S(2)}, u32[]{:S(2)}) async-start(bf16[8,128,512]{2,1,0:T(8,128)(2,1)} %bitcast.171), calls=%async_computation.2 | async-start | bytes 2097152 | tf_op jit(solution)/shard_map/all_to_all | solution.py:1110
  627.6 28.9 %copy-start.33 = (f32[8,512]{1,0:T(8,128)S(1)}, f32[8,512]{1,0:T(8,128)}, u32[]{:S(2)}) copy-start(f32[8,512]{1,0:T(8,128)} %get-tuple-element.163) | copy-start | bytes 49156
  803.7 4.6 copy-start.32
  803.7 4.7 copy-start.30
  876.5 3.9 copy-start.29
  (25 other events, 57.8 us)
Sparse Core Ops, SparseCore 0:
  109.5 83.3 all-gather.3
  194.4 171.8 all-gather.5
  409.1 69.5 reduce-scatter.2
  481.0 170.6 reduce-scatter.4

commit v4 on v3

--- a/solution.py
+++ b/solution.py
@@ -826,7 +826,7 @@
     return call_net(body, [tokens, sq, low, up, key], shapes, cid, 9, n_fixed + 4 * hops)[:5]
 
 
-def tail_exchange(dh, sq3, sq, down, wide, up, narrow, ffn, cid):
+def tail_exchange(dh, sq, down, wide, up, narrow, ffn, cid):
     A = lax.axis_size("sa")
     leads = [2, 1, 1, 0, 0, 0]
     halved = [1, 0, 0, None, None, 0]
@@ -835,7 +835,7 @@
     n = len(arrays)
 
     def body(ins, outs, scratch, net):
-        ps, pos = ins[2:], outs[2:]
+        ps, pos = ins[1:], outs[1:]
         own, other, chips = scratch[:n], scratch[n : 2 * n], scratch[2 * n :]
         line = line_shifts()
         net.greet(line + CHIPS + [OTHER_CORE])
@@ -854,7 +854,7 @@
             mine.append(net.locals)
             net.locals = []
         open_ = []
-        for x, o in zip(ins[:2], outs[:2]):
+        for x, o in zip(ins[:1], outs[:1]):
             open_ += [net.send(x.at[net.at(s)[0]], o.at[a], s) for s in line]
             net.keep(x.at[a], o.at[a])
 
@@ -938,10 +938,10 @@
         net.settle()
 
     sd = jax.ShapeDtypeStruct
-    shapes = [sd(dh.shape, BF), sd(sq3.shape, BF)] + [sd(s, BF) for s in blocks]
+    shapes = [sd(dh.shape, BF)] + [sd(s, BF) for s in blocks]
     scratch = [pltpu.VMEM((m,) + s, BF) for m in (4, 4, 3) for s in blocks]
-    n_send = 2 * (A - 1) + 10 * n
-    return call_net(body, [dh, sq3, *arrays], shapes, cid, 2 + 5 * n, n_send, scratch)
+    n_send = (A - 1) + 10 * n
+    return call_net(body, [dh, *arrays], shapes, cid, 1 + 5 * n, n_send, scratch)
 
 
 def last_exchange(swaps, sq, lines, key, cid):
@@ -1120,9 +1120,8 @@
     wide = jnp.pad(wide.T, ((0, 0), (0, 112)))
     narrow = jnp.pad(dvec.astype(BF).T, ((0, 0), (0, 120)))
     plane = (SB, RA, RC, w)
-    dh1_own, sq3_sum, sq_sum, down_sum, wide_sum, up_sum, narrow_sum, ffn = tail_exchange(
+    dh1_own, sq_sum, down_sum, wide_sum, up_sum, narrow_sum, ffn = tail_exchange(
         dh1.reshape(SA, T, D),
-        sq3_part.reshape(SA, w, D),
         sq_part.reshape((3, SA) + plane + (C,)),
         down_part.reshape((SA,) + plane + (640,)),
         wide.reshape((SA,) + plane + (128,)),
@@ -1135,10 +1134,10 @@
     _, norm1_pull = jax.vjp(lambda x: layer_norm(x, vec[0], vec[1]), x_own)
     (dx0,) = norm1_pull(dh1_own)
     mixed = (x1 + ffn.astype(F32)).astype(BF)
-    tokens_grad, mixed_out, sq_sum, down_sum, wide_sum, key_grad = last_exchange(
+    tokens_grad, mixed_out, sq_sum, down_sum, wide_sum, sq3_sum, key_grad = last_exchange(
         [(dx1 + dx0).astype(BF).reshape(SB, seg, D), mixed.reshape(SB, seg, D)],
         sq_sum,
-        [down_sum, wide_sum],
+        [down_sum, wide_sum, sq3_part.reshape(SA, w, D)],
         kv_grad[:FW].reshape(SB, RA, RC, w, half),
         6,
     )

time: 910 us -> 894 us (0.982)
  Pallas kernels: 644 us -> 630 us
    pallas_call x6, Pallas kernels: 418 us -> 404 us  [call_net(): pl.pallas_call(kernel, out_shape=out_shapes, in_specs=[HBM] * n, out_spec...]
  transfers between devices with their start and end apart: 7 -> 7, of which waited for: 5 -> 5; matrix products, arithmetic and copies ran while one was open for 14% -> 14% of each run, Pallas kernels for 52% -> 50%
where the time goes in v4:
time: 894 us; the launch traced here: 884 us
  Pallas kernels  630 us (70%)
  local copies, waits for them, and re-layouts  67.1 us (8%)
  other arithmetic  56.3 us (6%)
  waiting for transfers between devices  50.8 us (6%)
  matrix products  50.6 us (6%)
  between operations  16.4 us (2%)
  starting transfers between devices  13.5 us (2%)
    pallas_call x6, Pallas kernels, call_net(): pl.pallas_call(kernel, out_shape=out_shapes, in_specs=[HBM] * n, out_spec...  404 us
    dot_general x8, matrix products, mm(): return lax.dot_general(a, b, d, preferred_element_type=F32)  50.6 us
    pallas_call x1, Pallas kernels, recurrence_backward(): pl.pallas_call(functools.partial(blocks_kernel, backward_block, kinds, ra...  44.8 us
    pallas_call x1, Pallas kernels, recurrence_forward(): pl.pallas_call(functools.partial(blocks_kernel, forward_block, kinds, ran...  35.8 us
    pallas_call x1, Pallas kernels, hidden(): pl.pallas_call(hidden_kernel, grid=(n // 256,), in_specs=[tok(D), tok(D),...  32.9 us
    pallas_call x1, Pallas kernels, mix_forward(): pl.pallas_call(mix_forward_kernel, grid=(L // TILE,), in_specs=[tok(D), t...  28.5 us
    pallas_call x1, Pallas kernels, mix_backward(): pl.pallas_call(mix_backward_kernel, grid=(n,), in_specs=[tok(C)] * 7 + [t...  28 us
    pallas_call x1, Pallas kernels, weight_grads(): pl.pallas_call(weight_kernel, grid=(D // n,), in_specs=[feat] * 6 + [fix(...  26.3 us
  transfers between devices with their start and end apart: 7, of which 5 were waited for; matrix products, arithmetic and copies ran while one was open for 14% of the time, Pallas kernels for 50%

profile of v4, /device:TPU:0, one launch (start us, length us, event | category | flops | bytes accessed | tf_op | source)
XLA Modules:
  0.0 884.5 jit_solution(15757968073041693920)
XLA Ops:
  15.2 94.2 %shard_map.169 = (bf16[8,128,2048]{2,1,0:T(8,128)(2,1)}, bf16[3,4,2,2,2,64,512]{6,5,4,3,2,1,0:T(8,128)(2,1)}, bf16[4,2,2,2,64,768]{5,4,3,2,1,0:T(8,128)(2,1)}, b...) custom-call(bf16[2,128,2048]{2,1,0:T(8,128)(2,1)} %refs_0_.1, ...), custom_call_target="tpu_custom_call" | custom-call | tf_op jit(solution)/shard_map/pallas_call | solution.py:580
  123.6 28.5 %shard_map.170 = (bf16[1024,2048]{1,0:T(8,128)(2,1)}, bf16[1024,2048]{1,0:T(8,128)(2,1)}, bf16[1024,2048]{1,0:T(8,128)(2,1)}, bf16[1024,2048]{1,0:T(8,128)(2,1)}...) custom-call(bf16[1024,2048]{1,0:T(8,128)(2,1)} %bitcast.131, ...), custom_call_target="tpu_custom_call" | custom-call | flops 17999998976 | bytes 1048576 | tf_op jit(solution)/shard_map/pallas_call | solution.py:496
  153.7 13.4 %shard_map.171 = (bf16[1024,512]{1,0:T(8,128)(2,1)}, bf16[1024,512]{1,0:T(8,128)(2,1)}, bf16[1024,512]{1,0:T(8,128)(2,1)}, bf16[1024,512]{1,0:T(8,128)(2,1)}, bf...) custom-call(f32[1024,512]{1,0:T(8,128)} %get-tuple-element.105.refs_0_.refs_, ...), custom_call_target="tpu_custom_call" | custom-call | tf_op jit(solution)/shard_map/pallas_call | solution.py:273
  167.1 16.3 %shard_map.172.refs_6_.refs_10_ = f32[4,1024,128]{2,1,0:T(8,128)} custom-call(f32[4,1024,128]{2,1,0:T(8,128)} %get-tuple-element.117.ab), custom_call_target="tpu_custom_call" | custom-call | tf_op jit(solution)/shard_map/pallas_call | solution.py:282
  183.4 9.3 %all-gather.4.cloned.1.call-done = bf16[2048,2048]{1,0:T(8,128)(2,1)} async-done(((bf16[64,2048]{1,0:T(8,128)(2,1)}), bf16[2048,2048]{1,0:T(8,128)(2,1)}) %all-gather.4.cloned.1.call-update) | async-done | bytes 8388624 | tf_op jit(solution)/shard_map/all_gather | solution.py:1038
  196.9 35.8 %shard_map.173 = (bf16[1024,512]{1,0:T(8,128)(2,1)}, f32[1024,512]{1,0:T(8,128)}, f32[1024,512]{1,0:T(8,128)}, f32[1024,512]{1,0:T(8,128)}, bf16[1024,512]{1,0:T...) custom-call(bf16[1024,512]{1,0:T(8,128)(2,1)} %get-tuple-element.111.refs_0_.r, ...), custom_call_target="tpu_custom_call" | custom-call | tf_op jit(solution)/shard_map/pallas_call | solution.py:287
  235.5 43.4 %shard_map.174 = (bf16[4,272,512]{2,1,0:T(8,128)(2,1)}, bf16[2,2,2,2,128,2048]{5,4,3,2,1,0:T(8,128)(2,1)}) custom-call(bf16[4,272,512]{2,1,0:T(8,128)(2,1)} %fusion.20.refs_0_, bf16[2,128,2048]{2,1,0:T(8,128)(2,1)} %refs_1_.1), custom_call_target="tpu_custom_call" | custom-call | tf_op jit(solution)/shard_map/pallas_call | solution.py:580
  280.8 5.9 convolution_add_fusion
  295.2 60.7 %shard_map.175 = bf16[2,2,2,256,2048]{4,3,2,1,0:T(8,128)(2,1)} custom-call(bf16[256,2048]{1,0:T(8,128)(2,1)} %add_convert_fusion.2.refs_0_), custom_call_target="tpu_custom_call" | custom-call | tf_op jit(solution)/shard_map/pallas_call | solution.py:580
  355.9 10.5 %all-gather.6.cloned.1.call-done = bf16[4096,1024]{1,0:T(8,128)(2,1)} async-done(((bf16[1024,1024]{1,0:T(8,128)(2,1)}), bf16[4096,1024]{1,0:T(8,128)(2,1)}) %all-gather.6.cloned.1.call-update) | async-done | bytes 8388624 | tf_op jit(solution)/shard_map/all_gather | solution.py:1052
  376.2 32.9 %shard_map.176 = (bf16[2048,1024]{1,0:T(8,128)(2,1)}, bf16[2048,1024]{1,0:T(8,128)(2,1)}, bf16[2048,2048]{1,0:T(8,128)(2,1)}) custom-call(bf16[2048,2048]{1,0:T(8,128)(2,1)} %bitcast.120, bf16[2048,2048]{1,0:T(8,128)(2,1)} %bitcast.175, bf16[2048,1024]{1,0:T(8,128)(2,1)} %bitcast.147, bf16[1024,2048]{1,0:T(8,128)(2,1)} %pad_maximum_fusion.1.value), custom_call_target="tpu_custom_call" | custom-call | flops 17999998976 | bytes 1048576 | tf_op jit(solution)/shard_map/pallas_call | solution.py:437
  409.6 12.9 %convolution_convert_fusion.1 = bf16[1024,2048]{1,0:T(8,128)(2,1)S(1)} fusion(bf16[2048,1024]{1,0:T(8,128)(2,1)} %get-tuple-element.127, bf16[2048,2048]{1,0:T(8,128)(2,1)} %bitcast.176), kind=kOutput, calls=%fused_computation.4 | convolution fusion | flops 8592031744 | bytes 16777216 | tf_op jit(solution)/shard_map/dot_general | solution.py:18
  424.9 11.5 %convolution_convert_fusion.2 = bf16[2048,1024]{1,0:T(8,128)(2,1)S(1)} fusion(bf16[2048,2048]{1,0:T(8,128)(2,1)} %bitcast.121, bf16[2048,1024]{1,0:T(8,128)(2,1)S(1)} %copy-done.39), kind=kOutput, calls=%fused_computation.5 | convolution fusion | flops 8592031744 | bytes 16777216 | tf_op jit(solution)/shard_map/dot_general | solution.py:18
  443.1 10.9 %convolution_convert_fusion = bf16[2048,2048]{1,0:T(8,128)(2,1)} fusion(bf16[2048,1024]{1,0:T(8,128)(2,1)S(1)} %copy-done.38, bf16[1024,1024]{1,0:T(8,128)(2,1)S(1)} %bitcast.130, bf16[1024,1024]{1,0:T(8,128)(2,1)S(1)} %bitcast.128), kind=kOutput, calls=%fused_computation.2 | convolution fusion | flops 8602517504 | bytes 16777216 | tf_op jit(solution)/shard_map/dot_general | solution.py:18
  454.0 24.7 %reduce-scatter.3.cloned.1.call-done = bf16[256,2048]{1,0:T(8,128)(2,1)} async-done(((bf16[2048,2048]{1,0:T(8,128)(2,1)}), bf16[256,2048]{1,0:T(8,128)(2,1)}) %reduce-scatter.3.cloned.1.call-update) | async-done | bytes 1048592 | tf_op jit(solution)/shard_map/reduce_scatter | solution.py:1087
  494.0 5.7 collective-permute-done
  507.3 7.2 convolution_convert_fusion.3
  519.0 52.2 %shard_map.177 = (bf16[4,256,512]{2,1,0:T(8,128)(2,1)}, bf16[2,2,2,256,2048]{4,3,2,1,0:T(8,128)(2,1)}, bf16[2,2,2,256,256]{4,3,2,1,0:T(8,128)(2,1)}) custom-call(bf16[4,256,512]{2,1,0:T(8,128)(2,1)} %bitcast.146, bf16[256,2048]{1,0:T(8,128)(2,1)} %copy-done.17, bf16[2,2,2,256,256]{4,3,2,1,0:T(8,128)(2,1)} %copy.131.refs_2_), custom_call_target="tpu_custom_call" | custom-call | tf_op jit(solution)/shard_map/pallas_call | solution.py:580
  575.1 44.8 %shard_map.178 = (bf16[1024,512]{1,0:T(8,128)(2,1)}, bf16[1024,512]{1,0:T(8,128)(2,1)}, bf16[1024,512]{1,0:T(8,128)(2,1)}, bf16[1024,512]{1,0:T(8,128)(2,1)}, bf...) custom-call(bf16[1024,512]{1,0:T(8,128)(2,1)} %get-tuple-element.208.refs_0_,, ...), custom_call_target="tpu_custom_call" | custom-call | tf_op jit(solution)/shard_map/pallas_call | solution.py:314
  619.9 7.7 all-to-all-start.1
  627.6 28.0 %shard_map.179 = (bf16[1024,2048]{1,0:T(8,128)(2,1)}, bf16[1024,640]{1,0:T(8,128)(2,1)}, f32[8,2048]{1,0:T(8,128)}) custom-call(bf16[1024,512]{1,0:T(8,128)(2,1)} %get-tuple-element.138.drp, bf16[1024,512]{1,0:T(8,128)(2,1)} %get-tuple-element.139.dkp, bf16[1024,512]{1,0:T(8,128)(2,1)} %get-tuple-element.140.dvp, bf16[1024,512]{1,0:T(8,128)(2,1)} %get-tuple-element.141.duw, ...), custom_call_target="tpu_custom_call" | custom-call | flops 20999999488 | bytes 1048576 | tf_op jit(solution)/shard_map/pallas_call | solution.py:519
  660.6 26.3 %shard_map.180 = (bf16[3,2048,512]{2,1,0:T(8,128)(2,1)}, bf16[2048,640]{1,0:T(8,128)(2,1)}, bf16[512,640]{1,0:T(8,128)(2,1)}, bf16[256,2048]{1,0:T(8,128)(2,1)}) custom-call(bf16[1024,2048]{1,0:T(8,128)(2,1)} %get-tuple-element.147.x0, bf16[1024,2048]{1,0:T(8,128)(2,1)} %get-tuple-element.148.x1, bf16[1024,2048]{1,0:T(8,128)(2,1)} %get-tuple-element.149.x2, ...), custom_call_target="tpu_custom_call" | custom-call | flops 15600000000 | bytes 1048576 | tf_op jit(solution)/shard_map/pallas_call | solution.py:470
  686.9 96.6 %shard_map.181 = (bf16[4,256,2048]{2,1,0:T(8,128)(2,1)}, bf16[3,4,64,512]{3,2,1,0:T(8,128)(2,1)}, bf16[4,64,640]{2,1,0:T(8,128)(2,1)}, bf16[4,64,128]{2,1,0:T(8,...) custom-call(bf16[4,256,2048]{2,1,0:T(8,128)(2,1)} %bitcast.158, ...), custom_call_target="tpu_custom_call" | custom-call | tf_op jit(solution)/shard_map/pallas_call | solution.py:580
  803.2 56.4 %shard_map.182 = (bf16[2,128,2048]{2,1,0:T(8,128)(2,1)}, bf16[2,128,2048]{2,1,0:T(8,128)(2,1)}, bf16[4,3,64,512]{3,2,1,0:T(8,128)(2,1)}, bf16[4,64,640]{2,1,0:T(...) custom-call(bf16[2,128,2048]{2,1,0:T(8,128)(2,1)} %bitcast.161, ...), custom_call_target="tpu_custom_call" | custom-call | tf_op jit(solution)/shard_map/pallas_call | solution.py:580
  (233 shorter events, 132.3 us)
Async XLA Ops:
  7.2 5.9 copy-start
  7.2 185.5 %all-gather.4.cloned.1.call-start = ((), (), s32[]{:S(2)}) async-start(), calls=%async_computation.4 | async-start | bytes 8650752 | tf_op jit(solution)/shard_map/all_gather | solution.py:1038
  14.2 95.2 %copy-start.23 = (bf16[2,128,2048]{2,1,0:T(8,128)(2,1)S(1)}, bf16[2,128,2048]{2,1,0:T(8,128)(2,1)}, u32[]{:S(2)}) copy-start(bf16[2,128,2048]{2,1,0:T(8,128)(2,1)} %param.13) | copy-start | bytes 3145732
  110.2 5.0 copy-start.37
  111.4 41.4 %all-to-all-start = ((bf16[8,128,512]{2,1,0:T(8,128)(2,1)}), bf16[8,128,512]{2,1,0:T(8,128)(2,1)S(1)}, u32[]{:S(2)}, u32[]{:S(2)}) async-start(bf16[8,128,512]{2,1,0:T(8,128)(2,1)} %bitcast.13), calls=%async_computation | async-start | bytes 2097152 | tf_op jit(solution)/shard_map/all_to_all | solution.py:1025
  115.1 6.9 copy-start.24
  115.1 251.3 %all-gather.6.cloned.1.call-start = ((), (), s32[]{:S(2)}) async-start(), calls=%async_computation.7 | async-start | bytes 10485760 | tf_op jit(solution)/shard_map/all_gather | solution.py:1052
  192.7 286.0 %reduce-scatter.3.cloned.1.call-start = ((), (), s32[]{:S(2)}) async-start(), calls=%async_computation.5 | async-start | bytes 9437184 | tf_op jit(solution)/shard_map/reduce_scatter | solution.py:1087
  196.9 35.9 %copy-start.8 = (f32[1024,512]{1,0:T(8,128)S(1)}, f32[1024,512]{1,0:T(8,128)}, u32[]{:S(2)}) copy-start(f32[1024,512]{1,0:T(8,128)} %get-tuple-element.119) | copy-start | bytes 6291460
  366.4 6.2 copy-start.9
  409.1 391.8 %reduce-scatter.5.cloned.1.call-start = ((), (), s32[]{:S(2)}) async-start(), calls=%async_computation.6 | async-start | bytes 10485760 | tf_op jit(solution)/shard_map/reduce_scatter | solution.py:1104
  436.4 4.4 copy-start.11
  436.4 4.8 copy-start.13
  436.4 6.7 copy-start.38
  483.7 5.1 copy-start.18
  492.2 7.5 collective-permute-start
  493.9 5.7 copy-start.2
  507.3 7.2 copy-start.17
  519.0 52.3 %copy-start.19 = (bf16[1024,512]{1,0:T(8,128)(2,1)S(1)}, bf16[1024,512]{1,0:T(8,128)(2,1)}, u32[]{:S(2)}) copy-start(bf16[1024,512]{1,0:T(8,128)(2,1)} %get-tuple-element.118) | copy-start | bytes 3145732
  619.9 67.0 %all-to-all-start.1 = ((bf16[8,128,512]{2,1,0:T(8,128)(2,1)}), bf16[8,128,512]{2,1,0:T(8,128)(2,1)S(1)}, u32[]{:S(2)}, u32[]{:S(2)}) async-start(bf16[8,128,512]{2,1,0:T(8,128)(2,1)} %bitcast.170), calls=%async_computation.2 | async-start | bytes 2097152 | tf_op jit(solution)/shard_map/all_to_all | solution.py:1110
  627.6 28.9 %copy-start.34 = (f32[8,512]{1,0:T(8,128)S(1)}, f32[8,512]{1,0:T(8,128)}, u32[]{:S(2)}) copy-start(f32[8,512]{1,0:T(8,128)} %get-tuple-element.162) | copy-start | bytes 49156
  785.0 4.6 copy-start.33
  785.0 4.7 copy-start.31
  859.6 3.7 copy-start.29
  (26 other events, 60.6 us)
Sparse Core Ops, SparseCore 0:
  109.5 83.1 all-gather.3
  194.3 172.0 all-gather.5
  409.2 69.4 reduce-scatter.2
  481.0 170.6 reduce-scatter.4
